TPU v7x, 32 devices: a whole 2x2x4 slice. The times are simulated.
32 devices in a mesh: dp: 8 (over z, x), tensor: 4 (over y, core).
Axes of the slice: x: 2, y: 2, z: 4, core: 2. Of those that a mesh axis runs over, the one named last changes fastest.
Arguments:
- text_rows: bfloat16 [256, 40, 768], P(('dp', 'tensor')), may hold values from -6 to 6
- patch_features: bfloat16 [256, 145, 1024], P(('dp', 'tensor')), may hold values from -6 to 6
- lengths: int32 [256], P(('dp', 'tensor')), may hold values from 8 to 40, as said below
- text_cotangent: bfloat16 [256, 40, 768], P(('dp', 'tensor')), may hold values from -6 to 6
- join_cotangent: bfloat16 [256, 40, 768], P(('dp', 'tensor')), may hold values from -6 to 6
- text_project_in: bfloat16 [3, 768, 768], P(None, None, 'tensor'), may hold values from -0.21875 to 0.21875
- text_project_bias: bfloat16 [2, 768], P(None, 'tensor'), may hold values from -3 to 3
- text_project_out: bfloat16 [768, 768], P('tensor'), may hold values from -0.75 to 0.75
- text_expand: bfloat16 [768, 3072], P(None, 'tensor'), may hold values from -0.21875 to 0.21875
- text_expand_bias: bfloat16 [3072], P('tensor'), may hold values from -3 to 3
- text_contract: bfloat16 [3072, 768], P('tensor'), may hold values from -0.109375 to 0.109375
- text_out_bias: bfloat16 [2, 768], replicated, may hold values from -3 to 3
- text_norm_gain: bfloat16 [2, 768], replicated, may hold values from 0.099609375 to 1.8984375
- text_norm_shift: bfloat16 [2, 768], replicated, may hold values from -3 to 3
- join_project_in: bfloat16 [4, 768, 768], P(None, None, 'tensor'), may hold values from -0.21875 to 0.21875
- join_project_bias: bfloat16 [4, 768], P(None, 'tensor'), may hold values from -3 to 3
- join_project_out: bfloat16 [768, 768], P('tensor'), may hold values from -0.75 to 0.75
- cross_project_out: bfloat16 [768, 768], P('tensor'), may hold values from -1.5 to 1.5
- cross_key_value: bfloat16 [2, 1024, 768], P(None, None, 'tensor'), may hold values from -0.1875 to 0.1875
- join_expand: bfloat16 [768, 3072], P(None, 'tensor'), may hold values from -0.21875 to 0.21875
- join_expand_bias: bfloat16 [3072], P('tensor'), may hold values from -3 to 3
- join_contract: bfloat16 [3072, 768], P('tensor'), may hold values from -0.109375 to 0.109375
- join_out_bias: bfloat16 [3, 768], replicated, may hold values from -3 to 3
- join_norm_gain: bfloat16 [3, 768], replicated, may hold values from 0.099609375 to 1.8984375
- join_norm_shift: bfloat16 [3, 768], replicated, may hold values from -3 to 3
Outputs:
- text_out: bfloat16 [256, 40, 768], P(('dp', 'tensor'))
- join_out: bfloat16 [256, 40, 768], P(('dp', 'tensor'))
- grad_text: bfloat16 [256, 40, 768], P(('dp', 'tensor'))
- grad_patches: bfloat16 [256, 145, 1024], P(('dp', 'tensor'))
- grad_text_project_in: float32 [3, 768, 768], P(None, None, 'tensor')
- grad_text_project_bias: float32 [2, 768], P(None, 'tensor')
- grad_text_project_out: float32 [768, 768], P('tensor')
- grad_text_expand: float32 [768, 3072], P(None, 'tensor')
- grad_text_expand_bias: float32 [3072], P('tensor')
- grad_text_contract: float32 [3072, 768], P('tensor')
- grad_text_out_bias: float32 [2, 768], replicated
- grad_text_norm_gain: float32 [2, 768], replicated
- grad_text_norm_shift: float32 [2, 768], replicated
- grad_join_project_in: float32 [4, 768, 768], P(None, None, 'tensor')
- grad_join_project_bias: float32 [4, 768], P(None, 'tensor')
- grad_join_project_out: float32 [768, 768], P('tensor')
- grad_cross_project_out: float32 [768, 768], P('tensor')
- grad_cross_key_value: float32 [2, 1024, 768], P(None, None, 'tensor')
- grad_join_expand: float32 [768, 3072], P(None, 'tensor')
- grad_join_expand_bias: float32 [3072], P('tensor')
- grad_join_contract: float32 [3072, 768], P('tensor')
- grad_join_out_bias: float32 [3, 768], replicated
- grad_join_norm_gain: float32 [3, 768], replicated
- grad_join_norm_shift: float32 [3, 768], replicated
Inputs may be any that keep to these rules, and one draw needn't show every extreme that they name: An item's first lengths slots hold its text, the others padding; in every draw some item has all 40 slots real and some item only 8.
All inputs are finite; a program needn't handle non-finite values.
Results may differ from a plain program's by a relative error of at most 0.029.
Values may be sent and summed in bfloat16 or wider, within the bound.
A program may use at most 256 MiB of HBM per device.

v0:
```python
import jax
import jax.numpy as jnp
from jax import lax
from jax.sharding import PartitionSpec as P

HEAD_DIM = 64


def layer_norm(row_block, gain_vec, shift_vec):
    center = row_block - jnp.mean(row_block, axis=-1, keepdims=True)
    variance = jnp.mean(center * center, axis=-1, keepdims=True)
    return center * lax.rsqrt(variance + 1e-12) * gain_vec + shift_vec


def norm_back(pre_norm, gain_vec, shift_vec, grad_out):
    normed, pullback = jax.vjp(layer_norm, pre_norm, gain_vec, shift_vec)
    return pullback(grad_out)


def gelu_exact(pre_act):
    return jax.nn.gelu(pre_act, approximate=False)


def split_heads(source_array):
    return source_array.reshape(
        source_array.shape[:-1] + (source_array.shape[-1] // HEAD_DIM, HEAD_DIM)
    )


def attend_scores(queries, key_rows, valid_mask):
    scores = jnp.einsum(
        "iqhe,ikhe->ihqk",
        split_heads(queries),
        split_heads(key_rows),
        preferred_element_type=jnp.float32,
    ) * HEAD_DIM ** (-0.5)
    if valid_mask is None:
        return scores
    return jnp.where(valid_mask[:, None, None, :], scores, -1e30)


def attend_forward(queries, key_rows, values, valid_mask):
    scores = attend_scores(queries, key_rows, valid_mask)
    row_max = jnp.max(scores, axis=-1, keepdims=True)
    weights = jnp.exp(scores - row_max)
    totals = jnp.sum(weights, axis=-1, keepdims=True)
    probabilities = weights / totals
    mixed_heads = jnp.einsum(
        "ihqk,ikhe->iqhe",
        probabilities.astype(jnp.bfloat16),
        split_heads(values),
        preferred_element_type=jnp.float32,
    )
    return (mixed_heads.reshape(queries.shape).astype(jnp.bfloat16), row_max + jnp.log(totals))


def attend_backward(queries, key_rows, values, valid_mask, log_total, grad_mixed):
    probabilities = jnp.exp(attend_scores(queries, key_rows, valid_mask) - log_total)
    grad_heads = split_heads(grad_mixed)
    grad_values = jnp.einsum(
        "ihqk,iqhe->ikhe",
        probabilities.astype(jnp.bfloat16),
        grad_heads,
        preferred_element_type=jnp.float32,
    )
    grad_probs = jnp.einsum(
        "iqhe,ikhe->ihqk", grad_heads, split_heads(values), preferred_element_type=jnp.float32
    )
    inner_sum = jnp.sum(probabilities * grad_probs, axis=-1, keepdims=True)
    grad_scores = (probabilities * (grad_probs - inner_sum)).astype(jnp.bfloat16)
    scaling = HEAD_DIM ** (-0.5)
    grad_queries = (
        jnp.einsum(
            "ihqk,ikhe->iqhe",
            grad_scores,
            split_heads(key_rows),
            preferred_element_type=jnp.float32,
        )
        * scaling
    )
    grad_keys = (
        jnp.einsum(
            "ihqk,iqhe->ikhe", grad_scores, split_heads(queries), preferred_element_type=jnp.float32
        )
        * scaling
    )
    return (
        grad_queries.reshape(queries.shape).astype(jnp.bfloat16),
        grad_keys.reshape(key_rows.shape).astype(jnp.bfloat16),
        grad_values.reshape(values.shape).astype(jnp.bfloat16),
    )


def spread_rows(row_block):
    return lax.all_gather(row_block, "tensor", axis=0, tiled=True)


def branch_sum(inputs, weight):
    return lax.psum_scatter(
        jnp.dot(inputs, weight, preferred_element_type=jnp.float32),
        "tensor",
        scatter_dimension=0,
        tiled=True,
    )


def input_grads(grad_stack, weights):
    return lax.psum_scatter(
        jnp.einsum("cre,cde->rd", grad_stack, weights, preferred_element_type=jnp.float32),
        "tensor",
        scatter_dimension=0,
        tiled=True,
    )


def output_back(grad_pre, inputs, weight):
    gathered = lax.all_gather(grad_pre.astype(jnp.bfloat16), "tensor", axis=0, tiled=True)
    flat_grad = gathered.reshape(-1, gathered.shape[-1])
    grad_weight = jnp.einsum("re,rd->ed", inputs, flat_grad, preferred_element_type=jnp.float32)
    grad_inputs = jnp.einsum("rd,ed->re", flat_grad, weight, preferred_element_type=jnp.float32)
    return (grad_weight, grad_inputs, jnp.sum(grad_pre, axis=(0, 1)))


def self_forward(row_block, gathered, valid_mask, w_in, b_in, w_out, out_bias, gain_vec, shift_vec):
    bias_stack = jnp.stack([b_in[0], jnp.zeros_like(b_in[0]), b_in[1]])[:, None, None, :]
    projected = (
        jnp.einsum("isd,cde->cise", gathered, w_in, preferred_element_type=jnp.float32) + bias_stack
    ).astype(jnp.bfloat16)
    mixed_heads, log_total = attend_forward(projected[0], projected[1], projected[2], valid_mask)
    flat_mixed = mixed_heads.reshape(-1, mixed_heads.shape[-1])
    branch = branch_sum(flat_mixed, w_out)
    pre_norm = row_block + branch.reshape(row_block.shape) + out_bias
    return (
        layer_norm(pre_norm, gain_vec, shift_vec),
        (gathered, projected, flat_mixed, log_total, pre_norm),
    )


def self_backward(grad_out, saved_state, valid_mask, w_in, w_out, gain_vec, shift_vec):
    gathered, projected, flat_mixed, log_total, pre_norm = saved_state
    grad_pre, grad_gain, grad_shift = norm_back(pre_norm, gain_vec, shift_vec, grad_out)
    grad_w_out, grad_mixed, grad_bias = output_back(grad_pre, flat_mixed, w_out)
    grad_triple = attend_backward(
        projected[0],
        projected[1],
        projected[2],
        valid_mask,
        log_total,
        grad_mixed.astype(jnp.bfloat16).reshape(projected[0].shape),
    )
    grad_stack = jnp.stack(grad_triple)
    grad_w_in = jnp.einsum(
        "isd,cise->cde", gathered, grad_stack, preferred_element_type=jnp.float32
    )
    grad_b_in = jnp.stack(
        [
            jnp.sum(grad_triple[0], axis=(0, 1), dtype=jnp.float32),
            jnp.sum(grad_triple[2], axis=(0, 1), dtype=jnp.float32),
        ]
    )
    flat_grads = grad_stack.reshape(3, -1, grad_stack.shape[-1])
    grad_rows = grad_pre + input_grads(flat_grads, w_in).reshape(pre_norm.shape)
    return (grad_rows, (grad_w_in, grad_b_in, grad_w_out), (grad_bias, grad_gain, grad_shift))


def feed_forward(row_block, w_expand, b_expand, w_contract, out_bias, gain_vec, shift_vec):
    gathered = spread_rows(row_block.astype(jnp.bfloat16)).reshape(-1, row_block.shape[-1])
    pre_act = jnp.dot(gathered, w_expand, preferred_element_type=jnp.float32) + b_expand
    hidden = gelu_exact(pre_act).astype(jnp.bfloat16)
    branch = branch_sum(hidden, w_contract)
    pre_norm = row_block + branch.reshape(row_block.shape) + out_bias
    return (layer_norm(pre_norm, gain_vec, shift_vec), (gathered, pre_act, hidden, pre_norm))


def feed_backward(grad_out, saved_state, w_expand, w_contract, gain_vec, shift_vec):
    gathered, pre_act, hidden, pre_norm = saved_state
    grad_pre, grad_gain, grad_shift = norm_back(pre_norm, gain_vec, shift_vec, grad_out)
    grad_contract, grad_hidden, grad_bias = output_back(grad_pre, hidden, w_contract)
    activated, gelu_pull = jax.vjp(gelu_exact, pre_act)
    grad_act = gelu_pull(grad_hidden)[0].astype(jnp.bfloat16)
    grad_expand = jnp.einsum("rd,rf->df", gathered, grad_act, preferred_element_type=jnp.float32)
    grad_expand_bias = jnp.sum(grad_act, axis=0, dtype=jnp.float32)
    grad_rows = grad_pre + input_grads(grad_act[None], w_expand[None]).reshape(pre_norm.shape)
    return (
        grad_rows,
        (grad_expand, grad_expand_bias, grad_contract),
        (grad_bias, grad_gain, grad_shift),
    )


def cross_forward(
    row_block, patch_local, w_query, b_proj, w_keyval, w_out, out_bias, gain_vec, shift_vec
):
    gathered = spread_rows(row_block.astype(jnp.bfloat16))
    queries = (
        jnp.einsum("isd,de->ise", gathered, w_query, preferred_element_type=jnp.float32) + b_proj[2]
    ).astype(jnp.bfloat16)
    patch_all = lax.all_gather(patch_local, "tensor", axis=0, tiled=True)
    value_bias = jnp.stack([jnp.zeros_like(b_proj[3]), b_proj[3]])[:, None, None, :]
    keyval = (
        jnp.einsum("ipf,cfe->cipe", patch_all, w_keyval, preferred_element_type=jnp.float32)
        + value_bias
    ).astype(jnp.bfloat16)
    mixed_heads, log_total = attend_forward(queries, keyval[0], keyval[1], None)
    flat_mixed = mixed_heads.reshape(-1, mixed_heads.shape[-1])
    branch = branch_sum(flat_mixed, w_out)
    pre_norm = row_block + branch.reshape(row_block.shape) + out_bias
    return (
        layer_norm(pre_norm, gain_vec, shift_vec),
        (gathered, queries, keyval, patch_all, flat_mixed, log_total, pre_norm),
    )


def cross_backward(grad_out, saved_state, w_query, w_keyval, w_out, gain_vec, shift_vec):
    gathered, queries, keyval, kept_operand, flat_mixed, log_total, pre_norm = saved_state
    group_width = queries.shape[-1]
    grad_pre, grad_gain, grad_shift = norm_back(pre_norm, gain_vec, shift_vec, grad_out)
    grad_w_out, grad_mixed, grad_bias = output_back(grad_pre, flat_mixed, w_out)
    grad_queries, grad_keys, grad_values = attend_backward(
        queries,
        keyval[0],
        keyval[1],
        None,
        log_total,
        grad_mixed.astype(jnp.bfloat16).reshape(queries.shape),
    )
    grad_query_w = jnp.einsum(
        "isd,ise->de", gathered, grad_queries, preferred_element_type=jnp.float32
    )
    grad_query_b = jnp.sum(grad_queries, axis=(0, 1), dtype=jnp.float32)
    grad_value_b = jnp.sum(grad_values, axis=(0, 1), dtype=jnp.float32)
    grad_keyval = jnp.stack([grad_keys, grad_values])
    grad_w_keyval = jnp.einsum(
        "ipf,cipe->cfe", kept_operand, grad_keyval, preferred_element_type=jnp.float32
    )
    grad_patch = lax.psum_scatter(
        jnp.einsum("cipe,cfe->ipf", grad_keyval, w_keyval, preferred_element_type=jnp.float32),
        "tensor",
        scatter_dimension=0,
        tiled=True,
    )
    grad_rows = grad_pre + input_grads(
        grad_queries.reshape(1, -1, group_width), w_query[None]
    ).reshape(pre_norm.shape)
    return (
        grad_rows,
        grad_patch,
        (grad_query_w, grad_query_b, grad_value_b, grad_w_keyval, grad_w_out),
        (grad_bias, grad_gain, grad_shift),
    )


def per_device(
    text_rows,
    patch_features,
    lengths,
    text_cotangent,
    join_cotangent,
    text_project_in,
    text_project_bias,
    text_project_out,
    text_expand,
    text_expand_bias,
    text_contract,
    text_out_bias,
    text_norm_gain,
    text_norm_shift,
    join_project_in,
    join_project_bias,
    join_project_out,
    cross_project_out,
    cross_key_value,
    join_expand,
    join_expand_bias,
    join_contract,
    join_out_bias,
    join_norm_gain,
    join_norm_shift,
):
    text_biases = text_out_bias.astype(jnp.float32)
    text_gains = text_norm_gain.astype(jnp.float32)
    text_shifts = text_norm_shift.astype(jnp.float32)
    join_biases = join_out_bias.astype(jnp.float32)
    join_gains = join_norm_gain.astype(jnp.float32)
    join_shifts = join_norm_shift.astype(jnp.float32)
    gathered_text, all_lengths = (
        lax.all_gather(text_rows, "tensor", axis=0, tiled=True),
        lax.all_gather(lengths, "tensor", axis=0, tiled=True),
    )
    slot_index = lax.broadcasted_iota(jnp.int32, gathered_text.shape[:2], 1)
    valid_mask = slot_index < all_lengths[:, None]
    hidden_one, saved_one = self_forward(
        text_rows.astype(jnp.float32),
        gathered_text,
        valid_mask,
        text_project_in,
        text_project_bias,
        text_project_out,
        text_biases[0],
        text_gains[0],
        text_shifts[0],
    )
    text_final, saved_two = feed_forward(
        hidden_one,
        text_expand,
        text_expand_bias,
        text_contract,
        text_biases[1],
        text_gains[1],
        text_shifts[1],
    )
    text_out = text_final.astype(jnp.bfloat16)
    hidden_two, saved_three = self_forward(
        text_out.astype(jnp.float32),
        spread_rows(text_out),
        valid_mask,
        join_project_in[0:3],
        join_project_bias[0:2],
        join_project_out,
        join_biases[0],
        join_gains[0],
        join_shifts[0],
    )
    hidden_three, saved_four = cross_forward(
        hidden_two,
        patch_features,
        join_project_in[3],
        join_project_bias,
        cross_key_value,
        cross_project_out,
        join_biases[1],
        join_gains[1],
        join_shifts[1],
    )
    join_final, saved_five = feed_forward(
        hidden_three,
        join_expand,
        join_expand_bias,
        join_contract,
        join_biases[2],
        join_gains[2],
        join_shifts[2],
    )
    join_out = join_final.astype(jnp.bfloat16)
    grad_five, grads_five, shared_five = feed_backward(
        join_cotangent.astype(jnp.float32),
        saved_five,
        join_expand,
        join_contract,
        join_gains[2],
        join_shifts[2],
    )
    grad_four, grad_patch, grads_four, shared_four = cross_backward(
        grad_five,
        saved_four,
        join_project_in[3],
        cross_key_value,
        cross_project_out,
        join_gains[1],
        join_shifts[1],
    )
    grad_three, grads_three, shared_three = self_backward(
        grad_four,
        saved_three,
        valid_mask,
        join_project_in[0:3],
        join_project_out,
        join_gains[0],
        join_shifts[0],
    )
    grad_two, grads_two, shared_two = feed_backward(
        grad_three + text_cotangent.astype(jnp.float32),
        saved_two,
        text_expand,
        text_contract,
        text_gains[1],
        text_shifts[1],
    )
    grad_one, grads_one, shared_one = self_backward(
        grad_two,
        saved_one,
        valid_mask,
        text_project_in,
        text_project_out,
        text_gains[0],
        text_shifts[0],
    )
    join_in_grad = jnp.concatenate([grads_three[0], grads_four[0][None]], axis=0)
    join_bias_grad = jnp.stack([grads_three[1][0], grads_three[1][1], grads_four[1], grads_four[2]])
    summed = lax.psum(
        (
            grads_one[0],
            grads_one[1],
            grads_one[2],
            grads_two[0],
            grads_two[1],
            grads_two[2],
            join_in_grad,
            join_bias_grad,
            grads_three[2],
            grads_four[4],
            grads_four[3],
            grads_five[0],
            grads_five[1],
            grads_five[2],
        ),
        "dp",
    )
    text_bias_grad = jnp.stack([shared_one[0], shared_two[0]])
    text_gain_grad = jnp.stack([shared_one[1], shared_two[1]])
    text_shift_grad = jnp.stack([shared_one[2], shared_two[2]])
    join_out_grad = jnp.stack([shared_three[0], shared_four[0], shared_five[0]])
    join_gain_grad = jnp.stack([shared_three[1], shared_four[1], shared_five[1]])
    join_shift_grad = jnp.stack([shared_three[2], shared_four[2], shared_five[2]])
    totals = lax.psum(
        (
            text_bias_grad,
            text_gain_grad,
            text_shift_grad,
            join_out_grad,
            join_gain_grad,
            join_shift_grad,
        ),
        ("dp", "tensor"),
    )
    return (
        text_out,
        join_out,
        grad_one.astype(jnp.bfloat16),
        grad_patch.astype(jnp.bfloat16),
        summed[0],
        summed[1],
        summed[2],
        summed[3],
        summed[4],
        summed[5],
        totals[0],
        totals[1],
        totals[2],
        summed[6],
        summed[7],
        summed[8],
        summed[9],
        summed[10],
        summed[11],
        summed[12],
        summed[13],
        totals[3],
        totals[4],
        totals[5],
    )


def solution(mesh):
    in_specs = (
        P(("dp", "tensor"), None, None),
        P(("dp", "tensor"), None, None),
        P(("dp", "tensor")),
        P(("dp", "tensor"), None, None),
        P(("dp", "tensor"), None, None),
        P(None, None, "tensor"),
        P(None, "tensor"),
        P("tensor", None),
        P(None, "tensor"),
        P("tensor"),
        P("tensor", None),
        P(),
        P(),
        P(),
        P(None, None, "tensor"),
        P(None, "tensor"),
        P("tensor", None),
        P("tensor", None),
        P(None, None, "tensor"),
        P(None, "tensor"),
        P("tensor"),
        P("tensor", None),
        P(),
        P(),
        P(),
    )
    out_specs = (
        P(("dp", "tensor"), None, None),
        P(("dp", "tensor"), None, None),
        P(("dp", "tensor"), None, None),
        P(("dp", "tensor"), None, None),
        P(None, None, "tensor"),
        P(None, "tensor"),
        P("tensor", None),
        P(None, "tensor"),
        P("tensor"),
        P("tensor", None),
        P(),
        P(),
        P(),
        P(None, None, "tensor"),
        P(None, "tensor"),
        P("tensor", None),
        P("tensor", None),
        P(None, None, "tensor"),
        P(None, "tensor"),
        P("tensor"),
        P("tensor", None),
        P(),
        P(),
        P(),
    )
    return jax.shard_map(
        per_device, mesh=mesh, in_specs=in_specs, out_specs=out_specs, check_vma=False
    )
```

profile of v0, /device:TPU:0, one launch (start us, length us, event | category | flops | bytes accessed | tf_op | source)
XLA Modules:
  0.0 1672.8 jit_solution(17522014106802311651)
XLA Ops:
  10.8 6.4 all-reduce.1
  18.2 16.0 all-gather.12.cloned.1.call-done
  34.2 3.6 fusion.23
  49.4 42.3 %reduce-scatter.12.cloned.1.call-done = f32[320,768]{1,0:T(8,128)} async-done(((f32[1280,768]{1,0:T(8,128)}), f32[320,768]{1,0:T(8,128)}) %reduce-scatter.12.cloned.1.call-update) | async-done | bytes 983056 | tf_op jit(solution)/shard_map/reduce_scatter | solution.py:99
  95.0 21.5 %all-gather.14.cloned.1.call-done = bf16[32,40,768]{2,1,0:T(8,128)(2,1)} async-done(((bf16[8,40,768]{2,1,0:T(8,128)(2,1)}), bf16[32,40,768]{2,1,0:T(8,128)(2,1)}) %all-gather.14.cloned.1.call-update) | async-done | bytes 1966096 | tf_op jit(solution)/shard_map/all_gather | solution.py:95
  116.5 13.0 multiply_convert_fusion.3
  130.8 3.7 fusion.158
  134.5 43.0 %reduce-scatter.14.cloned.1.call-done = f32[320,768]{1,0:T(8,128)} async-done(((f32[1280,768]{1,0:T(8,128)}), f32[320,768]{1,0:T(8,128)}) %reduce-scatter.14.cloned.1.call-update) | async-done | bytes 983056 | tf_op jit(solution)/shard_map/reduce_scatter | solution.py:99
  180.6 22.0 %all-gather.16.cloned.1.call-done = bf16[32,40,768]{2,1,0:T(8,128)(2,1)} async-done(((bf16[8,40,768]{2,1,0:T(8,128)(2,1)}), bf16[32,40,768]{2,1,0:T(8,128)(2,1)}) %all-gather.16.cloned.1.call-update) | async-done | bytes 1966096 | tf_op jit(solution)/shard_map/all_gather | solution.py:95
  218.1 3.8 fusion.159
  224.0 40.9 %reduce-scatter.16.cloned.1.call-done = f32[320,768]{1,0:T(8,128)} async-done(((f32[1280,768]{1,0:T(8,128)}), f32[320,768]{1,0:T(8,128)}) %reduce-scatter.16.cloned.1.call-update) | async-done | bytes 983056 | tf_op jit(solution)/shard_map/reduce_scatter | solution.py:99
  268.9 62.3 %all-gather.18.cloned.1.call-done = bf16[32,145,1024]{2,0,1:T(8,128)(2,1)} async-done(((bf16[8,145,1024]{2,0,1:T(8,128)(2,1)}), bf16[32,145,1024]{2,0,1:T(8,128)(2,1)}) %all-gather.18.cloned.1.call-update) | async-done | bytes 9502736 | tf_op jit(solution)/shard_map/all_gather | solution.py:198
  331.2 25.8 %fusion.5 = bf16[2,32,145,192]{3,2,1,0:T(8,128)(2,1)S(1)} fusion(f32[2,192]{1,0:T(2,128)S(1)} %pad_convert_fusion, bf16[32,145,1024]{2,0,1:T(8,128)(2,1)} %all-gather.18.cloned.1.call-done, bf16[2,1024,192]{1,2,0:T(8,128)(2,1)S(1)} %copy-done.143), kind=kOutput, calls=%fused_computation.11 | convolution fusion | flops 3652608000 | bytes 13854208 | tf_op jit(solution)/shard_map/ipf,cfe->cipe/dot_general | solution.py:201
  359.6 4.8 copy.154
  364.5 4.7 copy.153
  385.4 3.7 fusion.160
  389.3 43.0 %reduce-scatter.18.cloned.1.call-done = f32[320,768]{1,0:T(8,128)} async-done(((f32[1280,768]{1,0:T(8,128)}), f32[320,768]{1,0:T(8,128)}) %reduce-scatter.18.cloned.1.call-update) | async-done | bytes 983056 | tf_op jit(solution)/shard_map/reduce_scatter | solution.py:99
  435.6 21.9 %all-gather.22.cloned.1.call-done = bf16[32,40,768]{2,1,0:T(8,128)(2,1)} async-done(((bf16[8,40,768]{2,1,0:T(8,128)(2,1)}), bf16[32,40,768]{2,1,0:T(8,128)(2,1)}) %all-gather.22.cloned.1.call-update) | async-done | bytes 1966096 | tf_op jit(solution)/shard_map/all_gather | solution.py:95
  457.6 12.5 multiply_convert_fusion.2
  471.4 3.6 fusion.161
  475.5 42.6 %reduce-scatter.20.cloned.1.call-done = f32[320,768]{1,0:T(8,128)} async-done(((f32[1280,768]{1,0:T(8,128)}), f32[320,768]{1,0:T(8,128)}) %reduce-scatter.20.cloned.1.call-update) | async-done | bytes 983056 | tf_op jit(solution)/shard_map/reduce_scatter | solution.py:99
  522.5 22.0 %all-gather.24.cloned.1.call-done = bf16[32,40,768]{2,1,0:T(8,128)(2,1)} async-done(((bf16[8,40,768]{2,1,0:T(8,128)(2,1)}), bf16[32,40,768]{2,1,0:T(8,128)(2,1)}) %all-gather.24.cloned.1.call-update) | async-done | bytes 1966096 | tf_op jit(solution)/shard_map/all_gather | solution.py:117
  544.4 7.5 convert_reduce_fusion.1
  553.2 3.7 fusion.162
  557.0 43.0 %reduce-scatter.22.cloned.1.call-done = f32[320,768]{1,0:T(8,128)} async-done(((f32[1280,768]{1,0:T(8,128)}), f32[320,768]{1,0:T(8,128)}) %reduce-scatter.22.cloned.1.call-update) | async-done | bytes 983056 | tf_op jit(solution)/shard_map/reduce_scatter | solution.py:108
  600.0 3.7 fusion.88
  606.1 21.7 %all-gather.26.cloned.1.call-done = bf16[32,40,768]{2,1,0:T(8,128)(2,1)} async-done(((bf16[8,40,768]{2,1,0:T(8,128)(2,1)}), bf16[32,40,768]{2,1,0:T(8,128)(2,1)}) %all-gather.26.cloned.1.call-update) | async-done | bytes 1966096 | tf_op jit(solution)/shard_map/all_gather | solution.py:117
  630.2 4.0 reshape.639
  636.7 5.3 multiply_reduce_fusion
  646.8 3.5 fusion.122
  650.4 43.0 %reduce-scatter.24.cloned.1.call-done = f32[320,768]{1,0:T(8,128)} async-done(((f32[1280,768]{1,0:T(8,128)}), f32[320,768]{1,0:T(8,128)}) %reduce-scatter.24.cloned.1.call-update) | async-done | bytes 983056 | tf_op jit(solution)/shard_map/reduce_scatter | solution.py:108
  696.7 21.9 %all-gather.28.cloned.1.call-done = bf16[32,40,768]{2,1,0:T(8,128)(2,1)} async-done(((bf16[8,40,768]{2,1,0:T(8,128)(2,1)}), bf16[32,40,768]{2,1,0:T(8,128)(2,1)}) %all-gather.28.cloned.1.call-update) | async-done | bytes 1966096 | tf_op jit(solution)/shard_map/all_gather | solution.py:117
  721.0 4.0 reshape.640
  741.7 4.0 reshape.635
  748.8 4.0 reshape.633
  754.9 3.7 reshape.634
  758.6 5.1 convolution_bitcast_fusion.2
  763.8 43.0 %reduce-scatter.26.cloned.1.call-done = f32[320,768]{1,0:T(8,128)} async-done(((f32[1280,768]{1,0:T(8,128)}), f32[320,768]{1,0:T(8,128)}) %reduce-scatter.26.cloned.1.call-update) | async-done | bytes 983056 | tf_op jit(solution)/shard_map/reduce_scatter | solution.py:108
  810.1 22.0 %all-gather.30.cloned.1.call-done = bf16[32,40,768]{2,1,0:T(8,128)(2,1)} async-done(((bf16[8,40,768]{2,1,0:T(8,128)(2,1)}), bf16[32,40,768]{2,1,0:T(8,128)(2,1)}) %all-gather.30.cloned.1.call-update) | async-done | bytes 1966096 | tf_op jit(solution)/shard_map/all_gather | solution.py:117
  832.1 7.0 convert_reduce_fusion.2
  840.4 3.6 fusion.163
  844.1 43.0 %reduce-scatter.28.cloned.1.call-done = f32[320,768]{1,0:T(8,128)} async-done(((f32[1280,768]{1,0:T(8,128)}), f32[320,768]{1,0:T(8,128)}) %reduce-scatter.28.cloned.1.call-update) | async-done | bytes 983056 | tf_op jit(solution)/shard_map/reduce_scatter | solution.py:108
  891.3 4.0 multiply_convert_fusion
  895.3 5.0 copy.188
  900.2 5.4 convert_reduce_fusion
  905.6 4.8 copy.189
  910.4 12.8 convolution_bitcast_fusion
  926.6 4.0 reshape.641
  930.5 3.7 copy.174
  938.3 4.1 reshape.638
  951.1 3.7 reshape.636
  959.0 3.8 reshape.637
  962.8 4.9 convolution_bitcast_fusion.1
  970.6 3.5 convert_element_type.571
  974.1 3.6 convert_element_type.572
  977.7 5.4 fusion.167
  993.5 18.3 %fusion.64 = f32[2,1024,192]{1,2,0:T(8,128)} fusion(bf16[32,145,1024,1]{2,0,1,3:T(8,128)(2,1)} %bitcast.274, bf16[1,32,145,192]{3,2,0,1:T(8,128)(2,1)S(1)} %copy-done.53, bf16[1,32,145,192]{3,2,0,1:T(8,128)(2,1)S(1)} %copy-done.52), kind=kOutput, calls=%fused_computation.117 | convolution fusion | flops 3650826240 | bytes 14639104 | tf_op jit(solution)/shard_map/ipf,cipe->cfe/dot_general | solution.py:233
  1017.7 3.6 convert_element_type.563
  1022.8 3.8 fusion.52
  1042.8 3.7 convert_element_type.556
  1051.3 4.2 fusion.57
  1056.9 41.4 %all-reduce.2 = (f32[2,768]{1,0:T(2,128)}, f32[2,768]{1,0:T(2,128)}, f32[2,768]{1,0:T(2,128)}, f32[3,768]{1,0:T(4,128)}, f32[3,768]{1,0:T(4,128)}, /*index=5*/f32[3,768]{1,0:T(4,128)}) all-reduce(f32[2,768]{1,0:T(2,128)S(1)} %pad_maximum_fusion.9, ...), channel_id=1, replica_groups=mesh['dp'=8,'tensor'=4] {'dp','tensor'}, use_global_device_ids=true, to_apply=%region_51.52 | all-reduce | flops 11520 | bytes 92160 | tf_op jit(solution)/shard_map/psum | solution.py:415
  1098.4 37.3 %all-reduce.3 = (f32[2,192]{1,0:T(2,128)}, f32[768]{0:T(1024)}, f32[4,192]{1,0:T(4,128)}, f32[768]{0:T(1024)}) all-reduce(f32[2,192]{1,0:T(2,128)S(1)} %pad_maximum_fusion.13, f32[768]{0:T(1024)S(1)} %get-tuple-element.150, f32[4,192]{1,0:T(4,128)S(1)} %pad_maximum_fusion.12, ...), channel_id=1, replica_groups=mesh['dp'=8,'tensor'=4] {'dp'}, use_global_device_ids=true, to_apply=%region_43.44 | all-reduce | flops 2688 | bytes 21504 | tf_op jit(solution)/shard_map/psum | solution.py:390
  1143.4 505.2 %all-reduce.7.cloned.1.call-done = (f32[3,768,192]{1,2,0:T(8,128)}, f32[192,768]{1,0:T(8,128)}, f32[768,768]{1,0:T(8,128)}, f32[768,768]{1,0:T(8,128)}, f32[4,76...) async-done(((f32[3,768,192]{1,2,0:T(8,128)}, f32[192,768]{1,0:T(8,128)}, ...) | async-done | bytes 16908304 | tf_op jit(solution)/shard_map/psum | solution.py:390
  (524 shorter events, 210.1 us)
Async XLA Ops:
  7.2 450.4 %copy-start = (bf16[768,768]{1,0:T(8,128)(2,1)S(1)}, bf16[768,768]{1,0:T(8,128)(2,1)}, u32[]{:S(2)}) copy-start(bf16[768,768]{1,0:T(8,128)(2,1)} %param.44) | copy-start | bytes 3538948
  7.2 27.0 %all-gather.12.cloned.1.call-start = ((), (), s32[]{:S(2)}) async-start(), calls=%async_computation.11 | async-start | bytes 2457600 | tf_op jit(solution)/shard_map/all_gather | solution.py:287
  7.9 83.8 %reduce-scatter.12.cloned.1.call-start = ((), (), s32[]{:S(2)}) async-start(), calls=%async_computation.12 | async-start | bytes 4915200 | tf_op jit(solution)/shard_map/reduce_scatter | solution.py:99
  48.6 43.1 %copy-start.59 = (bf16[8,40,768]{2,1,0:T(8,128)(2,1)S(1)}, bf16[8,40,768]{2,1,0:T(8,128)(2,1)}, u32[]{:S(2)}) copy-start(bf16[8,40,768]{2,1,0:T(8,128)(2,1)} %param.25) | copy-start | bytes 1474564
  48.6 67.8 %all-gather.14.cloned.1.call-start = ((), (), s32[]{:S(2)}) async-start(), calls=%async_computation.13 | async-start | bytes 2457600 | tf_op jit(solution)/shard_map/all_gather | solution.py:95
  49.4 128.2 %copy-start.97 = (f32[768]{0:T(1024)}, f32[768]{0:T(1024)S(1)}, u32[]{:S(2)}) copy-start(f32[768]{0:T(1024)S(1)} %get-tuple-element.237) | copy-start | bytes 9220
  93.1 84.4 %copy-start.4 = (f32[8,40,768]{2,1,0:T(8,128)}, f32[8,40,768]{2,1,0:T(8,128)S(1)}, u32[]{:S(2)}) copy-start(f32[8,40,768]{2,1,0:T(8,128)S(1)} %get-tuple-element.177) | copy-start | bytes 2949124
  93.2 84.4 %copy-start.95 = (f32[8,40]{1,0:T(8,128)}, f32[8,40]{1,0:T(8,128)S(1)}, u32[]{:S(2)}) copy-start(f32[8,40]{1,0:T(8,128)S(1)} %broadcast_multiply_fusion.4) | copy-start | bytes 3844
  93.4 36.1 %copy-start.113 = (f32[8,40]{1,0:T(8,128)}, f32[8,40]{1,0:T(8,128)S(1)}, u32[]{:S(2)}) copy-start(f32[8,40]{1,0:T(8,128)S(1)} %multiply_reduce_fusion.16) | copy-start | bytes 3844
  93.4 84.1 %copy-start.99 = (f32[8,40]{1,0:T(8,128)}, f32[8,40]{1,0:T(8,128)S(1)}, u32[]{:S(2)}) copy-start(f32[8,40]{1,0:T(8,128)S(1)} %fusion.126) | copy-start | bytes 3844
  94.5 83.1 %reduce-scatter.14.cloned.1.call-start = ((), (), s32[]{:S(2)}) async-start(), calls=%async_computation.14 | async-start | bytes 4915200 | tf_op jit(solution)/shard_map/reduce_scatter | solution.py:99
  116.5 14.3 copy-start.141
  134.5 68.0 %all-gather.16.cloned.1.call-start = ((), (), s32[]{:S(2)}) async-start(), calls=%async_computation.15 | async-start | bytes 2457600 | tf_op jit(solution)/shard_map/all_gather | solution.py:95
  179.2 23.3 %copy-start.109 = (bf16[4,768,192]{1,2,0:T(8,128)(2,1)S(1)}, bf16[4,768,192]{1,2,0:T(8,128)(2,1)}, u32[]{:S(2)}) copy-start(bf16[4,768,192]{1,2,0:T(8,128)(2,1)} %param.39) | copy-start | bytes 3538948
  179.5 23.1 %copy-start.115 = (f32[8,40]{1,0:T(8,128)}, f32[8,40]{1,0:T(8,128)S(1)}, u32[]{:S(2)}) copy-start(f32[8,40]{1,0:T(8,128)S(1)} %multiply_reduce_fusion.15) | copy-start | bytes 3844
  180.5 84.4 %reduce-scatter.16.cloned.1.call-start = ((), (), s32[]{:S(2)}) async-start(), calls=%async_computation.16 | async-start | bytes 4915200 | tf_op jit(solution)/shard_map/reduce_scatter | solution.py:99
  221.9 109.3 %all-gather.18.cloned.1.call-start = ((), (), s32[]{:S(2)}) async-start(), calls=%async_computation.17 | async-start | bytes 11878400 | tf_op jit(solution)/shard_map/all_gather | solution.py:198
  222.7 146.5 %all-gather.20.cloned.1.call-start = ((), (), s32[]{:S(2)}) async-start(), calls=%async_computation.18 | async-start | bytes 2457600 | tf_op jit(solution)/shard_map/all_gather | solution.py:95
  224.0 44.6 %copy-start.104 = (f32[768]{0:T(1024)}, f32[768]{0:T(1024)S(1)}, u32[]{:S(2)}) copy-start(f32[768]{0:T(1024)S(1)} %get-tuple-element.239) | copy-start | bytes 9220
  224.0 44.6 %copy-start.111 = (f32[768]{0:T(1024)}, f32[768]{0:T(1024)S(1)}, u32[]{:S(2)}) copy-start(f32[768]{0:T(1024)S(1)} %get-tuple-element.118) | copy-start | bytes 9220
  264.9 66.3 %copy-start.143 = (bf16[2,1024,192]{1,2,0:T(8,128)(2,1)S(1)}, bf16[2,1024,192]{1,2,0:T(8,128)(2,1)}, u32[]{:S(2)}) copy-start(bf16[2,1024,192]{1,2,0:T(8,128)(2,1)} %param.43) | copy-start | bytes 2359300
  266.9 90.2 %copy-start.117 = (f32[8,40]{1,0:T(8,128)}, f32[8,40]{1,0:T(8,128)S(1)}, u32[]{:S(2)}) copy-start(f32[8,40]{1,0:T(8,128)S(1)} %multiply_reduce_fusion.14) | copy-start | bytes 3844
  266.9 90.2 %copy-start.101 = (f32[8,40]{1,0:T(8,128)}, f32[8,40]{1,0:T(8,128)S(1)}, u32[]{:S(2)}) copy-start(f32[8,40]{1,0:T(8,128)S(1)} %fusion.128) | copy-start | bytes 3844
  268.7 163.6 %reduce-scatter.18.cloned.1.call-start = ((), (), s32[]{:S(2)}) async-start(), calls=%async_computation.19 | async-start | bytes 4915200 | tf_op jit(solution)/shard_map/reduce_scatter | solution.py:99
  389.2 43.1 %copy-start.102 = (f32[8,40]{1,0:T(8,128)S(1)}, f32[8,40]{1,0:T(8,128)}, u32[]{:S(2)}) copy-start(f32[8,40]{1,0:T(8,128)} %copy-done.101) | copy-start | bytes 3844
  389.2 43.1 %copy-start.105 = (f32[768]{0:T(1024)S(1)}, f32[768]{0:T(1024)}, u32[]{:S(2)}) copy-start(f32[768]{0:T(1024)} %copy-done.104) | copy-start | bytes 9220
  389.2 43.1 %copy-start.112 = (f32[768]{0:T(1024)S(1)}, f32[768]{0:T(1024)}, u32[]{:S(2)}) copy-start(f32[768]{0:T(1024)} %copy-done.111) | copy-start | bytes 9220
  389.2 43.1 %copy-start.126 = (f32[768]{0:T(1024)S(1)}, f32[768]{0:T(1024)}, u32[]{:S(2)}) copy-start(f32[768]{0:T(1024)} %get-tuple-element.120) | copy-start | bytes 9220
  389.2 45.3 %copy-start.107 = (f32[768]{0:T(1024)S(1)}, f32[768]{0:T(1024)}, u32[]{:S(2)}) copy-start(f32[768]{0:T(1024)} %get-tuple-element.240) | copy-start | bytes 9220
  389.2 45.3 %copy-start.110 = (f32[768]{0:T(1024)S(1)}, f32[768]{0:T(1024)}, u32[]{:S(2)}) copy-start(f32[768]{0:T(1024)} %get-tuple-element.117) | copy-start | bytes 9220
  389.3 68.3 %all-gather.22.cloned.1.call-start = ((), (), s32[]{:S(2)}) async-start(), calls=%async_computation.20 | async-start | bytes 2457600 | tf_op jit(solution)/shard_map/all_gather | solution.py:95
  435.6 82.5 %reduce-scatter.20.cloned.1.call-start = ((), (), s32[]{:S(2)}) async-start(), calls=%async_computation.21 | async-start | bytes 4915200 | tf_op jit(solution)/shard_map/reduce_scatter | solution.py:99
  475.0 43.1 %copy-start.125 = (f32[768]{0:T(1024)S(1)}, f32[768]{0:T(1024)}, u32[]{:S(2)}) copy-start(f32[768]{0:T(1024)} %get-tuple-element.119) | copy-start | bytes 9220
  475.0 44.8 %copy-start.108 = (f32[768]{0:T(1024)S(1)}, f32[768]{0:T(1024)}, u32[]{:S(2)}) copy-start(f32[768]{0:T(1024)} %get-tuple-element.241) | copy-start | bytes 9220
  475.0 69.4 %all-gather.24.cloned.1.call-start = ((), (), s32[]{:S(2)}) async-start(), calls=%async_computation.22 | async-start | bytes 2457600 | tf_op jit(solution)/shard_map/all_gather | solution.py:117
  522.4 77.6 %reduce-scatter.22.cloned.1.call-start = ((), (), s32[]{:S(2)}) async-start(), calls=%async_computation.23 | async-start | bytes 4915200 | tf_op jit(solution)/shard_map/reduce_scatter | solution.py:108
  556.9 43.1 %copy-start.14 = (f32[8,40,768]{2,1,0:T(8,128)S(1)}, f32[8,40,768]{2,1,0:T(8,128)}, u32[]{:S(2)}) copy-start(f32[8,40,768]{2,1,0:T(8,128)} %copy-done.13) | copy-start | bytes 2949124
  556.9 43.1 %copy-start.127 = (f32[768]{0:T(1024)S(1)}, f32[768]{0:T(1024)}, u32[]{:S(2)}) copy-start(f32[768]{0:T(1024)} %get-tuple-element.116) | copy-start | bytes 9220
  556.9 70.9 %all-gather.26.cloned.1.call-start = ((), (), s32[]{:S(2)}) async-start(), calls=%async_computation.24 | async-start | bytes 2457600 | tf_op jit(solution)/shard_map/all_gather | solution.py:117
  603.7 24.1 %copy-start.81 = (bf16[192,768]{1,0:T(8,128)(2,1)S(1)}, bf16[192,768]{1,0:T(8,128)(2,1)}, u32[]{:S(2)}) copy-start(bf16[192,768]{1,0:T(8,128)(2,1)} %param.42) | copy-start | bytes 884740
  604.1 26.1 %copy-start.34 = (f32[8,40,768]{2,1,0:T(8,128)}, f32[8,40,768]{2,1,0:T(8,128)S(1)}, u32[]{:S(2)}) copy-start(f32[8,40,768]{2,1,0:T(8,128)S(1)} %get-tuple-element.162) | copy-start | bytes 2949124
  605.8 87.6 %reduce-scatter.24.cloned.1.call-start = ((), (), s32[]{:S(2)}) async-start(), calls=%async_computation.25 | async-start | bytes 4915200 | tf_op jit(solution)/shard_map/reduce_scatter | solution.py:108
  650.3 43.1 %copy-start.7 = (f32[8,40,768]{2,1,0:T(8,128)S(1)}, f32[8,40,768]{2,1,0:T(8,128)}, u32[]{:S(2)}) copy-start(f32[8,40,768]{2,1,0:T(8,128)} %copy-done.6) | copy-start | bytes 2949124
  650.3 43.1 %copy-start.103 = (f32[8,40]{1,0:T(8,128)S(1)}, f32[8,40]{1,0:T(8,128)}, u32[]{:S(2)}) copy-start(f32[8,40]{1,0:T(8,128)} %copy-done.101) | copy-start | bytes 3844
  650.3 43.1 %copy-start.106 = (f32[768]{0:T(1024)S(1)}, f32[768]{0:T(1024)}, u32[]{:S(2)}) copy-start(f32[768]{0:T(1024)} %copy-done.104) | copy-start | bytes 9220
  650.3 43.1 %copy-start.35 = (f32[8,40,768]{2,1,0:T(8,128)S(1)}, f32[8,40,768]{2,1,0:T(8,128)}, u32[]{:S(2)}) copy-start(f32[8,40,768]{2,1,0:T(8,128)} %copy-done.34) | copy-start | bytes 2949124
  650.4 44.8 %copy-start.118 = (f32[8,40]{1,0:T(8,128)S(1)}, f32[8,40]{1,0:T(8,128)}, u32[]{:S(2)}) copy-start(f32[8,40]{1,0:T(8,128)} %copy-done.117) | copy-start | bytes 3844
  650.4 68.2 %all-gather.28.cloned.1.call-start = ((), (), s32[]{:S(2)}) async-start(), calls=%async_computation.26 | async-start | bytes 2457600 | tf_op jit(solution)/shard_map/all_gather | solution.py:117
  695.2 23.4 %copy-start.82 = (bf16[192,768]{1,0:T(8,128)(2,1)S(1)}, bf16[192,768]{1,0:T(8,128)(2,1)}, u32[]{:S(2)}) copy-start(bf16[192,768]{1,0:T(8,128)(2,1)} %param.41) | copy-start | bytes 884740
  696.6 110.2 %reduce-scatter.26.cloned.1.call-start = ((), (), s32[]{:S(2)}) async-start(), calls=%async_computation.27 | async-start | bytes 4915200 | tf_op jit(solution)/shard_map/reduce_scatter | solution.py:108
  763.7 45.0 %copy-start.116 = (f32[8,40]{1,0:T(8,128)S(1)}, f32[8,40]{1,0:T(8,128)}, u32[]{:S(2)}) copy-start(f32[8,40]{1,0:T(8,128)} %copy-done.115) | copy-start | bytes 3844
  763.7 68.4 %all-gather.30.cloned.1.call-start = ((), (), s32[]{:S(2)}) async-start(), calls=%async_computation.28 | async-start | bytes 2457600 | tf_op jit(solution)/shard_map/all_gather | solution.py:117
  810.1 77.0 %reduce-scatter.28.cloned.1.call-start = ((), (), s32[]{:S(2)}) async-start(), calls=%async_computation.29 | async-start | bytes 4915200 | tf_op jit(solution)/shard_map/reduce_scatter | solution.py:108
  844.0 43.1 %copy-start.5 = (f32[8,40,768]{2,1,0:T(8,128)S(1)}, f32[8,40,768]{2,1,0:T(8,128)}, u32[]{:S(2)}) copy-start(f32[8,40,768]{2,1,0:T(8,128)} %copy-done.4) | copy-start | bytes 2949124
  844.0 43.1 %copy-start.96 = (f32[8,40]{1,0:T(8,128)S(1)}, f32[8,40]{1,0:T(8,128)}, u32[]{:S(2)}) copy-start(f32[8,40]{1,0:T(8,128)} %copy-done.95) | copy-start | bytes 3844
  844.0 43.1 %copy-start.98 = (f32[768]{0:T(1024)S(1)}, f32[768]{0:T(1024)}, u32[]{:S(2)}) copy-start(f32[768]{0:T(1024)} %copy-done.97) | copy-start | bytes 9220
  844.0 43.1 %copy-start.100 = (f32[8,40]{1,0:T(8,128)S(1)}, f32[8,40]{1,0:T(8,128)}, u32[]{:S(2)}) copy-start(f32[8,40]{1,0:T(8,128)} %copy-done.99) | copy-start | bytes 3844
  844.0 44.8 %copy-start.114 = (f32[8,40]{1,0:T(8,128)S(1)}, f32[8,40]{1,0:T(8,128)}, u32[]{:S(2)}) copy-start(f32[8,40]{1,0:T(8,128)} %copy-done.113) | copy-start | bytes 3844
  844.0 80.0 %all-gather.32.cloned.1.call-start = ((), (), s32[]{:S(2)}) async-start(), calls=%async_computation.30 | async-start | bytes 2457600 | tf_op jit(solution)/shard_map/all_gather | solution.py:117
  891.2 244.5 %reduce-scatter.32.cloned.1.call-start = ((), (), s32[]{:S(2)}) async-start(), calls=%async_computation.32 | async-start | bytes 24903680 | tf_op jit(solution)/shard_map/reduce_scatter | solution.py:236
  923.2 218.1 %reduce-scatter.30.cloned.1.call-start = ((), (), s32[]{:S(2)}) async-start(), calls=%async_computation.31 | async-start | bytes 4915200 | tf_op jit(solution)/shard_map/reduce_scatter | solution.py:108
  967.8 680.8 %all-reduce.7.cloned.1.call-start = ((), (), s32[]{:S(2)}) async-start(), calls=%async_computation.33 | async-start | bytes 33816576 | tf_op jit(solution)/shard_map/psum | solution.py:390
  993.5 18.3 %copy-start.27 = (bf16[32,3,64,40]{2,3,1,0:T(8,128)(2,1)S(1)}, bf16[32,3,64,40]{2,3,1,0:T(8,128)(2,1)}, u32[]{:S(2)}) copy-start(bf16[32,3,64,40]{2,3,1,0:T(8,128)(2,1)} %copy-done.26) | copy-start | bytes 1474564
  1055.6 42.9 %copy-start.133 = (f32[768]{0:T(1024)S(1)}, f32[768]{0:T(1024)}, u32[]{:S(2)}) copy-start(f32[768]{0:T(1024)} %get-tuple-element.148) | copy-start | bytes 9220
  (104 other events, 292.9 us)
Sparse Core Ops, SparseCore 0:
  9.6 24.5 all-gather.11
  48.8 42.9 reduce-scatter.11
  94.6 21.8 all-gather.13
  134.6 42.8 reduce-scatter.13
  180.6 21.8 all-gather.15
  222.0 42.8 reduce-scatter.15
  266.6 64.6 all-gather.17
  333.5 21.8 all-gather.19
  389.4 42.8 reduce-scatter.17
  435.7 21.8 all-gather.21
  475.1 42.8 reduce-scatter.19
  522.5 21.8 all-gather.23
  557.0 42.8 reduce-scatter.21
  605.9 21.8 all-gather.25
  650.5 42.8 reduce-scatter.23
  696.7 21.8 all-gather.27
  763.8 42.8 reduce-scatter.25
  810.2 21.8 all-gather.29
  844.2 42.8 reduce-scatter.27
  891.3 21.8 all-gather.31
  923.3 146.8 reduce-scatter.31
  1072.7 43.4 reduce-scatter.29
  1125.5 523.0 all-reduce.6
where the time goes:
time: 1680 us; the launch traced here: 1670 us
  waiting for transfers between devices  1120 us (67%)
  matrix products  232 us (14%)
  local copies, waits for them, and re-layouts  171 us (10%)
  blocking collectives  85.1 us (5%)
  other arithmetic  43.9 us (3%)
  between operations  16.9 us (1%)
    psum x1, waiting for transfers between devices, per_device(): lax.psum((grads_one[0], grads_one[1], grads_one[2], grads_two[0], grads_t...  505 us
    reduce_scatter x5, waiting for transfers between devices, branch_sum(): lax.psum_scatter(jnp.dot(inputs, weight, preferred_element_type=jnp.float...  212 us
    reduce_scatter x5, waiting for transfers between devices, input_grads(): lax.psum_scatter(jnp.einsum('cre,cde->rd', grad_stack, weights, preferred...  172 us
    all_gather x5, waiting for transfers between devices, output_back(): lax.all_gather(grad_pre.astype(jnp.bfloat16), 'tensor', axis=0, tiled=True)  87.6 us
    all_gather x4, waiting for transfers between devices, spread_rows(): return lax.all_gather(row_block, 'tensor', axis=0, tiled=True)  65.4 us
    all_gather x1, waiting for transfers between devices, cross_forward(): patch_all = lax.all_gather(patch_local, 'tensor', axis=0, tiled=True)  62.3 us
    psum x1, blocking collectives, per_device(): lax.psum((text_bias_grad, text_gain_grad, text_shift_grad, join_out_grad,...  41.4 us
    unnamed x304, local copies, waits for them, and re-layouts  41.3 us
  transfers between devices with their start and end apart: 23, of which 19 were waited for; matrix products, arithmetic and copies ran while one was open for 13% of the time, Pallas kernels for 0%

commit v1 on v0

v1 whole, which is shorter than its diff:
```python
import functools

import jax
import jax.numpy as jnp
from jax import lax
from jax.experimental import pallas as pl
from jax.experimental.pallas import tpu as pltpu
from jax.sharding import PartitionSpec as P

HEAD_DIM = 64
BF = jnp.bfloat16
F32 = jnp.float32
ANY = pl.ANY
VMEM_LIMIT = 56 * 1024 * 1024


def dot_nn(a, b):
    return lax.dot_general(a, b, (((1,), (0,)), ((), ())), preferred_element_type=F32)


def dot_nt(a, b):
    return lax.dot_general(a, b, (((1,), (1,)), ((), ())), preferred_element_type=F32)


def dot_tn(a, b):
    return lax.dot_general(a, b, (((0,), (0,)), ((), ())), preferred_element_type=F32)


def norm_forward(e, gain, shift):
    center = e - jnp.mean(e, axis=-1, keepdims=True)
    variance = jnp.mean(center * center, axis=-1, keepdims=True)
    return center * lax.rsqrt(variance + 1e-12) * gain + shift


def norm_backward(e, gain, dy):
    center = e - jnp.mean(e, axis=-1, keepdims=True)
    variance = jnp.mean(center * center, axis=-1, keepdims=True)
    rstd = lax.rsqrt(variance + 1e-12)
    normed = center * rstd
    scaled = dy * gain
    de = rstd * (
        scaled
        - jnp.mean(scaled, axis=-1, keepdims=True)
        - normed * jnp.mean(scaled * normed, axis=-1, keepdims=True)
    )
    sums = jnp.concatenate(
        [
            jnp.sum(de, axis=0, keepdims=True),
            jnp.sum(dy * normed, axis=0, keepdims=True),
            jnp.sum(dy, axis=0, keepdims=True),
        ],
        axis=0,
    )
    return de, sums


def head_masks(width):
    lane = lax.broadcasted_iota(jnp.int32, (1, width), 1)
    return [
        ((lane >= h * HEAD_DIM) & (lane < (h + 1) * HEAD_DIM)).astype(F32)
        for h in range(width // HEAD_DIM)
    ]


def stack_heads(rows, masks):
    return jnp.concatenate([rows * mask for mask in masks], axis=0).astype(BF)


def merge_heads(stacked, masks):
    count = stacked.shape[0] // len(masks)
    total = stacked[:count] * masks[0]
    for h in range(1, len(masks)):
        total = total + stacked[h * count : (h + 1) * count] * masks[h]
    return total


def item_forward(q, k, v, masks, length):
    scores = dot_nt(stack_heads(q, masks), k) * HEAD_DIM ** (-0.5)
    column = lax.broadcasted_iota(jnp.int32, scores.shape, 1)
    scores = jnp.where(column < length, scores, -1e30)
    weights = jnp.exp(scores - jnp.max(scores, axis=-1, keepdims=True))
    probs = (weights / jnp.sum(weights, axis=-1, keepdims=True)).astype(BF)
    return probs, merge_heads(dot_nn(probs, v), masks)


def item_backward(q, k, v, da, probs, masks):
    qs = stack_heads(q, masks)
    das = stack_heads(da, masks)
    dv = dot_tn(probs, das)
    dp = dot_nt(das, v)
    p = probs.astype(F32)
    ds = (p * (dp - jnp.sum(p * dp, axis=-1, keepdims=True))).astype(BF)
    scaling = HEAD_DIM ** (-0.5)
    dq = merge_heads(dot_nn(ds, k), masks) * scaling
    dk = dot_tn(ds, qs) * scaling
    return dq, dk, dv


def fetch_start(sources, target, sem):
    for r in range(len(sources)):
        pltpu.make_async_copy(sources[r], target.at[r], sem.at[r]).start()


def fetch_wait(sources, target, sem, r):
    pltpu.make_async_copy(sources[0], target.at[r], sem.at[r]).wait()


def ffn_forward_kernel(u, *refs):
    w1, w2 = refs[0:4], refs[4:8]
    c1, vec, y, e_out, h_out, slope_out, w1_s, w2_s, ub, acc, sem1, sem2 = refs[8:]
    step = pl.program_id(0)

    @pl.when(step == 0)
    def _():
        fetch_start(w1, w1_s, sem1)
        fetch_start(w2, w2_s, sem2)
        ub[...] = u[...].astype(BF)
        acc[...] = u[...] + vec[0:1, :]

    for j in range(2):
        r = 2 * step + j
        fetch_wait(w1, w1_s, sem1, r)
        z = dot_nn(ub[...], w1_s[r]) + c1[r]
        cdf = 0.5 * (1.0 + lax.erf(z * 0.7071067811865476))
        slope = cdf + z * (jnp.exp(-0.5 * z * z) * 0.3989422804014327)
        h = (z * cdf).astype(BF)
        h_out[j] = h
        slope_out[j] = slope.astype(BF)
        fetch_wait(w2, w2_s, sem2, r)
        acc[...] += dot_nn(h, w2_s[r])

    @pl.when(step == 1)
    def _():
        e = acc[...]
        e_out[...] = e
        y[...] = norm_forward(e, vec[1:2, :], vec[2:3, :]).astype(y.dtype)


def ffn_backward_kernel(has_grad, *refs):
    if has_grad:
        grad, refs = refs[0], refs[1:]
    cot, e_in, u = refs[0:3]
    w1, w2 = refs[3:7], refs[7:11]
    h_in, slope_in, vec = refs[11:14]
    du, g1k, g1s, g2k, g2s, dc1, sums = refs[14:21]
    w1_s, w2_s, ub, dob, acc, sem1, sem2 = refs[21:]
    step = pl.program_id(0)

    @pl.when(step == 0)
    def _():
        fetch_start(w2, w2_s, sem2)
        fetch_start(w1, w1_s, sem1)
        dy = cot[...].astype(F32)
        if has_grad:
            dy = dy + grad[...]
        de, partial = norm_backward(e_in[...], vec[1:2, :], dy)
        sums[...] = partial
        dob[...] = de.astype(BF)
        acc[...] = de
        ub[...] = u[...].astype(BF)

    for j in range(2):
        r = 2 * step + j
        fetch_wait(w2, w2_s, sem2, r)
        dh = dot_nt(dob[...], w2_s[r])
        dz = (dh * slope_in[j].astype(F32)).astype(BF)
        (g2k if j == 0 else g2s)[0] = dot_tn(h_in[j], dob[...]).astype(BF)
        (g1k if j == 0 else g1s)[0] = dot_tn(ub[...], dz).astype(BF)
        dc1[0, j : j + 1, :] = jnp.sum(dz.astype(F32), axis=0, keepdims=True)
        fetch_wait(w1, w1_s, sem1, r)
        acc[...] += dot_nt(dz, w1_s[r])

    @pl.when(step == 1)
    def _():
        du[...] = acc[...]


def self_forward_kernel(items, lengths, x, *refs):
    w = refs[0:4]
    bias, vec, y, e_out, q_out, k_out, v_out, p_out, a_out = refs[4:13]
    w_s, acc, q_s, k_s, v_s, a_s, sem = refs[13:]
    step = pl.program_id(0)
    width = q_s.shape[1]
    slots = x.shape[0] // items

    @pl.when(step == 0)
    def _():
        fetch_start(w, w_s, sem)
        acc[...] = x[...].astype(F32) + vec[0:1, :]

    masks = head_masks(width)
    for j in range(2):
        r = 2 * step + j
        fetch_wait(w, w_s, sem, r)
        xb = x[...]
        q = (dot_nt(xb, w_s[r, 0:width]) + bias[r, 0:1]).astype(BF)
        k = dot_nt(xb, w_s[r, width : 2 * width]).astype(BF)
        v = (dot_nt(xb, w_s[r, 2 * width : 3 * width]) + bias[r, 1:2]).astype(BF)
        q_out[j], k_out[j], v_out[j] = q, k, v
        q_s[...], k_s[...], v_s[...] = q.astype(F32), k.astype(F32), v.astype(F32)
        for i in range(items):
            rows = pl.ds(i * slots, slots)
            probs, a = item_forward(
                q_s[rows], k_s[rows].astype(BF), v_s[rows].astype(BF), masks, lengths[i]
            )
            p_out[j, i] = probs
            a_s[rows] = a
        ab = a_s[...].astype(BF)
        a_out[j] = ab
        acc[...] += dot_nn(ab, w_s[r, 3 * width : 4 * width])

    @pl.when(step == 1)
    def _():
        e = acc[...]
        e_out[...] = e
        y[...] = norm_forward(e, vec[1:2, :], vec[2:3, :]).astype(y.dtype)


def self_backward_kernel(items, dy, e_in, x, *refs):
    w = refs[0:4]
    q_in, k_in, v_in, p_in, a_in, vec = refs[4:10]
    du, gk, gs, db, sums = refs[10:15]
    w_s, dob, acc, q_s, k_s, v_s, da_s, dq_s, dk_s, dv_s, sem = refs[15:]
    step = pl.program_id(0)
    width = q_s.shape[1]
    slots = x.shape[0] // items

    @pl.when(step == 0)
    def _():
        fetch_start(w, w_s, sem)
        de, partial = norm_backward(e_in[...], vec[1:2, :], dy[...])
        sums[...] = partial
        dob[...] = de.astype(BF)
        acc[...] = de

    masks = head_masks(width)
    for j in range(2):
        r = 2 * step + j
        g = gk if j == 0 else gs
        fetch_wait(w, w_s, sem, r)
        da_s[...] = dot_nt(dob[...], w_s[r, 3 * width : 4 * width])
        g[0, 3 * width : 4 * width] = dot_tn(a_in[j], dob[...]).astype(BF)
        q_s[...], k_s[...], v_s[...] = (
            q_in[j].astype(F32),
            k_in[j].astype(F32),
            v_in[j].astype(F32),
        )
        for i in range(items):
            rows = pl.ds(i * slots, slots)
            dq, dk, dv = item_backward(
                q_s[rows],
                k_s[rows].astype(BF),
                v_s[rows].astype(BF),
                da_s[rows],
                p_in[j, i],
                masks,
            )
            dq_s[rows], dk_s[rows], dv_s[rows] = dq, dk, dv
        xb = x[...]
        total = acc[...]
        for c, part in enumerate((dq_s, dk_s, dv_s)):
            pb = part[...].astype(BF)
            g[0, c * width : (c + 1) * width] = dot_tn(pb, xb).astype(BF)
            total = total + dot_nn(pb, w_s[r, c * width : (c + 1) * width])
            if c != 1:
                db[0, j, c // 2 : c // 2 + 1, :] = jnp.sum(
                    pb.astype(F32), axis=0, keepdims=True
                )
        acc[...] = total

    @pl.when(step == 1)
    def _():
        du[...] = acc[...].astype(du.dtype)


def key_value_weight(w_s, r, start, width, model):
    low = w_s[r, pl.ds(start, 2 * width)]
    tail = w_s[r, pl.ds(start + 2 * width, 2 * width * (1024 - model) // model)]
    side = 1024 - model
    high = jnp.concatenate(
        [tail[:, c * side : (c + 1) * side] for c in range(model // side)], axis=0
    )
    return low, high


def cross_forward_kernel(items, patches, u, pf, *refs):
    w = refs[0:4]
    bias, vec, y, e_out, q_out, k_out, v_out, p_out, a_out = refs[4:13]
    w_s, ub, acc, q_s, a_s, sem = refs[13:]
    step = pl.program_id(0)
    width = q_s.shape[1]
    model = u.shape[1]
    slots = u.shape[0] // items
    padded = pf.shape[0] // items

    @pl.when(step == 0)
    def _():
        fetch_start(w, w_s, sem)
        ub[...] = u[...].astype(BF)
        acc[...] = u[...] + vec[0:1, :]

    masks = head_masks(width)
    for j in range(2):
        r = 2 * step + j
        fetch_wait(w, w_s, sem, r)
        q_b = (dot_nt(ub[...], w_s[r, 0:width]) + bias[r, 0:1]).astype(BF)
        q_out[j] = q_b
        q_s[...] = q_b.astype(F32)
        low, high = key_value_weight(w_s, r, 2 * width, width, model)
        chunk = 2 * padded
        for m in range(items // 2):
            rows = slice(m * chunk, (m + 1) * chunk)
            left, right = pf[rows, 0:model], pf[rows, model:]
            k_out[j, rows] = (
                dot_nt(left, low[0:width]) + dot_nt(right, high[0:width])
            ).astype(BF)
            v_out[j, rows] = (
                dot_nt(left, low[width:]) + dot_nt(right, high[width:]) + bias[r, 1:2]
            ).astype(BF)
        for i in range(items):
            rows = pl.ds(i * slots, slots)
            keys = pl.ds(i * padded, padded)
            probs, a = item_forward(
                q_s[rows], k_out[j, keys], v_out[j, keys], masks, patches
            )
            p_out[j, i] = probs
            a_s[rows] = a
        ab = a_s[...].astype(BF)
        a_out[j] = ab
        acc[...] += dot_nn(ab, w_s[r, width : 2 * width])

    @pl.when(step == 1)
    def _():
        e = acc[...]
        e_out[...] = e
        y[...] = norm_forward(e, vec[1:2, :], vec[2:3, :]).astype(y.dtype)


def cross_backward_kernel(items, patches, dy, e_in, u, pf, *refs):
    w = refs[0:4]
    q_in, k_in, v_in, p_in, a_in, vec = refs[4:10]
    du, dpf, gk, gs, db, sums = refs[10:16]
    w_s, ub, dob, acc, pacc, q_s, da_s, dq_s, dkv_s, sem = refs[16:]
    step = pl.program_id(0)
    width = q_s.shape[1]
    model = u.shape[1]
    side = pf.shape[1] - model
    slots = u.shape[0] // items
    padded = pf.shape[0] // items

    @pl.when(step == 0)
    def _():
        fetch_start(w, w_s, sem)
        de, partial = norm_backward(e_in[...], vec[1:2, :], dy[...])
        sums[...] = partial
        dob[...] = de.astype(BF)
        acc[...] = de
        ub[...] = u[...].astype(BF)
        pacc[...] = jnp.zeros_like(pacc)

    masks = head_masks(width)
    for j in range(2):
        r = 2 * step + j
        g = gk if j == 0 else gs
        fetch_wait(w, w_s, sem, r)
        da_s[...] = dot_nt(dob[...], w_s[r, width : 2 * width])
        g[0, width : 2 * width] = dot_tn(a_in[j], dob[...]).astype(BF)
        q_s[...] = q_in[j].astype(F32)
        vsum = jnp.zeros((1, width), F32)
        for i in range(items):
            rows = pl.ds(i * slots, slots)
            keys = pl.ds(i * padded, padded)
            dq, dk, dv = item_backward(
                q_s[rows], k_in[j, keys], v_in[j, keys], da_s[rows], p_in[j, i], masks
            )
            dq_s[rows] = dq
            dkv_s[0, keys] = dk.astype(BF)
            dvb = dv.astype(BF)
            dkv_s[1, keys] = dvb
            vsum = vsum + jnp.sum(dvb.astype(F32), axis=0, keepdims=True)
        dqb = dq_s[...].astype(BF)
        g[0, 0:width] = dot_tn(dqb, ub[...]).astype(BF)
        acc[...] += dot_nn(dqb, w_s[r, 0:width])
        db[0, j, 0:1, :] = jnp.sum(dqb.astype(F32), axis=0, keepdims=True)
        db[0, j, 1:2, :] = vsum
        low, high = key_value_weight(w_s, r, 2 * width, width, model)
        tails = []
        for c in range(2):
            part = dkv_s[c]
            g[0, (2 + c) * width : (3 + c) * width] = dot_tn(part, pf[:, 0:model]).astype(BF)
            tails.append(dot_tn(part, pf[:, model:]).astype(BF))
            pacc[:, 0:model] += dot_nn(part, low[c * width : (c + 1) * width])
            pacc[:, model:] += dot_nn(part, high[c * width : (c + 1) * width])
        tail = jnp.concatenate(tails, axis=0)
        count = tail.shape[0] // (model // side)
        for c in range(model // side):
            g[0, 4 * width : 4 * width + count, c * side : (c + 1) * side] = tail[
                c * count : (c + 1) * count
            ]

    @pl.when(step == 1)
    def _():
        du[...] = acc[...]
        for i in range(items):
            dpf[i] = pacc[i * padded : i * padded + patches, :].astype(BF)


def whole(shape):
    zeros = (0,) * len(shape)
    return pl.BlockSpec(shape, lambda p: zeros)


def halves(shape):
    zeros = (0,) * (len(shape) - 1)
    return pl.BlockSpec((shape[0] // 2,) + tuple(shape[1:]), lambda p: (p,) + zeros)


def call(kernel, name, operands, outputs, scratch, flops, transcendentals=0):
    kinds = {
        "whole": lambda s: whole(s),
        "half": lambda s: halves(s),
        "any": lambda s: pl.BlockSpec(memory_space=ANY),
        "smem": lambda s: pl.BlockSpec(memory_space=pltpu.SMEM),
    }
    size = sum(a.size * a.dtype.itemsize for a, _ in operands)
    for shape, dtype, _ in outputs:
        count = jnp.dtype(dtype).itemsize
        for extent in shape:
            count *= extent
        size += count
    return pl.pallas_call(
        kernel,
        grid=(2,),
        in_specs=[kinds[kind](a.shape) for a, kind in operands],
        out_specs=[kinds[kind](shape) for shape, _, kind in outputs],
        out_shape=[jax.ShapeDtypeStruct(shape, dtype) for shape, dtype, _ in outputs],
        scratch_shapes=scratch,
        compiler_params=pltpu.CompilerParams(
            dimension_semantics=("arbitrary",), vmem_limit_bytes=VMEM_LIMIT
        ),
        cost_estimate=pl.CostEstimate(
            flops=flops, bytes_accessed=size, transcendentals=transcendentals
        ),
        name=name,
    )(*[a for a, _ in operands])


def feed_forward(u, w1, w2, c1, vec, name):
    rows, model = u.shape
    hidden = w1[0].shape[1]
    outs = call(
        ffn_forward_kernel,
        name,
        [(u, "whole")]
        + [(a, "any") for a in w1]
        + [(a, "any") for a in w2]
        + [(c1, "whole"), (vec, "whole")],
        [
            ((rows, model), BF, "whole"),
            ((rows, model), F32, "whole"),
            ((4, rows, hidden), BF, "half"),
            ((4, rows, hidden), BF, "half"),
        ],
        [
            pltpu.VMEM((4, model, hidden), BF),
            pltpu.VMEM((4, hidden, model), BF),
            pltpu.VMEM((rows, model), BF),
            pltpu.VMEM((rows, model), F32),
            pltpu.SemaphoreType.DMA((4,)),
            pltpu.SemaphoreType.DMA((4,)),
        ],
        16 * rows * model * hidden,
        8 * rows * hidden,
    )
    return outs[0], (u, outs[1], outs[2], outs[3])


def feed_backward(grad, cot, saved, w1, w2, vec, name):
    u, e, h, slope = saved
    rows, model = u.shape
    hidden = w1[0].shape[1]
    has_grad = grad is not None
    g = ((2, model, hidden), BF, "half")
    g2 = ((2, hidden, model), BF, "half")
    return call(
        functools.partial(ffn_backward_kernel, has_grad),
        name,
        ([(grad, "whole")] if has_grad else [])
        + [(cot, "whole"), (e, "whole"), (u, "whole")]
        + [(a, "any") for a in w1]
        + [(a, "any") for a in w2]
        + [(h, "half"), (slope, "half"), (vec, "whole")],
        [
            ((rows, model), F32, "whole"),
            g,
            g,
            g2,
            g2,
            ((2, 2, hidden), F32, "half"),
            ((3, model), F32, "whole"),
        ],
        [
            pltpu.VMEM((4, model, hidden), BF),
            pltpu.VMEM((4, hidden, model), BF),
            pltpu.VMEM((rows, model), BF),
            pltpu.VMEM((rows, model), BF),
            pltpu.VMEM((rows, model), F32),
            pltpu.SemaphoreType.DMA((4,)),
            pltpu.SemaphoreType.DMA((4,)),
        ],
        32 * rows * model * hidden,
    )


def self_forward(lengths, x, w, bias, vec, name):
    items = lengths.shape[0]
    rows, model = x.shape
    slots = rows // items
    width = w[0].shape[0] // 4
    heads = width // HEAD_DIM
    mid = ((4, rows, width), BF, "half")
    outs = call(
        functools.partial(self_forward_kernel, items),
        name,
        [(lengths, "smem"), (x, "whole")]
        + [(a, "any") for a in w]
        + [(bias, "whole"), (vec, "whole")],
        [
            ((rows, model), F32, "whole"),
            ((rows, model), F32, "whole"),
            mid,
            mid,
            mid,
            ((4, items, heads * slots, slots), BF, "half"),
            mid,
        ],
        [
            pltpu.VMEM((4,) + w[0].shape, BF),
            pltpu.VMEM((rows, model), F32),
            pltpu.VMEM((rows, width), F32),
            pltpu.VMEM((rows, width), F32),
            pltpu.VMEM((rows, width), F32),
            pltpu.VMEM((rows, width), F32),
            pltpu.SemaphoreType.DMA((4,)),
        ],
        32 * rows * model * width,
    )
    return outs[0], (x, outs[1], outs[2], outs[3], outs[4], outs[5], outs[6])


def self_backward(dy, saved, items, w, vec, dtype, name):
    x, e, q, k, v, p, a = saved
    rows, model = x.shape
    width = q.shape[2]
    g = ((2,) + w[0].shape, BF, "half")
    return call(
        functools.partial(self_backward_kernel, items),
        name,
        [(dy, "whole"), (e, "whole"), (x, "whole")]
        + [(m, "any") for m in w]
        + [(q, "half"), (k, "half"), (v, "half"), (p, "half"), (a, "half"), (vec, "whole")],
        [
            ((rows, model), dtype, "whole"),
            g,
            g,
            ((2, 2, 2, width), F32, "half"),
            ((3, model), F32, "whole"),
        ],
        [
            pltpu.VMEM((4,) + w[0].shape, BF),
            pltpu.VMEM((rows, model), BF),
            pltpu.VMEM((rows, model), F32),
        ]
        + [pltpu.VMEM((rows, width), F32)] * 7
        + [pltpu.SemaphoreType.DMA((4,))],
        64 * rows * model * width,
    )


def cross_forward(u, pf, patches, items, w, bias, vec, name):
    rows, model = u.shape
    slots, padded = rows // items, pf.shape[0] // items
    width = bias.shape[2]
    heads = width // HEAD_DIM
    mid = ((4, rows, width), BF, "half")
    key = ((4, pf.shape[0], width), BF, "half")
    outs = call(
        functools.partial(cross_forward_kernel, items, patches),
        name,
        [(u, "whole"), (pf, "whole")]
        + [(a, "any") for a in w]
        + [(bias, "whole"), (vec, "whole")],
        [
            ((rows, model), F32, "whole"),
            ((rows, model), F32, "whole"),
            mid,
            key,
            key,
            ((4, items, heads * slots, padded), BF, "half"),
            mid,
        ],
        [
            pltpu.VMEM((4,) + w[0].shape, BF),
            pltpu.VMEM((rows, model), BF),
            pltpu.VMEM((rows, model), F32),
            pltpu.VMEM((rows, width), F32),
            pltpu.VMEM((rows, width), F32),
            pltpu.SemaphoreType.DMA((4,)),
        ],
        16 * rows * model * width + 16 * pf.size * width,
    )
    return outs[0], (u, outs[1], outs[2], outs[3], outs[4], outs[5], outs[6])


def cross_backward(dy, saved, pf, patches, items, w, vec, name):
    u, e, q, k, v, p, a = saved
    rows, model = u.shape
    width = q.shape[2]
    g = ((2,) + w[0].shape, BF, "half")
    return call(
        functools.partial(cross_backward_kernel, items, patches),
        name,
        [(dy, "whole"), (e, "whole"), (u, "whole"), (pf, "whole")]
        + [(m, "any") for m in w]
        + [(q, "half"), (k, "half"), (v, "half"), (p, "half"), (a, "half"), (vec, "whole")],
        [
            ((rows, model), F32, "whole"),
            ((items, patches, pf.shape[1]), BF, "whole"),
            g,
            g,
            ((2, 2, 2, width), F32, "half"),
            ((3, model), F32, "whole"),
        ],
        [
            pltpu.VMEM((4,) + w[0].shape, BF),
            pltpu.VMEM((rows, model), BF),
            pltpu.VMEM((rows, model), BF),
            pltpu.VMEM((rows, model), F32),
            pltpu.VMEM(pf.shape, F32),
            pltpu.VMEM((rows, width), F32),
            pltpu.VMEM((rows, width), F32),
            pltpu.VMEM((rows, width), F32),
            pltpu.VMEM((2, pf.shape[0], width), BF),
            pltpu.SemaphoreType.DMA((4,)),
        ],
        32 * rows * model * width + 32 * pf.size * width,
    )


def swap(array, axis, size, distance):
    return lax.ppermute(array, axis, [(i, i ^ distance) for i in range(size)])


class Links:
    def __init__(self, mesh):
        self.tensor = mesh.shape["tensor"]
        self.dp = mesh.shape["dp"]
        self.bits = self.dp.bit_length() - 1

    def core(self, array):
        return swap(array, "tensor", self.tensor, 1)

    def far(self, array):
        return swap(array, "tensor", self.tensor, 2)

    def gather(self, own):
        across = self.far(own)
        return own, self.core(own), across, self.core(across)

    def reduce(self, keep, send):
        got = self.core(send)
        other = (keep[1].astype(F32) + got[1].astype(F32)).astype(BF)
        got_far = self.far(other)
        total = keep[0].astype(F32) + got[0].astype(F32) + got_far.astype(F32)
        total = total.astype(BF)
        me = lax.axis_index("dp")
        for b in range(self.bits):
            bit = (me >> b) & 1
            half = total.shape[0] // 2
            mine = lax.dynamic_slice_in_dim(total, bit * half, half, 0)
            gone = lax.dynamic_slice_in_dim(total, (1 - bit) * half, half, 0)
            got = swap(gone, "dp", self.dp, 1 << b)
            total = (mine.astype(F32) + got.astype(F32)).astype(BF)
        for b in reversed(range(self.bits)):
            bit = (me >> b) & 1
            got = swap(total, "dp", self.dp, 1 << b)
            total = jnp.where(
                bit == 0,
                jnp.concatenate([total, got], axis=0),
                jnp.concatenate([got, total], axis=0),
            )
        return total.astype(F32)


def flat(array):
    return array.reshape(-1)


def self_pack(w_in, w_out):
    turned = jnp.swapaxes(w_in, 1, 2)
    return jnp.concatenate([turned.reshape(-1, w_in.shape[1]), w_out], axis=0)


def self_unpack(total, width):
    model = total.shape[1]
    first = jnp.swapaxes(total[: 3 * width].reshape(3, width, model), 1, 2)
    return first, total[3 * width :]


def cross_pack(w_query, w_out, w_keyval):
    model = w_query.shape[0]
    keyval = jnp.swapaxes(w_keyval, 1, 2).reshape(-1, w_keyval.shape[1])
    side = w_keyval.shape[1] - model
    parts = model // side
    count = keyval.shape[0] // parts
    tail = keyval[:, model:].reshape(parts, count, side)
    tail = jnp.swapaxes(tail, 0, 1).reshape(count, model)
    return jnp.concatenate([w_query.T, w_out, keyval[:, :model], tail], axis=0)


def cross_unpack(total, width, patch_width):
    model = total.shape[1]
    side = patch_width - model
    parts = model // side
    tail = total[4 * width :]
    tail = jnp.swapaxes(tail.reshape(-1, parts, side), 0, 1).reshape(2 * width, side)
    keyval = jnp.concatenate([total[2 * width : 4 * width], tail], axis=1)
    keyval = jnp.swapaxes(keyval.reshape(2, width, patch_width), 1, 2)
    return total[:width].T, total[width : 2 * width], keyval


def per_device(
    links,
    text_rows,
    patch_features,
    lengths,
    text_cotangent,
    join_cotangent,
    text_project_in,
    text_project_bias,
    text_project_out,
    text_expand,
    text_expand_bias,
    text_contract,
    text_out_bias,
    text_norm_gain,
    text_norm_shift,
    join_project_in,
    join_project_bias,
    join_project_out,
    cross_project_out,
    cross_key_value,
    join_expand,
    join_expand_bias,
    join_contract,
    join_out_bias,
    join_norm_gain,
    join_norm_shift,
):
    items, slots, model = text_rows.shape
    patches, patch_width = patch_features.shape[1:]
    width = text_project_in.shape[2]
    hidden = text_expand.shape[1]

    biases = jnp.concatenate(
        [
            flat(text_project_bias),
            flat(join_project_bias),
            text_expand_bias,
            join_expand_bias,
        ]
    )[None]
    weights_one = links.gather(self_pack(text_project_in, text_project_out))
    biases = jnp.concatenate(links.gather(biases), axis=0).astype(F32)
    expand_one = links.gather(text_expand)
    contract_one = links.gather(text_contract)
    weights_two = links.gather(self_pack(join_project_in[0:3], join_project_out))
    weights_cross = links.gather(
        cross_pack(join_project_in[3], cross_project_out, cross_key_value)
    )
    expand_two = links.gather(join_expand)
    contract_two = links.gather(join_contract)

    bias_one = biases[:, : 2 * width].reshape(4, 2, width)
    bias_two = biases[:, 2 * width : 4 * width].reshape(4, 2, width)
    bias_cross = biases[:, 4 * width : 6 * width].reshape(4, 2, width)
    hidden_one = biases[:, 6 * width : 6 * width + hidden].reshape(4, 1, hidden)
    hidden_two = biases[:, 6 * width + hidden :].reshape(4, 1, hidden)

    def vec(bias, gain, shift, n):
        return jnp.stack([bias[n], gain[n], shift[n]]).astype(F32)

    text_vecs = [vec(text_out_bias, text_norm_gain, text_norm_shift, n) for n in range(2)]
    join_vecs = [vec(join_out_bias, join_norm_gain, join_norm_shift, n) for n in range(3)]

    padded = -(-patches // 16) * 16
    pf = jnp.pad(patch_features, ((0, 0), (0, padded - patches), (0, 0)))
    pf = pf.reshape(items * padded, patch_width)
    x = text_rows.reshape(items * slots, model)
    text_cot = text_cotangent.reshape(items * slots, model)
    join_cot = join_cotangent.reshape(items * slots, model)

    h1, saved_one = self_forward(lengths, x, weights_one, bias_one, text_vecs[0], "text_self_forward")
    text_out, saved_two = feed_forward(
        h1, expand_one, contract_one, hidden_one, text_vecs[1], "text_feed_forward"
    )
    h2, saved_three = self_forward(
        lengths, text_out, weights_two, bias_two, join_vecs[0], "join_self_forward"
    )
    h3, saved_four = cross_forward(
        h2, pf, patches, items, weights_cross, bias_cross, join_vecs[1], "cross_forward"
    )
    join_out, saved_five = feed_forward(
        h3, expand_two, contract_two, hidden_two, join_vecs[2], "join_feed_forward"
    )

    du, g1k, g1s, g2k, g2s, dc_two, sums_five = feed_backward(
        None, join_cot, saved_five, expand_two, contract_two, join_vecs[2], "join_feed_backward"
    )
    grad_join_contract = links.reduce(g2k, g2s)
    grad_join_expand = links.reduce(g1k, g1s)
    du, grad_patches, gk, gs, db_cross, sums_four = cross_backward(
        du, saved_four, pf, patches, items, weights_cross, join_vecs[1], "cross_backward"
    )
    grad_query, grad_cross_out, grad_keyval = cross_unpack(
        links.reduce(gk, gs), width, patch_width
    )
    du, gk, gs, db_two, sums_three = self_backward(
        du, saved_three, items, weights_two, join_vecs[0], F32, "join_self_backward"
    )
    grad_join_in, grad_join_out = self_unpack(links.reduce(gk, gs), width)
    du, g1k, g1s, g2k, g2s, dc_one, sums_two = feed_backward(
        du, text_cot, saved_two, expand_one, contract_one, text_vecs[1], "text_feed_backward"
    )
    grad_text_contract = links.reduce(g2k, g2s)
    grad_text_expand = links.reduce(g1k, g1s)
    grad_text, gk, gs, db_one, sums_one = self_backward(
        du, saved_one, items, weights_one, text_vecs[0], BF, "text_self_backward"
    )
    grad_text_in, grad_text_out = self_unpack(links.reduce(gk, gs), width)

    blocks = jnp.concatenate(
        [
            db_one.reshape(4, -1),
            db_two.reshape(4, -1),
            db_cross.reshape(4, -1),
            dc_one.reshape(4, -1),
            dc_two.reshape(4, -1),
        ],
        axis=1,
    )
    shared = jnp.stack([sums_one, sums_two, sums_three, sums_four, sums_five])
    units = blocks.shape[1]
    count = shared.size
    got = links.core(jnp.concatenate([blocks[1], blocks[3], flat(shared)]))
    own = blocks[0] + got[:units]
    other = blocks[2] + got[units : 2 * units]
    shared = flat(shared) + got[2 * units :]
    got = links.far(jnp.concatenate([other, shared]))
    small = jnp.concatenate([own, shared]) + got
    for b in range(links.bits):
        small = small + swap(small, "dp", links.dp, 1 << b)
    shared = small[units:].reshape(5, 3, model)
    attend = small[: 6 * width].reshape(6, width)
    text_shared, join_shared = shared[0:2], shared[2:5]

    return (
        text_out.reshape(text_rows.shape),
        join_out.reshape(text_rows.shape),
        grad_text.reshape(text_rows.shape),
        grad_patches,
        grad_text_in,
        attend[0:2],
        grad_text_out,
        grad_text_expand,
        small[6 * width : 6 * width + hidden],
        grad_text_contract,
        text_shared[:, 0],
        text_shared[:, 1],
        text_shared[:, 2],
        jnp.concatenate([grad_join_in, grad_query[None]], axis=0),
        attend[2:6],
        grad_join_out,
        grad_cross_out,
        grad_keyval,
        grad_join_expand,
        small[6 * width + hidden : 6 * width + 2 * hidden],
        grad_join_contract,
        join_shared[:, 0],
        join_shared[:, 1],
        join_shared[:, 2],
    )


def solution(mesh):
    rows = P(("dp", "tensor"), None, None)
    last = P(None, None, "tensor")
    second = P(None, "tensor")
    first = P("tensor", None)
    line = P("tensor")
    full = P()
    in_specs = (
        (rows, rows, P(("dp", "tensor")), rows, rows)
        + (last, second, first, second, line, first, full, full, full)
        + (last, second, first, first, last, second, line, first, full, full, full)
    )
    out_specs = (
        (rows, rows, rows, rows)
        + (last, second, first, second, line, first, full, full, full)
        + (last, second, first, first, last, second, line, first, full, full, full)
    )
    return jax.shard_map(
        functools.partial(per_device, Links(mesh)),
        mesh=mesh,
        in_specs=in_specs,
        out_specs=out_specs,
        check_vma=False,
    )
```

time: 1680 us -> 848 us (0.50)
  waiting for transfers between devices: 1120 us -> 510 us
  matrix products: 232 us -> 0 us
  Pallas kernels: 0 us -> 178 us
  local copies, waits for them, and re-layouts: 171 us -> 32.3 us
  blocking collectives: 85.1 us -> 0 us
  starting transfers between devices: 2.16 us -> 77.1 us
    ppermute x0 -> x85, waiting for transfers between devices: none -> 510 us  [swap(): return lax.ppermute(array, axis, [(i, i ^ distance) for i in range(size)])]
    psum x1 -> x0, waiting for transfers between devices: 505 us -> none  [per_device(): lax.psum((grads_one[0], grads_one[1], grads_one[2], grads_two[0], grads_t...]
    reduce_scatter x11 -> x0, waiting for transfers between devices: 384 us -> none  [the longest x5 212 us: branch_sum(): lax.psum_scatter(jnp.dot(inputs, weight, preferred_element_type=jnp.float...]
    dot_general x51 -> x0, matrix products: 232 us -> none  [the longest x1 25.8 us: cross_forward(): jnp.einsum('ipf,cfe->cipe', patch_all, w_keyval, preferred_element_type=j...]
    all_gather x11 -> x0, waiting for transfers between devices: 231 us -> none  [the longest x5 87.6 us: output_back(): lax.all_gather(grad_pre.astype(jnp.bfloat16), 'tensor', axis=0, tiled=True)]
    pallas_call x0 -> x10, Pallas kernels: none -> 178 us  [call(): pl.pallas_call(kernel, grid=(2,), in_specs=[kinds[kind](a.shape) for a, k...]
    convert_element_type x38 -> x0, local copies, waits for them, and re-layouts: 83 us -> none  [the longest x11 25.9 us: attend_backward(): grad_queries.reshape(queries.shape).astype(jnp.bfloat16)]
    psum x2 -> x0, blocking collectives: 78.7 us -> none  [the longest x1 41.4 us: per_device(): lax.psum((text_bias_grad, text_gain_grad, text_shift_grad, join_out_grad,...]
  transfers between devices with their start and end apart: 23 -> 85, of which waited for: 19 -> 44; matrix products, arithmetic and copies ran while one was open for 13% -> 7% of each run, Pallas kernels for 0% -> 7%
where the time goes in v1:
time: 848 us; the launch traced here: 843 us
  waiting for transfers between devices  510 us (60%)
  Pallas kernels  178 us (21%)
  starting transfers between devices  77.1 us (9%)
  other arithmetic  43.4 us (5%)
  local copies, waits for them, and re-layouts  32.3 us (4%)
    ppermute x85, waiting for transfers between devices, swap(): return lax.ppermute(array, axis, [(i, i ^ distance) for i in range(size)])  510 us
    pallas_call x10, Pallas kernels, call(): pl.pallas_call(kernel, grid=(2,), in_specs=[kinds[kind](a.shape) for a, k...  178 us
    ppermute x85, starting transfers between devices, swap(): return lax.ppermute(array, axis, [(i, i ^ distance) for i in range(size)])  77.1 us
  transfers between devices with their start and end apart: 85, of which 44 were waited for; matrix products, arithmetic and copies ran while one was open for 7% of the time, Pallas kernels for 7%

profile of v1, /device:TPU:0, one launch (start us, length us, event | category | flops | bytes accessed | tf_op | source)
XLA Modules:
  0.0 843.2 jit_solution(4324828276915172522)
XLA Ops:
  2.6 2.6 collective-permute-start.1
  6.1 25.9 %collective-permute-done.4 = bf16[1,2688]{1,0:T(2,128)(2,1)S(1)} collective-permute-done((bf16[1,2688]{1,0:T(2,128)(2,1)S(1)}, bf16[1,2688]{1,0:T(2,128)(2,1)S(1)}, u32[]{:S(2)}, u32[]{:S(2)}) %collective-permute-start.4) | collective-permute-done | bytes 5408 | tf_op jit(solution)/shard_map/ppermute | solution.py:651
  39.0 22.1 %collective-permute-done.7.refs_2_.refs_6_ = bf16[768,768]{1,0:T(8,128)(2,1)} collective-permute-done((bf16[768,768]{1,0:T(8,128)(2,1)}, bf16[768,768]{1,0:T(8,128)(2,1)}, u32[]{:S(2)}, u32[]{:S(2)}) %collective-permute-start.7) | collective-permute-done | bytes 1179680 | tf_op jit(solution)/shard_map/ppermute | solution.py:651
  63.1 23.2 %collective-permute-done.10.refs_6_.refs_10_ = bf16[768,768]{1,0:T(8,128)(2,1)} collective-permute-done((bf16[768,768]{1,0:T(8,128)(2,1)}, bf16[768,768]{1,0:T(8,128)(2,1)}, u32[]{:S(2)}, u32[]{:S(2)}) %collective-permute-start.10) | collective-permute-done | bytes 1179680 | tf_op jit(solution)/shard_map/ppermute | solution.py:651
  89.1 22.5 %collective-permute-done.13.refs_2_ = bf16[768,768]{1,0:T(8,128)(2,1)S(1)} collective-permute-done((bf16[768,768]{1,0:T(8,128)(2,1)}, bf16[768,768]{1,0:T(8,128)(2,1)S(1)}, u32[]{:S(2)}, u32[]{:S(2)}) %collective-permute-start.13) | collective-permute-done | bytes 1179680 | tf_op jit(solution)/shard_map/ppermute | solution.py:651
  111.5 25.4 %collective-permute-done.19.refs_2_.refs_5_ = bf16[768,768]{1,0:T(8,128)(2,1)} collective-permute-done((bf16[768,768]{1,0:T(8,128)(2,1)}, bf16[768,768]{1,0:T(8,128)(2,1)}, u32[]{:S(2)}, u32[]{:S(2)}) %collective-permute-start.19) | collective-permute-done | bytes 1179680 | tf_op jit(solution)/shard_map/ppermute | solution.py:651
  136.9 25.3 %collective-permute-done.22.refs_6_.refs_9_ = bf16[768,768]{1,0:T(8,128)(2,1)} collective-permute-done((bf16[768,768]{1,0:T(8,128)(2,1)}, bf16[768,768]{1,0:T(8,128)(2,1)}, u32[]{:S(2)}, u32[]{:S(2)}) %collective-permute-start.22) | collective-permute-done | bytes 1179680 | tf_op jit(solution)/shard_map/ppermute | solution.py:651
  164.6 26.7 %collective-permute-done.16.refs_2_ = bf16[896,768]{1,0:T(8,128)(2,1)} collective-permute-done((bf16[896,768]{1,0:T(8,128)(2,1)S(1)}, bf16[896,768]{1,0:T(8,128)(2,1)}, u32[]{:S(2)}, u32[]{:S(2)}) %collective-permute-start.16) | collective-permute-done | bytes 1376288 | tf_op jit(solution)/shard_map/ppermute | solution.py:651
  193.3 1.8 pad.4.clone
  200.8 13.5 %text_self_forward.1 = (f32[320,768]{1,0:T(8,128)}, f32[320,768]{1,0:T(8,128)}, bf16[4,320,192]{2,1,0:T(8,128)(2,1)}, bf16[4,320,192]{2,1,0:T(8,128)(2,1)}, bf16...) custom-call(s32[8]{0:T(128)} %lengths.3, bf16[320,768]{1,0:T(8,128)(2,1)} %bitcast.134, ...), custom_call_target="tpu_custom_call" | custom-call | flops 1509949440 | bytes 9464864 | tf_op jit(solution)/shard_map/text_self_forward/pallas_call | solution.py:431
  214.3 10.5 %text_feed_forward.1 = (bf16[320,768]{1,0:T(8,128)(2,1)}, f32[320,768]{1,0:T(8,128)}, bf16[4,320,768]{2,1,0:T(8,128)(2,1)}, bf16[4,320,768]{2,1,0:T(8,128)(2,1)}) custom-call(f32[320,768]{1,0:T(8,128)} %get-tuple-element.83.u.refs_3_, bf16[768,768]{1,0:T(8,128)(2,1)} %refs_4_.5, bf16[768,768]{1,0:T(8,128)(2,1)} %collective-permute-done.6.refs_1_.refs_5_, ...), custom_call_target="tpu_custom_call" | custom-call | flops 3019898880 | bytes 15848448 | tf_op jit(solution)/shard_map/text_feed_forward/pallas_call | solution.py:431
  224.8 13.3 %join_self_forward.1 = (f32[320,768]{1,0:T(8,128)}, f32[320,768]{1,0:T(8,128)}, bf16[4,320,192]{2,1,0:T(8,128)(2,1)}, bf16[4,320,192]{2,1,0:T(8,128)(2,1)}, bf16...) custom-call(s32[8]{0:T(128)} %lengths.3, ...), custom_call_target="tpu_custom_call" | custom-call | flops 1509949440 | bytes 9464864 | tf_op jit(solution)/shard_map/join_self_forward/pallas_call | solution.py:431
  238.1 21.2 %cross_forward.1 = (f32[320,768]{1,0:T(8,128)}, f32[320,768]{1,0:T(8,128)}, bf16[4,320,192]{2,1,0:T(8,128)(2,1)}, bf16[4,1280,192]{2,1,0:T(8,128)(2,1)}, bf16[4,...) custom-call(f32[320,768]{1,0:T(8,128)} %get-tuple-element.85.u, ...), custom_call_target="tpu_custom_call" | custom-call | flops 4781506560 | bytes 17234944 | tf_op jit(solution)/shard_map/cross_forward/pallas_call | solution.py:431
  260.8 10.5 %join_feed_forward.1 = (bf16[320,768]{1,0:T(8,128)(2,1)}, f32[320,768]{1,0:T(8,128)}, bf16[4,320,768]{2,1,0:T(8,128)(2,1)}, bf16[4,320,768]{2,1,0:T(8,128)(2,1)}) custom-call(f32[320,768]{1,0:T(8,128)} %get-tuple-element.86.u.refs_2_, bf16[768,768]{1,0:T(8,128)(2,1)} %refs_3_.1, bf16[768,768]{1,0:T(8,128)(2,1)} %copy-done.40, ...), custom_call_target="tpu_custom_call" | custom-call | flops 3019898880 | bytes 15848448 | tf_op jit(solution)/shard_map/join_feed_forward/pallas_call | solution.py:431
  271.3 17.0 %join_feed_backward.1 = (f32[320,768]{1,0:T(8,128)}, bf16[2,768,768]{2,1,0:T(8,128)(2,1)}, bf16[2,768,768]{2,1,0:T(8,128)(2,1)}, bf16[2,768,768]{2,1,0:T(8,128)(...) custom-call(bf16[320,768]{1,0:T(8,128)(2,1)} %bitcast.132, ...), custom_call_target="tpu_custom_call" | custom-call | flops 6039797760 | bytes 26277888 | tf_op jit(solution)/shard_map/join_feed_backward/pallas_call | solution.py:431
  288.3 32.7 %cross_backward.1 = (f32[320,768]{1,0:T(8,128)}, bf16[8,145,1024]{2,1,0:T(8,128)(2,1)}, bf16[2,896,768]{2,1,0:T(8,128)(2,1)}, bf16[2,896,768]{2,1,0:T(8,128)(2,1...) custom-call(f32[320,768]{1,0:T(8,128)} %get-tuple-element.91.dy, f32[320,768]{1,0:T(8,128)} %get-tuple-element.92.e_in, ...), custom_call_target="tpu_custom_call" | custom-call | flops 9563013120 | bytes 26107904 | tf_op jit(solution)/shard_map/cross_backward/pallas_call | solution.py:431
  321.1 21.4 %join_self_backward.1 = (f32[320,768]{1,0:T(8,128)}, bf16[2,768,768]{2,1,0:T(8,128)(2,1)}, bf16[2,768,768]{2,1,0:T(8,128)(2,1)}, f32[2,2,2,192]{3,2,1,0:T(2,128)}, f32[3,768]{1,0:T(4,128)}) custom-call(f32[320,768]{1,0:T(8,128)} %get-tuple-element.98.dy, f32[320,768]{1,0:T(8,128)} %get-tuple-element.99.e_in, bf16[320,768]{1,0:T(8,128)(2,1)} %get-tuple-element.84.x, ...), custom_call_target="tpu_custom_call" | custom-call | flops 3019898880 | bytes 15175680 | tf_op jit(solution)/shard_map/join_self_backward/pallas_call | solution.py:431
  342.4 17.3 %text_feed_backward.1 = (f32[320,768]{1,0:T(8,128)}, bf16[2,768,768]{2,1,0:T(8,128)(2,1)}, bf16[2,768,768]{2,1,0:T(8,128)(2,1)}, bf16[2,768,768]{2,1,0:T(8,128)(...) custom-call(f32[320,768]{1,0:T(8,128)} %get-tuple-element.105.refs_0_, ...), custom_call_target="tpu_custom_call" | custom-call | flops 6039797760 | bytes 27260928 | tf_op jit(solution)/shard_map/text_feed_backward/pallas_call | solution.py:431
  359.9 21.0 %text_self_backward.1 = (bf16[320,768]{1,0:T(8,128)(2,1)}, bf16[2,768,768]{2,1,0:T(8,128)(2,1)}, bf16[2,768,768]{2,1,0:T(8,128)(2,1)}, f32[2,2,2,192]{3,2,1,0:T(2,128)}, f32[3,768]{1,0:T(4,128)}) custom-call(f32[320,768]{1,0:T(8,128)} %get-tuple-element.109.dy, f32[320,768]{1,0:T(8,128)} %get-tuple-element.110.e_in, bf16[320,768]{1,0:T(8,128)(2,1)} %bitcast.135, ...), custom_call_target="tpu_custom_call" | custom-call | flops 3019898880 | bytes 14684160 | tf_op jit(solution)/shard_map/text_self_backward/pallas_call | solution.py:431
  385.7 1.8 collective-permute-start.33
  388.0 1.9 collective-permute-done.33
  391.7 2.5 collective-permute-done.34
  394.2 1.9 collective-permute-start.35
  396.0 2.4 collective-permute-done.35
  398.4 3.5 collective-permute-start.36
  401.9 2.2 collective-permute-done.36
  406.0 4.4 copy.66
  416.1 2.1 fusion.9
  433.6 15.4 %collective-permute-done.25 = bf16[768,768]{1,0:T(8,128)(2,1)S(1)} collective-permute-done((bf16[768,768]{1,0:T(8,128)(2,1)S(1)}, bf16[768,768]{1,0:T(8,128)(2,1)S(1)}, u32[]{:S(2)}, u32[]{:S(2)}) %collective-permute-start.25) | collective-permute-done | bytes 1179680 | tf_op jit(solution)/shard_map/ppermute | solution.py:651
  451.0 23.3 %collective-permute-done.38 = bf16[768,768]{1,0:T(8,128)(2,1)S(1)} collective-permute-done((bf16[768,768]{1,0:T(8,128)(2,1)S(1)}, bf16[768,768]{1,0:T(8,128)(2,1)S(1)}, u32[]{:S(2)}, u32[]{:S(2)}) %collective-permute-start.38) | collective-permute-done | bytes 1179680 | tf_op jit(solution)/shard_map/ppermute | solution.py:651
  477.8 21.9 %collective-permute-done.46 = bf16[768,768]{1,0:T(8,128)(2,1)S(1)} collective-permute-done((bf16[768,768]{1,0:T(8,128)(2,1)S(1)}, bf16[768,768]{1,0:T(8,128)(2,1)S(1)}, u32[]{:S(2)}, u32[]{:S(2)}) %collective-permute-start.46) | collective-permute-done | bytes 1179680 | tf_op jit(solution)/shard_map/ppermute | solution.py:651
  502.9 22.0 %collective-permute-done.54 = bf16[768,768]{1,0:T(8,128)(2,1)S(1)} collective-permute-done((bf16[768,768]{1,0:T(8,128)(2,1)S(1)}, bf16[768,768]{1,0:T(8,128)(2,1)S(1)}, u32[]{:S(2)}, u32[]{:S(2)}) %collective-permute-start.54) | collective-permute-done | bytes 1179680 | tf_op jit(solution)/shard_map/ppermute | solution.py:651
  528.2 21.9 %collective-permute-done.70 = bf16[768,768]{1,0:T(8,128)(2,1)S(1)} collective-permute-done((bf16[768,768]{1,0:T(8,128)(2,1)S(1)}, bf16[768,768]{1,0:T(8,128)(2,1)S(1)}, u32[]{:S(2)}, u32[]{:S(2)}) %collective-permute-start.70) | collective-permute-done | bytes 1179680 | tf_op jit(solution)/shard_map/ppermute | solution.py:651
  553.4 22.0 %collective-permute-done.78 = bf16[768,768]{1,0:T(8,128)(2,1)S(1)} collective-permute-done((bf16[768,768]{1,0:T(8,128)(2,1)S(1)}, bf16[768,768]{1,0:T(8,128)(2,1)S(1)}, u32[]{:S(2)}, u32[]{:S(2)}) %collective-permute-start.78) | collective-permute-done | bytes 1179680 | tf_op jit(solution)/shard_map/ppermute | solution.py:651
  583.0 21.6 %collective-permute-done.62 = bf16[896,768]{1,0:T(8,128)(2,1)S(1)} collective-permute-done((bf16[896,768]{1,0:T(8,128)(2,1)S(1)}, bf16[896,768]{1,0:T(8,128)(2,1)S(1)}, u32[]{:S(2)}, u32[]{:S(2)}) %collective-permute-start.62) | collective-permute-done | bytes 1376288 | tf_op jit(solution)/shard_map/ppermute | solution.py:651
  609.2 7.8 collective-permute-done.79
  621.0 3.3 collective-permute-start.28
  624.6 5.7 collective-permute-done.56
  630.3 2.0 collective-permute-start.41
  632.4 7.3 collective-permute-done.72
  639.7 2.0 collective-permute-start.49
  641.9 3.7 collective-permute-done.80
  650.3 13.0 %collective-permute-done.49 = bf16[96,768]{1,0:T(8,128)(2,1)S(1)} collective-permute-done((bf16[96,768]{1,0:T(8,128)(2,1)S(1)}, bf16[96,768]{1,0:T(8,128)(2,1)S(1)}, u32[]{:S(2)}, u32[]{:S(2)}) %collective-permute-start.49) | collective-permute-done | bytes 147488 | tf_op jit(solution)/shard_map/ppermute | solution.py:651
  663.3 9.4 %collective-permute-done.57 = bf16[96,768]{1,0:T(8,128)(2,1)S(1)} collective-permute-done((bf16[96,768]{1,0:T(8,128)(2,1)S(1)}, bf16[96,768]{1,0:T(8,128)(2,1)S(1)}, u32[]{:S(2)}, u32[]{:S(2)}) %collective-permute-start.57) | collective-permute-done | bytes 147488 | tf_op jit(solution)/shard_map/ppermute | solution.py:651
  672.7 9.4 %collective-permute-done.73 = bf16[96,768]{1,0:T(8,128)(2,1)S(1)} collective-permute-done((bf16[96,768]{1,0:T(8,128)(2,1)S(1)}, bf16[96,768]{1,0:T(8,128)(2,1)S(1)}, u32[]{:S(2)}, u32[]{:S(2)}) %collective-permute-start.73) | collective-permute-done | bytes 147488 | tf_op jit(solution)/shard_map/ppermute | solution.py:651
  682.2 9.4 %collective-permute-done.81 = bf16[96,768]{1,0:T(8,128)(2,1)S(1)} collective-permute-done((bf16[96,768]{1,0:T(8,128)(2,1)S(1)}, bf16[96,768]{1,0:T(8,128)(2,1)S(1)}, u32[]{:S(2)}, u32[]{:S(2)}) %collective-permute-start.81) | collective-permute-done | bytes 147488 | tf_op jit(solution)/shard_map/ppermute | solution.py:651
  691.7 3.1 collective-permute-done.29
  694.9 3.1 collective-permute-done.42
  698.0 3.1 collective-permute-done.50
  701.2 2.1 collective-permute-start.43
  704.4 3.1 collective-permute-done.74
  707.6 2.2 collective-permute-done.82
  709.9 19.9 %collective-permute-done.64 = bf16[224,768]{1,0:T(8,128)(2,1)S(1)} collective-permute-done((bf16[224,768]{1,0:T(8,128)(2,1)S(1)}, bf16[224,768]{1,0:T(8,128)(2,1)S(1)}, u32[]{:S(2)}, u32[]{:S(2)}) %collective-permute-start.64) | collective-permute-done | bytes 344096 | tf_op jit(solution)/shard_map/ppermute | solution.py:651
  732.5 12.4 %collective-permute-done.65 = bf16[112,768]{1,0:T(8,128)(2,1)S(1)} collective-permute-done((bf16[112,768]{1,0:T(8,128)(2,1)S(1)}, bf16[112,768]{1,0:T(8,128)(2,1)S(1)}, u32[]{:S(2)}, u32[]{:S(2)}) %collective-permute-start.65) | collective-permute-done | bytes 172064 | tf_op jit(solution)/shard_map/ppermute | solution.py:651
  746.5 3.4 collective-permute-start.66
  750.9 4.4 collective-permute-done.66
  756.4 6.1 collective-permute-done.83
  765.0 4.8 collective-permute-done.67
  771.5 15.0 %collective-permute-done.60 = bf16[384,768]{1,0:T(8,128)(2,1)S(1)} collective-permute-done((bf16[384,768]{1,0:T(8,128)(2,1)S(1)}, bf16[384,768]{1,0:T(8,128)(2,1)S(1)}, u32[]{:S(2)}, u32[]{:S(2)}) %collective-permute-start.60) | collective-permute-done | bytes 589856 | tf_op jit(solution)/shard_map/ppermute | solution.py:651
  794.2 4.9 collective-permute-done.52
  800.7 11.0 %collective-permute-done.76 = bf16[384,768]{1,0:T(8,128)(2,1)S(1)} collective-permute-done((bf16[384,768]{1,0:T(8,128)(2,1)S(1)}, bf16[384,768]{1,0:T(8,128)(2,1)S(1)}, u32[]{:S(2)}, u32[]{:S(2)}) %collective-permute-start.76) | collective-permute-done | bytes 589856 | tf_op jit(solution)/shard_map/ppermute | solution.py:651
  813.4 11.0 %collective-permute-done.84 = bf16[384,768]{1,0:T(8,128)(2,1)S(1)} collective-permute-done((bf16[384,768]{1,0:T(8,128)(2,1)S(1)}, bf16[384,768]{1,0:T(8,128)(2,1)S(1)}, u32[]{:S(2)}, u32[]{:S(2)}) %collective-permute-start.84) | collective-permute-done | bytes 589856 | tf_op jit(solution)/shard_map/ppermute | solution.py:651
  826.0 9.0 %collective-permute-done.68 = bf16[448,768]{1,0:T(8,128)(2,1)S(1)} collective-permute-done((bf16[448,768]{1,0:T(8,128)(2,1)S(1)}, bf16[448,768]{1,0:T(8,128)(2,1)S(1)}, u32[]{:S(2)}, u32[]{:S(2)}) %collective-permute-start.68) | collective-permute-done | bytes 688160 | tf_op jit(solution)/shard_map/ppermute | solution.py:651
  838.5 3.2 pad_maximum_fusion
  (365 shorter events, 121.6 us)
Async XLA Ops:
  2.1 31.9 %collective-permute-start = (bf16[768,768]{1,0:T(8,128)(2,1)S(1)}, bf16[768,768]{1,0:T(8,128)(2,1)}, u32[]{:S(2)}, u32[]{:S(2)}) collective-permute-start(bf16[768,768]{1,0:T(8,128)(2,1)S(1)} %pad_maximum_fusion.2.refs_0_), channel_id=1, source_target_pairs={{0,1},{1,0},{2,3},{3,2},{4,5},{5,4},{6,7},{7,6},{8,9},{9,8},{10,11... | collective-permute-start | bytes 3538952 | tf_op jit(solution)/shard_map/ppermute | solution.py:651
  2.6 33.6 %collective-permute-start.1 = (bf16[768,768]{1,0:T(8,128)(2,1)S(1)}, bf16[768,768]{1,0:T(8,128)(2,1)}, u32[]{:S(2)}, u32[]{:S(2)}) collective-permute-start(bf16[768,768]{1,0:T(8,128)(2,1)S(1)} %pad_maximum_fusion.2.refs_0_), channel_id=1, source_target_pairs={{0,2},{1,3},{2,0},{3,1},{4,6},{5,7},{6,4},{7,5},{8,10},{9,11},{10,... | collective-permute-start | bytes 3538952 | tf_op jit(solution)/shard_map/ppermute | solution.py:651
  5.2 33.7 %collective-permute-start.6 = (bf16[768,768]{1,0:T(8,128)(2,1)}, bf16[768,768]{1,0:T(8,128)(2,1)}, u32[]{:S(2)}, u32[]{:S(2)}) collective-permute-start(bf16[768,768]{1,0:T(8,128)(2,1)} %refs_4_.5), channel_id=1, source_target_pairs={{0,1},{1,0},{2,3},{3,2},{4,5},{5,4},{6,7},{7,6},{8,9},{9,8},{10,11... | collective-permute-start | bytes 3538952 | tf_op jit(solution)/shard_map/ppermute | solution.py:651
  5.6 26.4 %collective-permute-start.4 = (bf16[1,2688]{1,0:T(2,128)(2,1)S(1)}, bf16[1,2688]{1,0:T(2,128)(2,1)S(1)}, u32[]{:S(2)}, u32[]{:S(2)}) collective-permute-start(bf16[1,2688]{1,0:T(2,128)(2,1)S(1)} %broadcast_in_dim.6), channel_id=1, source_target_pairs={{0,2},{1,3},{2,0},{3,1},{4,6},{5,7},{6,4},{7,5},{8,10},{9,11},{10,... | collective-permute-start | bytes 16136 | tf_op jit(solution)/shard_map/ppermute | solution.py:651
  5.9 26.1 %collective-permute-start.3 = (bf16[1,2688]{1,0:T(2,128)(2,1)S(1)}, bf16[1,2688]{1,0:T(2,128)(2,1)S(1)}, u32[]{:S(2)}, u32[]{:S(2)}) collective-permute-start(bf16[1,2688]{1,0:T(2,128)(2,1)S(1)} %broadcast_in_dim.6), channel_id=1, source_target_pairs={{0,1},{1,0},{2,3},{3,2},{4,5},{5,4},{6,7},{7,6},{8,9},{9,8},{10,11... | collective-permute-start | bytes 16136 | tf_op jit(solution)/shard_map/ppermute | solution.py:651
  32.0 29.1 %collective-permute-start.7 = (bf16[768,768]{1,0:T(8,128)(2,1)}, bf16[768,768]{1,0:T(8,128)(2,1)}, u32[]{:S(2)}, u32[]{:S(2)}) collective-permute-start(bf16[768,768]{1,0:T(8,128)(2,1)} %refs_4_.5), channel_id=1, source_target_pairs={{0,2},{1,3},{2,0},{3,1},{4,6},{5,7},{6,4},{7,5},{8,10},{9,11},{10,... | collective-permute-start | bytes 3538952 | tf_op jit(solution)/shard_map/ppermute | solution.py:651
  33.8 29.1 %collective-permute-start.9 = (bf16[768,768]{1,0:T(8,128)(2,1)}, bf16[768,768]{1,0:T(8,128)(2,1)}, u32[]{:S(2)}, u32[]{:S(2)}) collective-permute-start(bf16[768,768]{1,0:T(8,128)(2,1)} %refs_8_.1), channel_id=1, source_target_pairs={{0,1},{1,0},{2,3},{3,2},{4,5},{5,4},{6,7},{7,6},{8,9},{9,8},{10,11... | collective-permute-start | bytes 3538952 | tf_op jit(solution)/shard_map/ppermute | solution.py:651
  34.0 52.4 %collective-permute-start.10 = (bf16[768,768]{1,0:T(8,128)(2,1)}, bf16[768,768]{1,0:T(8,128)(2,1)}, u32[]{:S(2)}, u32[]{:S(2)}) collective-permute-start(bf16[768,768]{1,0:T(8,128)(2,1)} %refs_8_.1), channel_id=1, source_target_pairs={{0,2},{1,3},{2,0},{3,1},{4,6},{5,7},{6,4},{7,5},{8,10},{9,11},{10,... | collective-permute-start | bytes 3538952 | tf_op jit(solution)/shard_map/ppermute | solution.py:651
  36.2 51.9 %collective-permute-start.12 = (bf16[768,768]{1,0:T(8,128)(2,1)}, bf16[768,768]{1,0:T(8,128)(2,1)}, u32[]{:S(2)}, u32[]{:S(2)}) collective-permute-start(bf16[768,768]{1,0:T(8,128)(2,1)} %pad_maximum_fusion.3.refs_0_), channel_id=1, source_target_pairs={{0,1},{1,0},{2,3},{3,2},{4,5},{5,4},{6,7},{7,6},{8,9},{9,8},{10,11... | collective-permute-start | bytes 3538952 | tf_op jit(solution)/shard_map/ppermute | solution.py:651
  38.9 123.3 %collective-permute-start.15 = (bf16[896,768]{1,0:T(8,128)(2,1)S(1)}, bf16[896,768]{1,0:T(8,128)(2,1)S(1)}, u32[]{:S(2)}, u32[]{:S(2)}) collective-permute-start(bf16[896,768]{1,0:T(8,128)(2,1)S(1)} %pad_maximum_fusion.1.refs_0_), channel_id=1, source_target_pairs={{0,1},{1,0},{2,3},{3,2},{4,5},{5,4},{6,7},{7,6},{8,9},{9,8},{10,11... | collective-permute-start | bytes 4128776 | tf_op jit(solution)/shard_map/ppermute | solution.py:651
  61.1 50.5 %collective-permute-start.13 = (bf16[768,768]{1,0:T(8,128)(2,1)}, bf16[768,768]{1,0:T(8,128)(2,1)S(1)}, u32[]{:S(2)}, u32[]{:S(2)}) collective-permute-start(bf16[768,768]{1,0:T(8,128)(2,1)} %pad_maximum_fusion.3.refs_0_), channel_id=1, source_target_pairs={{0,2},{1,3},{2,0},{3,1},{4,6},{5,7},{6,4},{7,5},{8,10},{9,11},{10,... | collective-permute-start | bytes 3538952 | tf_op jit(solution)/shard_map/ppermute | solution.py:651
  62.8 74.1 %collective-permute-start.19 = (bf16[768,768]{1,0:T(8,128)(2,1)}, bf16[768,768]{1,0:T(8,128)(2,1)}, u32[]{:S(2)}, u32[]{:S(2)}) collective-permute-start(bf16[768,768]{1,0:T(8,128)(2,1)} %refs_3_.1), channel_id=1, source_target_pairs={{0,2},{1,3},{2,0},{3,1},{4,6},{5,7},{6,4},{7,5},{8,10},{9,11},{10,... | collective-permute-start | bytes 3538952 | tf_op jit(solution)/shard_map/ppermute | solution.py:651
  86.4 75.8 %collective-permute-start.22 = (bf16[768,768]{1,0:T(8,128)(2,1)}, bf16[768,768]{1,0:T(8,128)(2,1)}, u32[]{:S(2)}, u32[]{:S(2)}) collective-permute-start(bf16[768,768]{1,0:T(8,128)(2,1)} %refs_7_.1), channel_id=1, source_target_pairs={{0,2},{1,3},{2,0},{3,1},{4,6},{5,7},{6,4},{7,5},{8,10},{9,11},{10,... | collective-permute-start | bytes 3538952 | tf_op jit(solution)/shard_map/ppermute | solution.py:651
  88.1 103.2 %collective-permute-start.16 = (bf16[896,768]{1,0:T(8,128)(2,1)S(1)}, bf16[896,768]{1,0:T(8,128)(2,1)}, u32[]{:S(2)}, u32[]{:S(2)}) collective-permute-start(bf16[896,768]{1,0:T(8,128)(2,1)S(1)} %pad_maximum_fusion.1.refs_0_), channel_id=1, source_target_pairs={{0,2},{1,3},{2,0},{3,1},{4,6},{5,7},{6,4},{7,5},{8,10},{9,11},{10,... | collective-permute-start | bytes 4128776 | tf_op jit(solution)/shard_map/ppermute | solution.py:651
  111.5 83.6 %collective-permute-start.2 = (bf16[768,768]{1,0:T(8,128)(2,1)}, bf16[768,768]{1,0:T(8,128)(2,1)S(1)}, u32[]{:S(2)}, u32[]{:S(2)}) collective-permute-start(bf16[768,768]{1,0:T(8,128)(2,1)} %collective-permute-done.1.refs_2_), channel_id=1, source_target_pairs={{0,1},{1,0},{2,3},{3,2},{4,5},{5,4},{6,7},{7,6},{8,9},{9,8},{10,11... | collective-permute-start | bytes 3538952 | tf_op jit(solution)/shard_map/ppermute | solution.py:651
  136.9 58.8 %collective-permute-start.8 = (bf16[768,768]{1,0:T(8,128)(2,1)}, bf16[768,768]{1,0:T(8,128)(2,1)S(1)}, u32[]{:S(2)}, u32[]{:S(2)}) collective-permute-start(bf16[768,768]{1,0:T(8,128)(2,1)} %collective-permute-done.7.refs_2_.refs_6_), channel_id=1, source_target_pairs={{0,1},{1,0},{2,3},{3,2},{4,5},{5,4},{6,7},{7,6},{8,9},{9,8},{10,11... | collective-permute-start | bytes 3538952 | tf_op jit(solution)/shard_map/ppermute | solution.py:651
  162.2 33.7 %collective-permute-start.11 = (bf16[768,768]{1,0:T(8,128)(2,1)}, bf16[768,768]{1,0:T(8,128)(2,1)S(1)}, u32[]{:S(2)}, u32[]{:S(2)}) collective-permute-start(bf16[768,768]{1,0:T(8,128)(2,1)} %collective-permute-done.10.refs_6_.refs_10_), channel_id=1, source_target_pairs={{0,1},{1,0},{2,3},{3,2},{4,5},{5,4},{6,7},{7,6},{8,9},{9,8},{10,11... | collective-permute-start | bytes 3538952 | tf_op jit(solution)/shard_map/ppermute | solution.py:651
  162.2 34.1 %collective-permute-start.14 = (bf16[768,768]{1,0:T(8,128)(2,1)S(1)}, bf16[768,768]{1,0:T(8,128)(2,1)S(1)}, u32[]{:S(2)}, u32[]{:S(2)}) collective-permute-start(bf16[768,768]{1,0:T(8,128)(2,1)S(1)} %collective-permute-done.13.refs_2_), channel_id=1, source_target_pairs={{0,1},{1,0},{2,3},{3,2},{4,5},{5,4},{6,7},{7,6},{8,9},{9,8},{10,11... | collective-permute-start | bytes 3538952 | tf_op jit(solution)/shard_map/ppermute | solution.py:651
  191.3 46.8 %collective-permute-start.17 = (bf16[896,768]{1,0:T(8,128)(2,1)}, bf16[896,768]{1,0:T(8,128)(2,1)}, u32[]{:S(2)}, u32[]{:S(2)}) collective-permute-start(bf16[896,768]{1,0:T(8,128)(2,1)} %collective-permute-done.16.refs_2_), channel_id=1, source_target_pairs={{0,1},{1,0},{2,3},{3,2},{4,5},{5,4},{6,7},{7,6},{8,9},{9,8},{10,11... | collective-permute-start | bytes 4128776 | tf_op jit(solution)/shard_map/ppermute | solution.py:651
  195.2 64.2 %collective-permute-start.18 = (bf16[768,768]{1,0:T(8,128)(2,1)}, bf16[768,768]{1,0:T(8,128)(2,1)S(1)}, u32[]{:S(2)}, u32[]{:S(2)}) collective-permute-start(bf16[768,768]{1,0:T(8,128)(2,1)} %refs_3_.1), channel_id=1, source_target_pairs={{0,1},{1,0},{2,3},{3,2},{4,5},{5,4},{6,7},{7,6},{8,9},{9,8},{10,11... | collective-permute-start | bytes 3538952 | tf_op jit(solution)/shard_map/ppermute | solution.py:651
  195.8 63.6 %collective-permute-start.21 = (bf16[768,768]{1,0:T(8,128)(2,1)}, bf16[768,768]{1,0:T(8,128)(2,1)S(1)}, u32[]{:S(2)}, u32[]{:S(2)}) collective-permute-start(bf16[768,768]{1,0:T(8,128)(2,1)} %refs_7_.1), channel_id=1, source_target_pairs={{0,1},{1,0},{2,3},{3,2},{4,5},{5,4},{6,7},{7,6},{8,9},{9,8},{10,11... | collective-permute-start | bytes 3538952 | tf_op jit(solution)/shard_map/ppermute | solution.py:651
  195.9 63.5 %collective-permute-start.20 = (bf16[768,768]{1,0:T(8,128)(2,1)}, bf16[768,768]{1,0:T(8,128)(2,1)}, u32[]{:S(2)}, u32[]{:S(2)}) collective-permute-start(bf16[768,768]{1,0:T(8,128)(2,1)} %collective-permute-done.19.refs_2_.refs_5_), channel_id=1, source_target_pairs={{0,1},{1,0},{2,3},{3,2},{4,5},{5,4},{6,7},{7,6},{8,9},{9,8},{10,11... | collective-permute-start | bytes 3538952 | tf_op jit(solution)/shard_map/ppermute | solution.py:651
  196.3 63.1 %collective-permute-start.23 = (bf16[768,768]{1,0:T(8,128)(2,1)}, bf16[768,768]{1,0:T(8,128)(2,1)}, u32[]{:S(2)}, u32[]{:S(2)}) collective-permute-start(bf16[768,768]{1,0:T(8,128)(2,1)} %collective-permute-done.22.refs_6_.refs_9_), channel_id=1, source_target_pairs={{0,1},{1,0},{2,3},{3,2},{4,5},{5,4},{6,7},{7,6},{8,9},{9,8},{10,11... | collective-permute-start | bytes 3538952 | tf_op jit(solution)/shard_map/ppermute | solution.py:651
  380.8 23.2 %collective-permute-start.24 = (bf16[2,768,768]{2,1,0:T(8,128)(2,1)}, bf16[2,768,768]{2,1,0:T(8,128)(2,1)S(1)}, u32[]{:S(2)}, u32[]{:S(2)}) collective-permute-start(bf16[2,768,768]{2,1,0:T(8,128)(2,1)} %get-tuple-element.119), channel_id=1, source_target_pairs={{0,1},{1,0},{2,3},{3,2},{4,5},{5,4},{6,7},{7,6},{8,9},{9,8},{10,11... | collective-permute-start | bytes 7077896 | tf_op jit(solution)/shard_map/ppermute | solution.py:651
  387.5 32.7 %collective-permute-start.45 = (bf16[2,768,768]{2,1,0:T(8,128)(2,1)}, bf16[2,768,768]{2,1,0:T(8,128)(2,1)}, u32[]{:S(2)}, u32[]{:S(2)}) collective-permute-start(bf16[2,768,768]{2,1,0:T(8,128)(2,1)} %get-tuple-element.133), channel_id=1, source_target_pairs={{0,1},{1,0},{2,3},{3,2},{4,5},{5,4},{6,7},{7,6},{8,9},{9,8},{10,11... | collective-permute-start | bytes 7077896 | tf_op jit(solution)/shard_map/ppermute | solution.py:651
  387.5 36.1 %collective-permute-start.53 = (bf16[2,768,768]{2,1,0:T(8,128)(2,1)}, bf16[2,768,768]{2,1,0:T(8,128)(2,1)}, u32[]{:S(2)}, u32[]{:S(2)}) collective-permute-start(bf16[2,768,768]{2,1,0:T(8,128)(2,1)} %get-tuple-element.135), channel_id=1, source_target_pairs={{0,1},{1,0},{2,3},{3,2},{4,5},{5,4},{6,7},{7,6},{8,9},{9,8},{10,11... | collective-permute-start | bytes 7077896 | tf_op jit(solution)/shard_map/ppermute | solution.py:651
  405.5 26.1 %collective-permute-start.61 = (bf16[2,896,768]{2,1,0:T(8,128)(2,1)}, bf16[2,896,768]{2,1,0:T(8,128)(2,1)S(1)}, u32[]{:S(2)}, u32[]{:S(2)}) collective-permute-start(bf16[2,896,768]{2,1,0:T(8,128)(2,1)} %get-tuple-element.137), channel_id=1, source_target_pairs={{0,1},{1,0},{2,3},{3,2},{4,5},{5,4},{6,7},{7,6},{8,9},{9,8},{10,11... | collective-permute-start | bytes 8257544 | tf_op jit(solution)/shard_map/ppermute | solution.py:651
  406.0 23.3 %collective-permute-start.77 = (bf16[2,768,768]{2,1,0:T(8,128)(2,1)}, bf16[2,768,768]{2,1,0:T(8,128)(2,1)}, u32[]{:S(2)}, u32[]{:S(2)}) collective-permute-start(bf16[2,768,768]{2,1,0:T(8,128)(2,1)} %get-tuple-element.141), channel_id=1, source_target_pairs={{0,1},{1,0},{2,3},{3,2},{4,5},{5,4},{6,7},{7,6},{8,9},{9,8},{10,11... | collective-permute-start | bytes 7077896 | tf_op jit(solution)/shard_map/ppermute | solution.py:651
  420.2 28.8 %collective-permute-start.25 = (bf16[768,768]{1,0:T(8,128)(2,1)S(1)}, bf16[768,768]{1,0:T(8,128)(2,1)S(1)}, u32[]{:S(2)}, u32[]{:S(2)}) collective-permute-start(bf16[768,768]{1,0:T(8,128)(2,1)S(1)} %fusion.9), channel_id=1, source_target_pairs={{0,2},{1,3},{2,0},{3,1},{4,6},{5,7},{6,4},{7,5},{8,10},{9,11},{10,... | collective-permute-start | bytes 3538952 | tf_op jit(solution)/shard_map/ppermute | solution.py:651
  423.6 50.8 %collective-permute-start.38 = (bf16[768,768]{1,0:T(8,128)(2,1)S(1)}, bf16[768,768]{1,0:T(8,128)(2,1)S(1)}, u32[]{:S(2)}, u32[]{:S(2)}) collective-permute-start(bf16[768,768]{1,0:T(8,128)(2,1)S(1)} %fusion.10), channel_id=1, source_target_pairs={{0,2},{1,3},{2,0},{3,1},{4,6},{5,7},{6,4},{7,5},{8,10},{9,11},{10,... | collective-permute-start | bytes 3538952 | tf_op jit(solution)/shard_map/ppermute | solution.py:651
  425.9 73.7 %collective-permute-start.46 = (bf16[768,768]{1,0:T(8,128)(2,1)S(1)}, bf16[768,768]{1,0:T(8,128)(2,1)S(1)}, u32[]{:S(2)}, u32[]{:S(2)}) collective-permute-start(bf16[768,768]{1,0:T(8,128)(2,1)S(1)} %fusion.11), channel_id=1, source_target_pairs={{0,2},{1,3},{2,0},{3,1},{4,6},{5,7},{6,4},{7,5},{8,10},{9,11},{10,... | collective-permute-start | bytes 3538952 | tf_op jit(solution)/shard_map/ppermute | solution.py:651
  429.3 95.6 %collective-permute-start.54 = (bf16[768,768]{1,0:T(8,128)(2,1)S(1)}, bf16[768,768]{1,0:T(8,128)(2,1)S(1)}, u32[]{:S(2)}, u32[]{:S(2)}) collective-permute-start(bf16[768,768]{1,0:T(8,128)(2,1)S(1)} %fusion.12), channel_id=1, source_target_pairs={{0,2},{1,3},{2,0},{3,1},{4,6},{5,7},{6,4},{7,5},{8,10},{9,11},{10,... | collective-permute-start | bytes 3538952 | tf_op jit(solution)/shard_map/ppermute | solution.py:651
  431.6 118.5 %collective-permute-start.70 = (bf16[768,768]{1,0:T(8,128)(2,1)S(1)}, bf16[768,768]{1,0:T(8,128)(2,1)S(1)}, u32[]{:S(2)}, u32[]{:S(2)}) collective-permute-start(bf16[768,768]{1,0:T(8,128)(2,1)S(1)} %fusion.13), channel_id=1, source_target_pairs={{0,2},{1,3},{2,0},{3,1},{4,6},{5,7},{6,4},{7,5},{8,10},{9,11},{10,... | collective-permute-start | bytes 3538952 | tf_op jit(solution)/shard_map/ppermute | solution.py:651
  449.0 126.4 %collective-permute-start.78 = (bf16[768,768]{1,0:T(8,128)(2,1)S(1)}, bf16[768,768]{1,0:T(8,128)(2,1)S(1)}, u32[]{:S(2)}, u32[]{:S(2)}) collective-permute-start(bf16[768,768]{1,0:T(8,128)(2,1)S(1)} %fusion.14), channel_id=1, source_target_pairs={{0,2},{1,3},{2,0},{3,1},{4,6},{5,7},{6,4},{7,5},{8,10},{9,11},{10,... | collective-permute-start | bytes 3538952 | tf_op jit(solution)/shard_map/ppermute | solution.py:651
  474.3 130.2 %collective-permute-start.62 = (bf16[896,768]{1,0:T(8,128)(2,1)S(1)}, bf16[896,768]{1,0:T(8,128)(2,1)S(1)}, u32[]{:S(2)}, u32[]{:S(2)}) collective-permute-start(bf16[896,768]{1,0:T(8,128)(2,1)S(1)} %fusion.7), channel_id=1, source_target_pairs={{0,2},{1,3},{2,0},{3,1},{4,6},{5,7},{6,4},{7,5},{8,10},{9,11},{10,... | collective-permute-start | bytes 4128776 | tf_op jit(solution)/shard_map/ppermute | solution.py:651
  499.6 79.2 %collective-permute-start.26 = (bf16[384,768]{1,0:T(8,128)(2,1)S(1)}, bf16[384,768]{1,0:T(8,128)(2,1)S(1)}, u32[]{:S(2)}, u32[]{:S(2)}) collective-permute-start(bf16[384,768]{1,0:T(8,128)(2,1)S(1)} %constant_dynamic-slice_fusion.20), channel_id=1, source_target_pairs={{0,4},{4,0},{8,12},{12,8},{16,20},{20,16},{24,28},{28,24},{1,5},{5... | collective-permute-start | bytes 1769480 | tf_op jit(solution)/shard_map/ppermute | solution.py:651
  524.9 54.8 %collective-permute-start.39 = (bf16[384,768]{1,0:T(8,128)(2,1)S(1)}, bf16[384,768]{1,0:T(8,128)(2,1)S(1)}, u32[]{:S(2)}, u32[]{:S(2)}) collective-permute-start(bf16[384,768]{1,0:T(8,128)(2,1)S(1)} %constant_dynamic-slice_fusion.17), channel_id=1, source_target_pairs={{0,4},{4,0},{8,12},{12,8},{16,20},{20,16},{24,28},{28,24},{1,5},{5... | collective-permute-start | bytes 1769480 | tf_op jit(solution)/shard_map/ppermute | solution.py:651
  550.2 31.2 %collective-permute-start.47 = (bf16[384,768]{1,0:T(8,128)(2,1)S(1)}, bf16[384,768]{1,0:T(8,128)(2,1)S(1)}, u32[]{:S(2)}, u32[]{:S(2)}) collective-permute-start(bf16[384,768]{1,0:T(8,128)(2,1)S(1)} %constant_dynamic-slice_fusion.14), channel_id=1, source_target_pairs={{0,4},{4,0},{8,12},{12,8},{16,20},{20,16},{24,28},{28,24},{1,5},{5... | collective-permute-start | bytes 1769480 | tf_op jit(solution)/shard_map/ppermute | solution.py:651
  575.4 31.0 %collective-permute-start.55 = (bf16[384,768]{1,0:T(8,128)(2,1)S(1)}, bf16[384,768]{1,0:T(8,128)(2,1)S(1)}, u32[]{:S(2)}, u32[]{:S(2)}) collective-permute-start(bf16[384,768]{1,0:T(8,128)(2,1)S(1)} %constant_dynamic-slice_fusion.11), channel_id=1, source_target_pairs={{0,4},{4,0},{8,12},{12,8},{16,20},{20,16},{24,28},{28,24},{1,5},{5... | collective-permute-start | bytes 1769480 | tf_op jit(solution)/shard_map/ppermute | solution.py:651
  578.8 28.7 %collective-permute-start.71 = (bf16[384,768]{1,0:T(8,128)(2,1)S(1)}, bf16[384,768]{1,0:T(8,128)(2,1)S(1)}, u32[]{:S(2)}, u32[]{:S(2)}) collective-permute-start(bf16[384,768]{1,0:T(8,128)(2,1)S(1)} %constant_dynamic-slice_fusion.5), channel_id=1, source_target_pairs={{0,4},{4,0},{8,12},{12,8},{16,20},{20,16},{24,28},{28,24},{1,5},{5... | collective-permute-start | bytes 1769480 | tf_op jit(solution)/shard_map/ppermute | solution.py:651
  579.6 37.3 %collective-permute-start.79 = (bf16[384,768]{1,0:T(8,128)(2,1)S(1)}, bf16[384,768]{1,0:T(8,128)(2,1)S(1)}, u32[]{:S(2)}, u32[]{:S(2)}) collective-permute-start(bf16[384,768]{1,0:T(8,128)(2,1)S(1)} %constant_dynamic-slice_fusion.2), channel_id=1, source_target_pairs={{0,4},{4,0},{8,12},{12,8},{16,20},{20,16},{24,28},{28,24},{1,5},{5... | collective-permute-start | bytes 1769480 | tf_op jit(solution)/shard_map/ppermute | solution.py:651
  581.4 37.2 %collective-permute-start.27 = (bf16[192,768]{1,0:T(8,128)(2,1)S(1)}, bf16[192,768]{1,0:T(8,128)(2,1)S(1)}, u32[]{:S(2)}, u32[]{:S(2)}) collective-permute-start(bf16[192,768]{1,0:T(8,128)(2,1)S(1)} %constant_dynamic-slice_fusion.19), channel_id=1, source_target_pairs={{0,8},{4,12},{8,0},{12,4},{16,24},{20,28},{24,16},{28,20},{1,9},{5... | collective-permute-start | bytes 884744 | tf_op jit(solution)/shard_map/ppermute | solution.py:651
  607.5 93.7 %collective-permute-start.63 = (bf16[448,768]{1,0:T(8,128)(2,1)S(1)}, bf16[448,768]{1,0:T(8,128)(2,1)S(1)}, u32[]{:S(2)}, u32[]{:S(2)}) collective-permute-start(bf16[448,768]{1,0:T(8,128)(2,1)S(1)} %constant_dynamic-slice_fusion.8), channel_id=1, source_target_pairs={{0,4},{4,0},{8,12},{12,8},{16,20},{20,16},{24,28},{28,24},{1,5},{5... | collective-permute-start | bytes 2064392 | tf_op jit(solution)/shard_map/ppermute | solution.py:651
  619.5 26.1 %collective-permute-start.80 = (bf16[192,768]{1,0:T(8,128)(2,1)S(1)}, bf16[192,768]{1,0:T(8,128)(2,1)S(1)}, u32[]{:S(2)}, u32[]{:S(2)}) collective-permute-start(bf16[192,768]{1,0:T(8,128)(2,1)S(1)} %constant_dynamic-slice_fusion.1), channel_id=1, source_target_pairs={{0,8},{4,12},{8,0},{12,4},{16,24},{20,28},{24,16},{28,20},{1,9},{5... | collective-permute-start | bytes 884744 | tf_op jit(solution)/shard_map/ppermute | solution.py:651
  621.0 26.1 %collective-permute-start.28 = (bf16[96,768]{1,0:T(8,128)(2,1)S(1)}, bf16[96,768]{1,0:T(8,128)(2,1)S(1)}, u32[]{:S(2)}, u32[]{:S(2)}) collective-permute-start(bf16[96,768]{1,0:T(8,128)(2,1)S(1)} %constant_dynamic-slice_fusion.18), channel_id=1, source_target_pairs={{0,16},{4,20},{8,24},{12,28},{16,0},{20,4},{24,8},{28,12},{1,17},{... | collective-permute-start | bytes 442376 | tf_op jit(solution)/shard_map/ppermute | solution.py:651
  639.7 23.5 %collective-permute-start.49 = (bf16[96,768]{1,0:T(8,128)(2,1)S(1)}, bf16[96,768]{1,0:T(8,128)(2,1)S(1)}, u32[]{:S(2)}, u32[]{:S(2)}) collective-permute-start(bf16[96,768]{1,0:T(8,128)(2,1)S(1)} %constant_dynamic-slice_fusion.12), channel_id=1, source_target_pairs={{0,16},{4,20},{8,24},{12,28},{16,0},{20,4},{24,8},{28,12},{1,17},{... | collective-permute-start | bytes 442376 | tf_op jit(solution)/shard_map/ppermute | solution.py:651
  645.6 27.1 %collective-permute-start.57 = (bf16[96,768]{1,0:T(8,128)(2,1)S(1)}, bf16[96,768]{1,0:T(8,128)(2,1)S(1)}, u32[]{:S(2)}, u32[]{:S(2)}) collective-permute-start(bf16[96,768]{1,0:T(8,128)(2,1)S(1)} %constant_dynamic-slice_fusion.9), channel_id=1, source_target_pairs={{0,16},{4,20},{8,24},{12,28},{16,0},{20,4},{24,8},{28,12},{1,17},{... | collective-permute-start | bytes 442376 | tf_op jit(solution)/shard_map/ppermute | solution.py:651
  647.1 35.1 %collective-permute-start.73 = (bf16[96,768]{1,0:T(8,128)(2,1)S(1)}, bf16[96,768]{1,0:T(8,128)(2,1)S(1)}, u32[]{:S(2)}, u32[]{:S(2)}) collective-permute-start(bf16[96,768]{1,0:T(8,128)(2,1)S(1)} %constant_dynamic-slice_fusion.3), channel_id=1, source_target_pairs={{0,16},{4,20},{8,24},{12,28},{16,0},{20,4},{24,8},{28,12},{1,17},{... | collective-permute-start | bytes 442376 | tf_op jit(solution)/shard_map/ppermute | solution.py:651
  648.8 42.9 %collective-permute-start.81 = (bf16[96,768]{1,0:T(8,128)(2,1)S(1)}, bf16[96,768]{1,0:T(8,128)(2,1)S(1)}, u32[]{:S(2)}, u32[]{:S(2)}) collective-permute-start(bf16[96,768]{1,0:T(8,128)(2,1)S(1)} %constant_dynamic-slice_fusion), channel_id=1, source_target_pairs={{0,16},{4,20},{8,24},{12,28},{16,0},{20,4},{24,8},{28,12},{1,17},{... | collective-permute-start | bytes 442376 | tf_op jit(solution)/shard_map/ppermute | solution.py:651
  663.2 31.6 %collective-permute-start.29 = (bf16[96,768]{1,0:T(8,128)(2,1)S(1)}, bf16[96,768]{1,0:T(8,128)(2,1)S(1)}, u32[]{:S(2)}, u32[]{:S(2)}) collective-permute-start(bf16[96,768]{1,0:T(8,128)(2,1)S(1)} %add_convert_fusion.27), channel_id=1, source_target_pairs={{0,16},{4,20},{8,24},{12,28},{16,0},{20,4},{24,8},{28,12},{1,17},{... | collective-permute-start | bytes 442376 | tf_op jit(solution)/shard_map/ppermute | solution.py:651
  672.7 25.3 %collective-permute-start.42 = (bf16[96,768]{1,0:T(8,128)(2,1)S(1)}, bf16[96,768]{1,0:T(8,128)(2,1)S(1)}, u32[]{:S(2)}, u32[]{:S(2)}) collective-permute-start(bf16[96,768]{1,0:T(8,128)(2,1)S(1)} %add_convert_fusion.26), channel_id=1, source_target_pairs={{0,16},{4,20},{8,24},{12,28},{16,0},{20,4},{24,8},{28,12},{1,17},{... | collective-permute-start | bytes 442376 | tf_op jit(solution)/shard_map/ppermute | solution.py:651
  701.1 28.9 %collective-permute-start.30 = (bf16[192,768]{1,0:T(8,128)(2,1)S(1)}, bf16[192,768]{1,0:T(8,128)(2,1)S(1)}, u32[]{:S(2)}, u32[]{:S(2)}) collective-permute-start(bf16[192,768]{1,0:T(8,128)(2,1)S(1)} %maximum_select_fusion.15), channel_id=1, source_target_pairs={{0,8},{4,12},{8,0},{12,4},{16,24},{20,28},{24,16},{28,20},{1,9},{5... | collective-permute-start | bytes 884744 | tf_op jit(solution)/shard_map/ppermute | solution.py:651
  701.2 30.0 %collective-permute-start.43 = (bf16[192,768]{1,0:T(8,128)(2,1)S(1)}, bf16[192,768]{1,0:T(8,128)(2,1)S(1)}, u32[]{:S(2)}, u32[]{:S(2)}) collective-permute-start(bf16[192,768]{1,0:T(8,128)(2,1)S(1)} %maximum_select_fusion.16), channel_id=1, source_target_pairs={{0,8},{4,12},{8,0},{12,4},{16,24},{20,28},{24,16},{28,20},{1,9},{5... | collective-permute-start | bytes 884744 | tf_op jit(solution)/shard_map/ppermute | solution.py:651
  704.4 25.5 %collective-permute-start.64 = (bf16[224,768]{1,0:T(8,128)(2,1)S(1)}, bf16[224,768]{1,0:T(8,128)(2,1)S(1)}, u32[]{:S(2)}, u32[]{:S(2)}) collective-permute-start(bf16[224,768]{1,0:T(8,128)(2,1)S(1)} %constant_dynamic-slice_fusion.7), channel_id=1, source_target_pairs={{0,8},{4,12},{8,0},{12,4},{16,24},{20,28},{24,16},{28,20},{1,9},{5... | collective-permute-start | bytes 1032200 | tf_op jit(solution)/shard_map/ppermute | solution.py:651
  707.5 38.9 %collective-permute-start.51 = (bf16[192,768]{1,0:T(8,128)(2,1)S(1)}, bf16[192,768]{1,0:T(8,128)(2,1)S(1)}, u32[]{:S(2)}, u32[]{:S(2)}) collective-permute-start(bf16[192,768]{1,0:T(8,128)(2,1)S(1)} %maximum_select_fusion.17), channel_id=1, source_target_pairs={{0,8},{4,12},{8,0},{12,4},{16,24},{20,28},{24,16},{28,20},{1,9},{5... | collective-permute-start | bytes 884744 | tf_op jit(solution)/shard_map/ppermute | solution.py:651
  709.9 40.3 %collective-permute-start.59 = (bf16[192,768]{1,0:T(8,128)(2,1)S(1)}, bf16[192,768]{1,0:T(8,128)(2,1)S(1)}, u32[]{:S(2)}, u32[]{:S(2)}) collective-permute-start(bf16[192,768]{1,0:T(8,128)(2,1)S(1)} %maximum_select_fusion.18), channel_id=1, source_target_pairs={{0,8},{4,12},{8,0},{12,4},{16,24},{20,28},{24,16},{28,20},{1,9},{5... | collective-permute-start | bytes 884744 | tf_op jit(solution)/shard_map/ppermute | solution.py:651
  729.9 26.3 %collective-permute-start.75 = (bf16[192,768]{1,0:T(8,128)(2,1)S(1)}, bf16[192,768]{1,0:T(8,128)(2,1)S(1)}, u32[]{:S(2)}, u32[]{:S(2)}) collective-permute-start(bf16[192,768]{1,0:T(8,128)(2,1)S(1)} %maximum_select_fusion.19), channel_id=1, source_target_pairs={{0,8},{4,12},{8,0},{12,4},{16,24},{20,28},{24,16},{28,20},{1,9},{5... | collective-permute-start | bytes 884744 | tf_op jit(solution)/shard_map/ppermute | solution.py:651
  731.2 31.3 %collective-permute-start.83 = (bf16[192,768]{1,0:T(8,128)(2,1)S(1)}, bf16[192,768]{1,0:T(8,128)(2,1)S(1)}, u32[]{:S(2)}, u32[]{:S(2)}) collective-permute-start(bf16[192,768]{1,0:T(8,128)(2,1)S(1)} %maximum_select_fusion.20), channel_id=1, source_target_pairs={{0,8},{4,12},{8,0},{12,4},{16,24},{20,28},{24,16},{28,20},{1,9},{5... | collective-permute-start | bytes 884744 | tf_op jit(solution)/shard_map/ppermute | solution.py:651
  750.1 42.5 %collective-permute-start.44 = (bf16[384,768]{1,0:T(8,128)(2,1)S(1)}, bf16[384,768]{1,0:T(8,128)(2,1)S(1)}, u32[]{:S(2)}, u32[]{:S(2)}) collective-permute-start(bf16[384,768]{1,0:T(8,128)(2,1)S(1)} %maximum_select_fusion.9), channel_id=1, source_target_pairs={{0,4},{4,0},{8,12},{12,8},{16,20},{20,16},{24,28},{28,24},{1,5},{5... | collective-permute-start | bytes 1769480 | tf_op jit(solution)/shard_map/ppermute | solution.py:651
  755.3 31.2 %collective-permute-start.60 = (bf16[384,768]{1,0:T(8,128)(2,1)S(1)}, bf16[384,768]{1,0:T(8,128)(2,1)S(1)}, u32[]{:S(2)}, u32[]{:S(2)}) collective-permute-start(bf16[384,768]{1,0:T(8,128)(2,1)S(1)} %maximum_select_fusion.11), channel_id=1, source_target_pairs={{0,4},{4,0},{8,12},{12,8},{16,20},{20,16},{24,28},{28,24},{1,5},{5... | collective-permute-start | bytes 1769480 | tf_op jit(solution)/shard_map/ppermute | solution.py:651
  762.5 36.6 %collective-permute-start.52 = (bf16[384,768]{1,0:T(8,128)(2,1)S(1)}, bf16[384,768]{1,0:T(8,128)(2,1)S(1)}, u32[]{:S(2)}, u32[]{:S(2)}) collective-permute-start(bf16[384,768]{1,0:T(8,128)(2,1)S(1)} %maximum_select_fusion.10), channel_id=1, source_target_pairs={{0,4},{4,0},{8,12},{12,8},{16,20},{20,16},{24,28},{28,24},{1,5},{5... | collective-permute-start | bytes 1769480 | tf_op jit(solution)/shard_map/ppermute | solution.py:651
  764.2 47.6 %collective-permute-start.76 = (bf16[384,768]{1,0:T(8,128)(2,1)S(1)}, bf16[384,768]{1,0:T(8,128)(2,1)S(1)}, u32[]{:S(2)}, u32[]{:S(2)}) collective-permute-start(bf16[384,768]{1,0:T(8,128)(2,1)S(1)} %maximum_select_fusion.12), channel_id=1, source_target_pairs={{0,4},{4,0},{8,12},{12,8},{16,20},{20,16},{24,28},{28,24},{1,5},{5... | collective-permute-start | bytes 1769480 | tf_op jit(solution)/shard_map/ppermute | solution.py:651
  769.8 54.6 %collective-permute-start.84 = (bf16[384,768]{1,0:T(8,128)(2,1)S(1)}, bf16[384,768]{1,0:T(8,128)(2,1)S(1)}, u32[]{:S(2)}, u32[]{:S(2)}) collective-permute-start(bf16[384,768]{1,0:T(8,128)(2,1)S(1)} %maximum_select_fusion.13), channel_id=1, source_target_pairs={{0,4},{4,0},{8,12},{12,8},{16,20},{20,16},{24,28},{28,24},{1,5},{5... | collective-permute-start | bytes 1769480 | tf_op jit(solution)/shard_map/ppermute | solution.py:651
  786.5 48.6 %collective-permute-start.68 = (bf16[448,768]{1,0:T(8,128)(2,1)S(1)}, bf16[448,768]{1,0:T(8,128)(2,1)S(1)}, u32[]{:S(2)}, u32[]{:S(2)}) collective-permute-start(bf16[448,768]{1,0:T(8,128)(2,1)S(1)} %maximum_select_fusion.7), channel_id=1, source_target_pairs={{0,4},{4,0},{8,12},{12,8},{16,20},{20,16},{24,28},{28,24},{1,5},{5... | collective-permute-start | bytes 2064392 | tf_op jit(solution)/shard_map/ppermute | solution.py:651
  (65 other events, 1516.1 us)

commit v2 on v1

--- a/solution.py
+++ b/solution.py
@@ -164,8 +164,9 @@
         fetch_wait(w2, w2_s, sem2, r)
         dh = dot_nt(dob[...], w2_s[r])
         dz = (dh * slope_in[j].astype(F32)).astype(BF)
-        (g2k if j == 0 else g2s)[0] = dot_tn(h_in[j], dob[...]).astype(BF)
-        (g1k if j == 0 else g1s)[0] = dot_tn(ub[...], dz).astype(BF)
+        hidden, model = w2_s.shape[1:]
+        (g2k if j == 0 else g2s)[0, 0:hidden] = dot_tn(h_in[j], dob[...]).astype(BF)
+        (g1k if j == 0 else g1s)[0, 0:model] = dot_tn(ub[...], dz).astype(BF)
         dc1[0, j : j + 1, :] = jnp.sum(dz.astype(F32), axis=0, keepdims=True)
         fetch_wait(w1, w1_s, sem1, r)
         acc[...] += dot_nt(dz, w1_s[r])
@@ -475,13 +476,13 @@
     return outs[0], (u, outs[1], outs[2], outs[3])
 
 
-def feed_backward(grad, cot, saved, w1, w2, vec, name):
+def feed_backward(links, grad, cot, saved, w1, w2, vec, name):
     u, e, h, slope = saved
     rows, model = u.shape
     hidden = w1[0].shape[1]
     has_grad = grad is not None
-    g = ((2, model, hidden), BF, "half")
-    g2 = ((2, hidden, model), BF, "half")
+    g = ((2, links.padded(model), hidden), BF, "half")
+    g2 = ((2, links.padded(hidden), model), BF, "half")
     return call(
         functools.partial(ffn_backward_kernel, has_grad),
         name,
@@ -548,11 +549,11 @@
     return outs[0], (x, outs[1], outs[2], outs[3], outs[4], outs[5], outs[6])
 
 
-def self_backward(dy, saved, items, w, vec, dtype, name):
+def self_backward(links, dy, saved, items, w, vec, dtype, name):
     x, e, q, k, v, p, a = saved
     rows, model = x.shape
     width = q.shape[2]
-    g = ((2,) + w[0].shape, BF, "half")
+    g = ((2, links.padded(w[0].shape[0]), model), BF, "half")
     return call(
         functools.partial(self_backward_kernel, items),
         name,
@@ -612,11 +613,11 @@
     return outs[0], (u, outs[1], outs[2], outs[3], outs[4], outs[5], outs[6])
 
 
-def cross_backward(dy, saved, pf, patches, items, w, vec, name):
+def cross_backward(links, dy, saved, pf, patches, items, w, vec, name):
     u, e, q, k, v, p, a = saved
     rows, model = u.shape
     width = q.shape[2]
-    g = ((2,) + w[0].shape, BF, "half")
+    g = ((2, links.padded(w[0].shape[0]), model), BF, "half")
     return call(
         functools.partial(cross_backward_kernel, items, patches),
         name,
@@ -647,6 +648,246 @@
     )
 
 
+def pair(index, width):
+    return index + width - 2 * width * ((index // width) % 2)
+
+
+def add_rounded(a, b):
+    return (a.astype(F32) + b.astype(F32)).astype(BF)
+
+
+def reduce_kernel(n_tensor, n_dp, counts, chunk, *refs):
+    arrays = len(counts)
+    bits = n_dp.bit_length() - 1
+    sends, keeps = refs[:arrays], refs[arrays : 2 * arrays]
+    small_send, small_keep = refs[2 * arrays : 2 * arrays + 2]
+    outs = refs[2 * arrays + 2 : 3 * arrays + 2]
+    small_out = refs[3 * arrays + 2]
+    rest = list(refs[3 * arrays + 3 :])
+    core_in, kept, far_out, far_in, own, whole_sum = rest[:6]
+    parts, halves_in = rest[6 : 6 + bits], rest[6 + bits : 6 + 2 * bits]
+    gathered, tiny_sum, tiny_core, tiny_far, tiny_dp = rest[6 + 2 * bits : 11 + 2 * bits]
+    send_sem, recv_sem, kept_sem, out_sem, tiny_send, tiny_recv = rest[11 + 2 * bits :]
+
+    t, d = lax.axis_index("tensor"), lax.axis_index("dp")
+    core_peer = {"tensor": pair(t, 1)}
+    far_peer = {"tensor": lax.rem(t + 2, n_tensor)}
+    dp_peers = [{"dp": pair(d, 1 << b)} for b in range(bits)]
+    dp_bits = [(d // (1 << b)) % 2 for b in range(bits)]
+    peers = [core_peer, far_peer] + dp_peers
+
+    barrier = pltpu.get_barrier_semaphore()
+    for peer in peers:
+        pl.semaphore_signal(
+            barrier, inc=1, device_id=peer, device_id_type=pl.DeviceIdType.MESH
+        )
+    pl.semaphore_wait(barrier, len(peers))
+
+    total = sum(counts)
+    stages = 2 + 2 * bits
+    slots = core_in.shape[0]
+    depth = gathered.shape[0]
+
+    def remote(source, target, stage, slot, peer):
+        return pltpu.make_async_remote_copy(
+            src_ref=source,
+            dst_ref=target,
+            send_sem=send_sem.at[stage, slot],
+            recv_sem=recv_sem.at[stage, slot],
+            device_id=peer,
+            device_id_type=pl.DeviceIdType.MESH,
+        )
+
+    def region(b):
+        size = chunk >> (b + 1)
+        start = 0
+        for i in range(b + 1):
+            start = start + dp_bits[i] * (chunk >> (i + 1))
+        return pl.ds(pl.multiple_of(start, size), size)
+
+    def copy_of(stage, m):
+        slot, ring = lax.rem(m, slots), lax.rem(m, depth)
+        if stage == 0:
+            return remote(
+                sends[0].at[:, pl.ds(0, chunk)], core_in.at[slot], 0, slot, core_peer
+            )
+        if stage == 1:
+            return remote(far_out.at[slot], far_in.at[slot], 1, slot, far_peer)
+        if stage < 2 + bits:
+            b = stage - 2
+            size = chunk >> (b + 1)
+            source = whole_sum if b == 0 else parts[b - 1]
+            gone = pl.ds(pl.multiple_of((1 - dp_bits[b]) * size, size), size)
+            return remote(
+                source.at[slot, gone], halves_in[b].at[slot], stage, slot, dp_peers[b]
+            )
+        b = 2 * bits + 1 - stage
+        held = gathered.at[ring, region(b)]
+        return remote(held, held, stage, slot, dp_peers[b])
+
+    def kept_copy(a, m, base):
+        slot = lax.rem(m, slots)
+        rows = pl.ds(pl.multiple_of((m - base) * chunk, chunk), chunk)
+        return pltpu.make_async_copy(keeps[a].at[:, rows], kept.at[slot], kept_sem.at[slot])
+
+    def out_copy(a, m, base):
+        ring = lax.rem(m, depth)
+        rows = pl.ds(pl.multiple_of((m - base) * chunk, chunk), chunk)
+        return pltpu.make_async_copy(gathered.at[ring], outs[a].at[rows], out_sem.at[ring])
+
+    def each_array(m, act):
+        base = 0
+        for a in range(arrays):
+
+            @pl.when((m >= base) & (m < base + counts[a]))
+            def _(a=a, base=base):
+                act(a, base)
+
+            base += counts[a]
+
+    def process(stage, m):
+        slot, ring = lax.rem(m, slots), lax.rem(m, depth)
+        if stage == 0:
+
+            def begin(a, base):
+                rows = pl.ds(pl.multiple_of((m - base) * chunk, chunk), chunk)
+                remote(
+                    sends[a].at[:, rows], core_in.at[slot], 0, slot, core_peer
+                ).start()
+                kept_copy(a, m, base).start()
+
+            each_array(m, begin)
+            return
+        if stage <= stages:
+            copy_of(stage - 1, m).wait()
+        if stage == 1:
+            kept_copy(0, m, m).wait()
+            far_out[slot] = add_rounded(kept[slot, 1], core_in[slot, 1])
+            own[slot] = add_rounded(kept[slot, 0], core_in[slot, 0])
+        elif stage == 2:
+            whole_sum[slot] = add_rounded(own[slot], far_in[slot])
+        elif stage <= 2 + bits:
+            b = stage - 3
+            size = chunk >> (b + 1)
+            source = whole_sum if b == 0 else parts[b - 1]
+            mine = pl.ds(pl.multiple_of(dp_bits[b] * size, size), size)
+            summed = add_rounded(source[slot, mine], halves_in[b][slot])
+            if b < bits - 1:
+                parts[b][slot] = summed
+            else:
+                gathered[ring, region(b)] = summed
+        elif stage == stages:
+            each_array(m, lambda a, base: out_copy(a, m, base).start())
+        elif stage == stages + 1:
+            out_copy(0, m, m).wait()
+        if stage < stages:
+            copy_of(stage, m).start()
+
+    units = small_keep.shape[0] - tiny_far.shape[0]
+
+    def tiny(stage):
+        if stage == 0:
+            source, target = small_send, tiny_core
+        elif stage == 1:
+            source, target = tiny_sum.at[0, pl.ds(units, tiny_far.shape[0])], tiny_far
+        else:
+            source = tiny_sum.at[stage - 1, pl.ds(0, tiny_far.shape[0])]
+            target = tiny_dp.at[stage - 2]
+        return pltpu.make_async_remote_copy(
+            src_ref=source,
+            dst_ref=target,
+            send_sem=tiny_send.at[stage],
+            recv_sem=tiny_recv.at[stage],
+            device_id=peers[stage],
+            device_id_type=pl.DeviceIdType.MESH,
+        )
+
+    def tiny_step(stage):
+        if stage > 0:
+            tiny(stage - 1).wait()
+        count = tiny_far.shape[0]
+        if stage == 1:
+            tiny_sum[0] = small_keep[...] + tiny_core[...]
+        elif stage == 2:
+            tiny_sum[1, 0:units] = tiny_sum[0, 0:units] + tiny_far[0:units]
+            tiny_sum[1, units:count] = tiny_sum[0, 2 * units :] + tiny_far[units:]
+        elif stage > 2:
+            summed = tiny_sum[stage - 2, 0:count] + tiny_dp[stage - 3]
+            if stage == 2 + bits:
+                small_out[...] = summed
+            else:
+                tiny_sum[stage - 1, 0:count] = summed
+        if stage < 2 + bits:
+            tiny(stage).start()
+
+    def tick(k, carry):
+        for stage in range(stages + 2):
+            m = k - stage
+
+            @pl.when((m >= 0) & (m < total))
+            def _(stage=stage, m=m):
+                process(stage, m)
+
+        for stage in range(3 + bits):
+
+            @pl.when(k == stage)
+            def _(stage=stage):
+                tiny_step(stage)
+
+        return carry
+
+    lax.fori_loop(0, total + stages + 2, tick, 0)
+
+
+def reduce_all(links, pairs, small_keep, small_send, units):
+    chunk = links.chunk
+    model = pairs[0][0].shape[2]
+    bits = links.bits
+    counts = [keep.shape[1] // chunk for keep, _ in pairs]
+    sends = [send for _, send in pairs]
+    keeps = [keep for keep, _ in pairs]
+    slots, depth = 4, 8
+    anywhere = pl.BlockSpec(memory_space=ANY)
+    vmem = pl.BlockSpec(memory_space=pltpu.VMEM)
+    rows = small_keep.shape[0]
+    stages = 2 + 2 * bits
+    outs = pl.pallas_call(
+        functools.partial(reduce_kernel, links.tensor, links.dp, counts, chunk),
+        in_specs=[anywhere] * (2 * len(pairs)) + [vmem] * 2,
+        out_specs=[anywhere] * len(pairs) + [vmem],
+        out_shape=[jax.ShapeDtypeStruct(keep.shape[1:], BF) for keep in keeps]
+        + [jax.ShapeDtypeStruct((rows - units, 128), F32)],
+        scratch_shapes=[
+            pltpu.VMEM((slots, 2, chunk, model), BF),
+            pltpu.VMEM((slots, 2, chunk, model), BF),
+            pltpu.VMEM((slots, chunk, model), BF),
+            pltpu.VMEM((slots, chunk, model), BF),
+            pltpu.VMEM((slots, chunk, model), BF),
+            pltpu.VMEM((slots, chunk, model), BF),
+        ]
+        + [pltpu.VMEM((slots, chunk >> (b + 1), model), BF) for b in range(bits)]
+        + [pltpu.VMEM((slots, chunk >> (b + 1), model), BF) for b in range(bits)]
+        + [
+            pltpu.VMEM((depth, chunk, model), BF),
+            pltpu.VMEM((1 + bits, rows, 128), F32),
+            pltpu.VMEM((rows, 128), F32),
+            pltpu.VMEM((rows - units, 128), F32),
+            pltpu.VMEM((bits, rows - units, 128), F32),
+            pltpu.SemaphoreType.DMA((stages, slots)),
+            pltpu.SemaphoreType.DMA((stages, slots)),
+            pltpu.SemaphoreType.DMA((slots,)),
+            pltpu.SemaphoreType.DMA((depth,)),
+            pltpu.SemaphoreType.DMA((2 + bits,)),
+            pltpu.SemaphoreType.DMA((2 + bits,)),
+        ],
+        compiler_params=pltpu.CompilerParams(
+            collective_id=0, has_side_effects=True, vmem_limit_bytes=VMEM_LIMIT
+        ),
+        name="reduce_gradients",
+    )(*sends, *keeps, small_send, small_keep)
+    return outs[:-1], outs[-1]
+
+
 def swap(array, axis, size, distance):
     return lax.ppermute(array, axis, [(i, i ^ distance) for i in range(size)])
 
@@ -656,6 +897,10 @@
         self.tensor = mesh.shape["tensor"]
         self.dp = mesh.shape["dp"]
         self.bits = self.dp.bit_length() - 1
+        self.chunk = max(256, 16 * self.dp)
+
+    def padded(self, rows):
+        return -(-rows // self.chunk) * self.chunk
 
     def core(self, array):
         return swap(array, "tensor", self.tensor, 1)
@@ -667,33 +912,15 @@
         across = self.far(own)
         return own, self.core(own), across, self.core(across)
 
-    def reduce(self, keep, send):
-        got = self.core(send)
-        other = (keep[1].astype(F32) + got[1].astype(F32)).astype(BF)
-        got_far = self.far(other)
-        total = keep[0].astype(F32) + got[0].astype(F32) + got_far.astype(F32)
-        total = total.astype(BF)
-        me = lax.axis_index("dp")
-        for b in range(self.bits):
-            bit = (me >> b) & 1
-            half = total.shape[0] // 2
-            mine = lax.dynamic_slice_in_dim(total, bit * half, half, 0)
-            gone = lax.dynamic_slice_in_dim(total, (1 - bit) * half, half, 0)
-            got = swap(gone, "dp", self.dp, 1 << b)
-            total = (mine.astype(F32) + got.astype(F32)).astype(BF)
-        for b in reversed(range(self.bits)):
-            bit = (me >> b) & 1
-            got = swap(total, "dp", self.dp, 1 << b)
-            total = jnp.where(
-                bit == 0,
-                jnp.concatenate([total, got], axis=0),
-                jnp.concatenate([got, total], axis=0),
-            )
-        return total.astype(F32)
-
 
 def flat(array):
     return array.reshape(-1)
+
+
+def lines(array):
+    n, values = array.shape
+    rows = -(-values // 1024) * 8
+    return jnp.pad(array, ((0, 0), (0, rows * 128 - values))).reshape(n, rows, 128)
 
 
 def self_pack(w_in, w_out):
@@ -704,7 +931,7 @@
 def self_unpack(total, width):
     model = total.shape[1]
     first = jnp.swapaxes(total[: 3 * width].reshape(3, width, model), 1, 2)
-    return first, total[3 * width :]
+    return first, total[3 * width : 4 * width]
 
 
 def cross_pack(w_query, w_out, w_keyval):
@@ -722,7 +949,7 @@
     model = total.shape[1]
     side = patch_width - model
     parts = model // side
-    tail = total[4 * width :]
+    tail = total[4 * width : 4 * width + 2 * width // parts]
     tail = jnp.swapaxes(tail.reshape(-1, parts, side), 0, 1).reshape(2 * width, side)
     keyval = jnp.concatenate([total[2 * width : 4 * width], tail], axis=1)
     keyval = jnp.swapaxes(keyval.reshape(2, width, patch_width), 1, 2)
@@ -814,30 +1041,21 @@
         h3, expand_two, contract_two, hidden_two, join_vecs[2], "join_feed_forward"
     )
 
-    du, g1k, g1s, g2k, g2s, dc_two, sums_five = feed_backward(
-        None, join_cot, saved_five, expand_two, contract_two, join_vecs[2], "join_feed_backward"
-    )
-    grad_join_contract = links.reduce(g2k, g2s)
-    grad_join_expand = links.reduce(g1k, g1s)
-    du, grad_patches, gk, gs, db_cross, sums_four = cross_backward(
-        du, saved_four, pf, patches, items, weights_cross, join_vecs[1], "cross_backward"
-    )
-    grad_query, grad_cross_out, grad_keyval = cross_unpack(
-        links.reduce(gk, gs), width, patch_width
-    )
-    du, gk, gs, db_two, sums_three = self_backward(
-        du, saved_three, items, weights_two, join_vecs[0], F32, "join_self_backward"
-    )
-    grad_join_in, grad_join_out = self_unpack(links.reduce(gk, gs), width)
-    du, g1k, g1s, g2k, g2s, dc_one, sums_two = feed_backward(
-        du, text_cot, saved_two, expand_one, contract_one, text_vecs[1], "text_feed_backward"
-    )
-    grad_text_contract = links.reduce(g2k, g2s)
-    grad_text_expand = links.reduce(g1k, g1s)
-    grad_text, gk, gs, db_one, sums_one = self_backward(
-        du, saved_one, items, weights_one, text_vecs[0], BF, "text_self_backward"
-    )
-    grad_text_in, grad_text_out = self_unpack(links.reduce(gk, gs), width)
+    du, e2k, e2s, k2k, k2s, dc_two, sums_five = feed_backward(
+        links, None, join_cot, saved_five, expand_two, contract_two, join_vecs[2], "join_feed_backward"
+    )
+    du, grad_patches, ck, cs, db_cross, sums_four = cross_backward(
+        links, du, saved_four, pf, patches, items, weights_cross, join_vecs[1], "cross_backward"
+    )
+    du, s2k, s2s, db_two, sums_three = self_backward(
+        links, du, saved_three, items, weights_two, join_vecs[0], F32, "join_self_backward"
+    )
+    du, e1k, e1s, k1k, k1s, dc_one, sums_two = feed_backward(
+        links, du, text_cot, saved_two, expand_one, contract_one, text_vecs[1], "text_feed_backward"
+    )
+    grad_text, s1k, s1s, db_one, sums_one = self_backward(
+        links, du, saved_one, items, weights_one, text_vecs[0], BF, "text_self_backward"
+    )
 
     blocks = jnp.concatenate(
         [
@@ -849,18 +1067,22 @@
         ],
         axis=1,
     )
-    shared = jnp.stack([sums_one, sums_two, sums_three, sums_four, sums_five])
-    units = blocks.shape[1]
-    count = shared.size
-    got = links.core(jnp.concatenate([blocks[1], blocks[3], flat(shared)]))
-    own = blocks[0] + got[:units]
-    other = blocks[2] + got[units : 2 * units]
-    shared = flat(shared) + got[2 * units :]
-    got = links.far(jnp.concatenate([other, shared]))
-    small = jnp.concatenate([own, shared]) + got
-    for b in range(links.bits):
-        small = small + swap(small, "dp", links.dp, 1 << b)
-    shared = small[units:].reshape(5, 3, model)
+    shared = flat(jnp.stack([sums_one, sums_two, sums_three, sums_four, sums_five]))
+    units, count = blocks.shape[1], shared.shape[0]
+    blocks = lines(blocks)
+    shared = lines(shared[None])[0]
+    small_keep = jnp.concatenate([blocks[0], blocks[2], shared], axis=0)
+    small_send = jnp.concatenate([blocks[1], blocks[3], shared], axis=0)
+    pairs = [(k2k, k2s), (e2k, e2s), (ck, cs), (s2k, s2s), (k1k, k1s), (e1k, e1s), (s1k, s1s)]
+    totals, small = reduce_all(links, pairs, small_keep, small_send, blocks.shape[1])
+    totals = [total.astype(F32) for total in totals]
+    grad_join_contract, grad_join_expand = totals[0][:hidden], totals[1][:model]
+    grad_query, grad_cross_out, grad_keyval = cross_unpack(totals[2], width, patch_width)
+    grad_join_in, grad_join_out = self_unpack(totals[3], width)
+    grad_text_contract, grad_text_expand = totals[4][:hidden], totals[5][:model]
+    grad_text_in, grad_text_out = self_unpack(totals[6], width)
+    shared = flat(small[blocks.shape[1] :])[:count].reshape(5, 3, model)
+    small = flat(small[: blocks.shape[1]])[:units]
     attend = small[: 6 * width].reshape(6, width)
     text_shared, join_shared = shared[0:2], shared[2:5]
 

time: 848 us -> 660 us (0.78)
  waiting for transfers between devices: 510 us -> 173 us
  Pallas kernels: 178 us -> 412 us
  starting transfers between devices: 77.1 us -> 14 us
  other arithmetic: 43.4 us -> 20 us
    ppermute x85 -> x24, waiting for transfers between devices: 510 us -> 173 us  [swap(): return lax.ppermute(array, axis, [(i, i ^ distance) for i in range(size)])]
    pallas_call x0 -> x1, Pallas kernels: none -> 234 us  [reduce_all(): pl.pallas_call(functools.partial(reduce_kernel, links.tensor, links.dp, c...]
    ppermute x85 -> x24, starting transfers between devices: 77.1 us -> 14 us  [swap(): return lax.ppermute(array, axis, [(i, i ^ distance) for i in range(size)])]
    convert_element_type x42 -> x5, other arithmetic: 30.3 us -> 9.53 us  [per_device(): totals = [total.astype(F32) for total in totals]]
  transfers between devices with their start and end apart: 85 -> 24, of which waited for: 44 -> 6; matrix products, arithmetic and copies ran while one was open for 7% -> 2% of each run, Pallas kernels for 7% -> 9%
where the time goes in v2:
time: 660 us; the launch traced here: 655 us
  Pallas kernels  412 us (62%)
  waiting for transfers between devices  173 us (26%)
  local copies, waits for them, and re-layouts  33.9 us (5%)
  other arithmetic  20 us (3%)
  starting transfers between devices  14 us (2%)
    pallas_call x1, Pallas kernels, reduce_all(): pl.pallas_call(functools.partial(reduce_kernel, links.tensor, links.dp, c...  234 us
    pallas_call x10, Pallas kernels, call(): pl.pallas_call(kernel, grid=(2,), in_specs=[kinds[kind](a.shape) for a, k...  178 us
    ppermute x24, waiting for transfers between devices, swap(): return lax.ppermute(array, axis, [(i, i ^ distance) for i in range(size)])  173 us
    ppermute x24, starting transfers between devices, swap(): return lax.ppermute(array, axis, [(i, i ^ distance) for i in range(size)])  14 us
    unnamed x94, local copies, waits for them, and re-layouts  13.3 us
  transfers between devices with their start and end apart: 24, of which 6 were waited for; matrix products, arithmetic and copies ran while one was open for 2% of the time, Pallas kernels for 9%

profile of v2, /device:TPU:0, one launch (start us, length us, event | category | flops | bytes accessed | tf_op | source)
XLA Modules:
  0.0 655.5 jit_solution(9504680279952242389)
XLA Ops:
  0.7 1.4 pad_maximum_fusion.2.refs_0_
  2.1 3.0 collective-permute-start.1
  5.2 1.1 pad_maximum_fusion.3.refs_0_
  6.7 1.9 collective-permute-start.4
  8.6 48.0 %collective-permute-done.4 = bf16[1,2688]{1,0:T(2,128)(2,1)S(1)} collective-permute-done((bf16[1,2688]{1,0:T(2,128)(2,1)S(1)}, bf16[1,2688]{1,0:T(2,128)(2,1)S(1)}, u32[]{:S(2)}, u32[]{:S(2)}) %collective-permute-start.4) | collective-permute-done | bytes 5408 | tf_op jit(solution)/shard_map/ppermute | solution.py:892
  57.1 0.7 collective-permute-done.5
  57.8 1.7 collective-permute-start.7
  60.5 1.2 pad_maximum_fusion.1.refs_0_
  61.7 1.8 collective-permute-start.16
  63.5 23.4 %collective-permute-done.7.refs_2_.refs_6_ = bf16[768,768]{1,0:T(8,128)(2,1)} collective-permute-done((bf16[768,768]{1,0:T(8,128)(2,1)}, bf16[768,768]{1,0:T(8,128)(2,1)}, u32[]{:S(2)}, u32[]{:S(2)}) %collective-permute-start.7) | collective-permute-done | bytes 1179680 | tf_op jit(solution)/shard_map/ppermute | solution.py:892
  86.9 1.7 collective-permute-start.19
  89.0 23.2 %collective-permute-done.10.refs_6_.refs_10_ = bf16[768,768]{1,0:T(8,128)(2,1)} collective-permute-done((bf16[768,768]{1,0:T(8,128)(2,1)}, bf16[768,768]{1,0:T(8,128)(2,1)}, u32[]{:S(2)}, u32[]{:S(2)}) %collective-permute-start.10) | collective-permute-done | bytes 1179680 | tf_op jit(solution)/shard_map/ppermute | solution.py:892
  112.3 0.6 maximum_convert_fusion.3.refs_9_.refs_14_
  113.5 53.5 %collective-permute-done.19.refs_2_.refs_5_ = bf16[768,768]{1,0:T(8,128)(2,1)} collective-permute-done((bf16[768,768]{1,0:T(8,128)(2,1)}, bf16[768,768]{1,0:T(8,128)(2,1)}, u32[]{:S(2)}, u32[]{:S(2)}) %collective-permute-start.19) | collective-permute-done | bytes 1179680 | tf_op jit(solution)/shard_map/ppermute | solution.py:892
  167.0 24.5 %collective-permute-done.22.refs_6_.refs_9_ = bf16[768,768]{1,0:T(8,128)(2,1)} collective-permute-done((bf16[768,768]{1,0:T(8,128)(2,1)}, bf16[768,768]{1,0:T(8,128)(2,1)}, u32[]{:S(2)}, u32[]{:S(2)}) %collective-permute-start.22) | collective-permute-done | bytes 1179680 | tf_op jit(solution)/shard_map/ppermute | solution.py:892
  192.0 0.6 maximum_convert_fusion.2.refs_5_.refs_9_
  192.7 0.6 maximum_convert_fusion.6.refs_9_.refs_13_
  193.3 0.6 maximum_convert_fusion.4.refs_5_.refs_9_
  194.1 0.9 copy-done.32
  195.0 0.6 maximum_convert_fusion.5.refs_5_.refs_9_
  195.6 1.3 copy.85
  196.9 1.9 pad.12.clone
  200.0 1.0 reshape.172.refs_8_
  201.7 0.7 reshape.171.refs_4_
  202.4 0.7 reshape.166.refs_4_
  203.1 0.7 reshape.162.refs_4_
  203.8 13.4 %text_self_forward.1 = (f32[320,768]{1,0:T(8,128)}, f32[320,768]{1,0:T(8,128)}, bf16[4,320,192]{2,1,0:T(8,128)(2,1)}, bf16[4,320,192]{2,1,0:T(8,128)(2,1)}, bf16...) custom-call(s32[8]{0:T(128)} %lengths.3, bf16[320,768]{1,0:T(8,128)(2,1)} %bitcast.106, ...), custom_call_target="tpu_custom_call" | custom-call | flops 1509949440 | bytes 9464864 | tf_op jit(solution)/shard_map/text_self_forward/pallas_call | solution.py:432
  217.2 10.6 %text_feed_forward.1 = (bf16[320,768]{1,0:T(8,128)(2,1)}, f32[320,768]{1,0:T(8,128)}, bf16[4,320,768]{2,1,0:T(8,128)(2,1)}, bf16[4,320,768]{2,1,0:T(8,128)(2,1)}) custom-call(f32[320,768]{1,0:T(8,128)} %get-tuple-element.91.u.refs_3_, bf16[768,768]{1,0:T(8,128)(2,1)} %refs_4_.5, bf16[768,768]{1,0:T(8,128)(2,1)} %collective-permute-done.6.refs_1_.refs_5_, ...), custom_call_target="tpu_custom_call" | custom-call | flops 3019898880 | bytes 15848448 | tf_op jit(solution)/shard_map/text_feed_forward/pallas_call | solution.py:432
  227.8 13.3 %join_self_forward.1 = (f32[320,768]{1,0:T(8,128)}, f32[320,768]{1,0:T(8,128)}, bf16[4,320,192]{2,1,0:T(8,128)(2,1)}, bf16[4,320,192]{2,1,0:T(8,128)(2,1)}, bf16...) custom-call(s32[8]{0:T(128)} %lengths.3, ...), custom_call_target="tpu_custom_call" | custom-call | flops 1509949440 | bytes 9464864 | tf_op jit(solution)/shard_map/join_self_forward/pallas_call | solution.py:432
  241.1 21.2 %cross_forward.1 = (f32[320,768]{1,0:T(8,128)}, f32[320,768]{1,0:T(8,128)}, bf16[4,320,192]{2,1,0:T(8,128)(2,1)}, bf16[4,1280,192]{2,1,0:T(8,128)(2,1)}, bf16[4,...) custom-call(f32[320,768]{1,0:T(8,128)} %get-tuple-element.93.u, ...), custom_call_target="tpu_custom_call" | custom-call | flops 4781506560 | bytes 17234944 | tf_op jit(solution)/shard_map/cross_forward/pallas_call | solution.py:432
  262.3 1.0 copy-done.38
  263.3 10.5 %join_feed_forward.1 = (bf16[320,768]{1,0:T(8,128)(2,1)}, f32[320,768]{1,0:T(8,128)}, bf16[4,320,768]{2,1,0:T(8,128)(2,1)}, bf16[4,320,768]{2,1,0:T(8,128)(2,1)}) custom-call(f32[320,768]{1,0:T(8,128)} %get-tuple-element.94.u.refs_2_, bf16[768,768]{1,0:T(8,128)(2,1)} %refs_3_.1, bf16[768,768]{1,0:T(8,128)(2,1)} %copy-done.38, ...), custom_call_target="tpu_custom_call" | custom-call | flops 3019898880 | bytes 15848448 | tf_op jit(solution)/shard_map/join_feed_forward/pallas_call | solution.py:432
  273.8 17.0 %join_feed_backward.1 = (f32[320,768]{1,0:T(8,128)}, bf16[2,768,768]{2,1,0:T(8,128)(2,1)}, bf16[2,768,768]{2,1,0:T(8,128)(2,1)}, bf16[2,768,768]{2,1,0:T(8,128)(...) custom-call(bf16[320,768]{1,0:T(8,128)(2,1)} %bitcast.104, ...), custom_call_target="tpu_custom_call" | custom-call | flops 6039797760 | bytes 26277888 | tf_op jit(solution)/shard_map/join_feed_backward/pallas_call | solution.py:432
  290.7 32.9 %cross_backward.1 = (f32[320,768]{1,0:T(8,128)}, bf16[8,145,1024]{2,1,0:T(8,128)(2,1)}, bf16[2,1024,768]{2,1,0:T(8,128)(2,1)}, bf16[2,1024,768]{2,1,0:T(8,128)(2...) custom-call(f32[320,768]{1,0:T(8,128)} %get-tuple-element.99.dy, f32[320,768]{1,0:T(8,128)} %get-tuple-element.100.e_in, ...), custom_call_target="tpu_custom_call" | custom-call | flops 9563013120 | bytes 26894336 | tf_op jit(solution)/shard_map/cross_backward/pallas_call | solution.py:432
  323.6 21.2 %join_self_backward.1 = (f32[320,768]{1,0:T(8,128)}, bf16[2,768,768]{2,1,0:T(8,128)(2,1)}, bf16[2,768,768]{2,1,0:T(8,128)(2,1)}, f32[2,2,2,192]{3,2,1,0:T(2,128)}, f32[3,768]{1,0:T(4,128)}) custom-call(f32[320,768]{1,0:T(8,128)} %get-tuple-element.106.dy, f32[320,768]{1,0:T(8,128)} %get-tuple-element.107.e_in, bf16[320,768]{1,0:T(8,128)(2,1)} %get-tuple-element.92.x, ...), custom_call_target="tpu_custom_call" | custom-call | flops 3019898880 | bytes 15175680 | tf_op jit(solution)/shard_map/join_self_backward/pallas_call | solution.py:432
  344.8 17.3 %text_feed_backward.1 = (f32[320,768]{1,0:T(8,128)}, bf16[2,768,768]{2,1,0:T(8,128)(2,1)}, bf16[2,768,768]{2,1,0:T(8,128)(2,1)}, bf16[2,768,768]{2,1,0:T(8,128)(...) custom-call(f32[320,768]{1,0:T(8,128)} %get-tuple-element.113.refs_0_, ...), custom_call_target="tpu_custom_call" | custom-call | flops 6039797760 | bytes 27260928 | tf_op jit(solution)/shard_map/text_feed_backward/pallas_call | solution.py:432
  362.2 21.1 %text_self_backward.1 = (bf16[320,768]{1,0:T(8,128)(2,1)}, bf16[2,768,768]{2,1,0:T(8,128)(2,1)}, bf16[2,768,768]{2,1,0:T(8,128)(2,1)}, f32[2,2,2,192]{3,2,1,0:T(2,128)}, f32[3,768]{1,0:T(4,128)}) custom-call(f32[320,768]{1,0:T(8,128)} %get-tuple-element.117.dy, f32[320,768]{1,0:T(8,128)} %get-tuple-element.118.e_in, bf16[320,768]{1,0:T(8,128)(2,1)} %bitcast.107, ...), custom_call_target="tpu_custom_call" | custom-call | flops 3019898880 | bytes 14684160 | tf_op jit(solution)/shard_map/text_self_backward/pallas_call | solution.py:432
  383.3 0.8 reshape.177
  384.4 0.7 constant_dynamic-update-slice_fusion.9
  385.3 0.7 pad_maximum_fusion.4
  386.0 234.0 %reduce_gradients.1 = (bf16[768,768]{1,0:T(8,128)(2,1)}, bf16[768,768]{1,0:T(8,128)(2,1)}, bf16[1024,768]{1,0:T(8,128)(2,1)}, bf16[768,768]{1,0:T(8,128)(2,1)}, ...) custom-call(bf16[2,768,768]{2,1,0:T(8,128)(2,1)} %get-tuple-element.126.refs, ...), custom_call_target="tpu_custom_call" | custom-call | tf_op jit(solution)/shard_map/reduce_gradients/pallas_call | solution.py:854
  620.0 0.8 slice.212
  620.8 1.4 slice_bitcast_fusion.3
  622.1 0.7 slice.217
  622.9 0.8 slice.232
  623.6 1.8 slice.241
  625.5 1.3 slice.240
  627.3 0.9 slice.247
  628.2 1.3 copy-done
  629.5 0.9 slice.248
  630.5 1.9 convert_element_type.55
  632.3 0.7 slice.213
  633.0 0.7 slice.225
  637.4 0.9 copy.73
  638.3 1.2 copy.74
  639.4 2.9 convert_element_type.52
  642.4 1.1 slice_bitcast_fusion
  643.5 1.6 convert_element_type.53
  645.2 1.6 convert_element_type.56
  646.9 1.6 convert_element_type.57
  648.4 1.0 copy-done.4
  649.4 2.7 copy.78
  652.1 1.4 maximum_bitcast_fusion
  653.5 1.6 pad_maximum_fusion
  (160 shorter events, 10.3 us)
Async XLA Ops:
  0.7 4.5 slice-start
  0.7 4.5 copy-start.12
  2.1 4.2 copy-start.10
  2.1 57.4 %collective-permute-start.1 = (bf16[768,768]{1,0:T(8,128)(2,1)S(1)}, bf16[768,768]{1,0:T(8,128)(2,1)}, u32[]{:S(2)}, u32[]{:S(2)}) collective-permute-start(bf16[768,768]{1,0:T(8,128)(2,1)S(1)} %pad_maximum_fusion.2.refs_0_), channel_id=1, source_target_pairs={{0,2},{1,3},{2,0},{3,1},{4,6},{5,7},{6,4},{7,5},{8,10},{9,11},{10,... | collective-permute-start | bytes 3538952 | tf_op jit(solution)/shard_map/ppermute | solution.py:892
  5.2 54.4 %collective-permute-start = (bf16[768,768]{1,0:T(8,128)(2,1)S(1)}, bf16[768,768]{1,0:T(8,128)(2,1)}, u32[]{:S(2)}, u32[]{:S(2)}) collective-permute-start(bf16[768,768]{1,0:T(8,128)(2,1)S(1)} %pad_maximum_fusion.2.refs_0_), channel_id=1, source_target_pairs={{0,1},{1,0},{2,3},{3,2},{4,5},{5,4},{6,7},{7,6},{8,9},{9,8},{10,11... | collective-permute-start | bytes 3538952 | tf_op jit(solution)/shard_map/ppermute | solution.py:892
  5.2 1.4 copy-start.30
  5.2 1.5 copy-start.27
  5.2 1.6 copy-start.28
  5.2 1.5 copy-start.29
  5.2 54.7 %copy-start.11 = (bf16[2,1024,192]{1,2,0:T(8,128)(2,1)S(1)}, bf16[2,1024,192]{1,2,0:T(8,128)(2,1)}, u32[]{:S(2)}) copy-start(bf16[2,1024,192]{1,2,0:T(8,128)(2,1)} %param.43) | copy-start | bytes 2359300
  6.3 54.0 %copy-start.3 = (bf16[4,768,192]{1,2,0:T(8,128)(2,1)S(1)}, bf16[4,768,192]{1,2,0:T(8,128)(2,1)}, u32[]{:S(2)}) copy-start(bf16[4,768,192]{1,2,0:T(8,128)(2,1)} %param.39) | copy-start | bytes 3538948
  6.3 55.4 %collective-permute-start.13 = (bf16[768,768]{1,0:T(8,128)(2,1)}, bf16[768,768]{1,0:T(8,128)(2,1)}, u32[]{:S(2)}, u32[]{:S(2)}) collective-permute-start(bf16[768,768]{1,0:T(8,128)(2,1)} %pad_maximum_fusion.3.refs_0_), channel_id=1, source_target_pairs={{0,2},{1,3},{2,0},{3,1},{4,6},{5,7},{6,4},{7,5},{8,10},{9,11},{10,... | collective-permute-start | bytes 3538952 | tf_op jit(solution)/shard_map/ppermute | solution.py:892
  6.7 49.9 %collective-permute-start.4 = (bf16[1,2688]{1,0:T(2,128)(2,1)S(1)}, bf16[1,2688]{1,0:T(2,128)(2,1)S(1)}, u32[]{:S(2)}, u32[]{:S(2)}) collective-permute-start(bf16[1,2688]{1,0:T(2,128)(2,1)S(1)} %broadcast_in_dim.6), channel_id=1, source_target_pairs={{0,2},{1,3},{2,0},{3,1},{4,6},{5,7},{6,4},{7,5},{8,10},{9,11},{10,... | collective-permute-start | bytes 16136 | tf_op jit(solution)/shard_map/ppermute | solution.py:892
  8.6 48.0 %collective-permute-start.3 = (bf16[1,2688]{1,0:T(2,128)(2,1)S(1)}, bf16[1,2688]{1,0:T(2,128)(2,1)S(1)}, u32[]{:S(2)}, u32[]{:S(2)}) collective-permute-start(bf16[1,2688]{1,0:T(2,128)(2,1)S(1)} %broadcast_in_dim.6), channel_id=1, source_target_pairs={{0,1},{1,0},{2,3},{3,2},{4,5},{5,4},{6,7},{7,6},{8,9},{9,8},{10,11... | collective-permute-start | bytes 16136 | tf_op jit(solution)/shard_map/ppermute | solution.py:892
  56.6 1.2 collective-permute-start.5
  56.6 6.8 %collective-permute-start.12 = (bf16[768,768]{1,0:T(8,128)(2,1)}, bf16[768,768]{1,0:T(8,128)(2,1)}, u32[]{:S(2)}, u32[]{:S(2)}) collective-permute-start(bf16[768,768]{1,0:T(8,128)(2,1)} %pad_maximum_fusion.3.refs_0_), channel_id=1, source_target_pairs={{0,1},{1,0},{2,3},{3,2},{4,5},{5,4},{6,7},{7,6},{8,9},{9,8},{10,11... | collective-permute-start | bytes 3538952 | tf_op jit(solution)/shard_map/ppermute | solution.py:892
  57.8 29.1 %collective-permute-start.7 = (bf16[768,768]{1,0:T(8,128)(2,1)}, bf16[768,768]{1,0:T(8,128)(2,1)}, u32[]{:S(2)}, u32[]{:S(2)}) collective-permute-start(bf16[768,768]{1,0:T(8,128)(2,1)} %refs_4_.5), channel_id=1, source_target_pairs={{0,2},{1,3},{2,0},{3,1},{4,6},{5,7},{6,4},{7,5},{8,10},{9,11},{10,... | collective-permute-start | bytes 3538952 | tf_op jit(solution)/shard_map/ppermute | solution.py:892
  59.6 29.1 %collective-permute-start.6 = (bf16[768,768]{1,0:T(8,128)(2,1)}, bf16[768,768]{1,0:T(8,128)(2,1)}, u32[]{:S(2)}, u32[]{:S(2)}) collective-permute-start(bf16[768,768]{1,0:T(8,128)(2,1)} %refs_4_.5), channel_id=1, source_target_pairs={{0,1},{1,0},{2,3},{3,2},{4,5},{5,4},{6,7},{7,6},{8,9},{9,8},{10,11... | collective-permute-start | bytes 3538952 | tf_op jit(solution)/shard_map/ppermute | solution.py:892
  59.6 52.7 %collective-permute-start.10 = (bf16[768,768]{1,0:T(8,128)(2,1)}, bf16[768,768]{1,0:T(8,128)(2,1)}, u32[]{:S(2)}, u32[]{:S(2)}) collective-permute-start(bf16[768,768]{1,0:T(8,128)(2,1)} %refs_8_.1), channel_id=1, source_target_pairs={{0,2},{1,3},{2,0},{3,1},{4,6},{5,7},{6,4},{7,5},{8,10},{9,11},{10,... | collective-permute-start | bytes 3538952 | tf_op jit(solution)/shard_map/ppermute | solution.py:892
  60.3 51.9 %copy-start.22 = (bf16[2,768]{1,0:T(2,128)(2,1)S(1)}, bf16[2,768]{1,0:T(2,128)(2,1)}, u32[]{:S(2)}) copy-start(bf16[2,768]{1,0:T(2,128)(2,1)} %param.38) | copy-start | bytes 9220
  60.3 51.9 %copy-start.23 = (bf16[2,768]{1,0:T(2,128)(2,1)S(1)}, bf16[2,768]{1,0:T(2,128)(2,1)}, u32[]{:S(2)}) copy-start(bf16[2,768]{1,0:T(2,128)(2,1)} %param.36) | copy-start | bytes 9220
  60.4 51.9 %copy-start.24 = (bf16[2,768]{1,0:T(2,128)(2,1)S(1)}, bf16[2,768]{1,0:T(2,128)(2,1)}, u32[]{:S(2)}) copy-start(bf16[2,768]{1,0:T(2,128)(2,1)} %param.37) | copy-start | bytes 9220
  60.4 52.5 %copy-start.13 = (bf16[3,768]{1,0:T(4,128)(2,1)S(1)}, bf16[3,768]{1,0:T(4,128)(2,1)}, u32[]{:S(2)}) copy-start(bf16[3,768]{1,0:T(4,128)(2,1)} %param.49) | copy-start | bytes 13828
  60.4 132.2 %copy-start.14 = (bf16[3,768]{1,0:T(4,128)(2,1)S(1)}, bf16[3,768]{1,0:T(4,128)(2,1)}, u32[]{:S(2)}) copy-start(bf16[3,768]{1,0:T(4,128)(2,1)} %param.47) | copy-start | bytes 13828
  60.4 132.2 %copy-start.15 = (bf16[3,768]{1,0:T(4,128)(2,1)S(1)}, bf16[3,768]{1,0:T(4,128)(2,1)}, u32[]{:S(2)}) copy-start(bf16[3,768]{1,0:T(4,128)(2,1)} %param.48) | copy-start | bytes 13828
  60.4 135.1 %copy-start.5 = (bf16[8,145,1024]{2,0,1:T(8,128)(2,1)S(1)}, bf16[8,145,1024]{2,0,1:T(8,128)(2,1)}, u32[]{:S(2)}) copy-start(bf16[8,145,1024]{2,0,1:T(8,128)(2,1)} %param.26) | copy-start | bytes 7127044
  61.7 135.2 %copy-start.6 = (bf16[896,768]{1,0:T(8,128)(2,1)}, bf16[896,768]{1,0:T(8,128)(2,1)S(1)}, u32[]{:S(2)}) copy-start(bf16[896,768]{1,0:T(8,128)(2,1)S(1)} %pad_maximum_fusion.1.refs_0_) | copy-start | bytes 4128772
  61.7 129.8 %collective-permute-start.16 = (bf16[896,768]{1,0:T(8,128)(2,1)S(1)}, bf16[896,768]{1,0:T(8,128)(2,1)S(1)}, u32[]{:S(2)}, u32[]{:S(2)}) collective-permute-start(bf16[896,768]{1,0:T(8,128)(2,1)S(1)} %pad_maximum_fusion.1.refs_0_), channel_id=1, source_target_pairs={{0,2},{1,3},{2,0},{3,1},{4,6},{5,7},{6,4},{7,5},{8,10},{9,11},{10,... | collective-permute-start | bytes 4128776 | tf_op jit(solution)/shard_map/ppermute | solution.py:892
  63.5 49.4 %collective-permute-start.9 = (bf16[768,768]{1,0:T(8,128)(2,1)}, bf16[768,768]{1,0:T(8,128)(2,1)S(1)}, u32[]{:S(2)}, u32[]{:S(2)}) collective-permute-start(bf16[768,768]{1,0:T(8,128)(2,1)} %refs_8_.1), channel_id=1, source_target_pairs={{0,1},{1,0},{2,3},{3,2},{4,5},{5,4},{6,7},{7,6},{8,9},{9,8},{10,11... | collective-permute-start | bytes 3538952 | tf_op jit(solution)/shard_map/ppermute | solution.py:892
  86.9 80.1 %collective-permute-start.19 = (bf16[768,768]{1,0:T(8,128)(2,1)}, bf16[768,768]{1,0:T(8,128)(2,1)}, u32[]{:S(2)}, u32[]{:S(2)}) collective-permute-start(bf16[768,768]{1,0:T(8,128)(2,1)} %refs_3_.1), channel_id=1, source_target_pairs={{0,2},{1,3},{2,0},{3,1},{4,6},{5,7},{6,4},{7,5},{8,10},{9,11},{10,... | collective-permute-start | bytes 3538952 | tf_op jit(solution)/shard_map/ppermute | solution.py:892
  88.7 102.8 %collective-permute-start.22 = (bf16[768,768]{1,0:T(8,128)(2,1)}, bf16[768,768]{1,0:T(8,128)(2,1)}, u32[]{:S(2)}, u32[]{:S(2)}) collective-permute-start(bf16[768,768]{1,0:T(8,128)(2,1)} %refs_7_.1), channel_id=1, source_target_pairs={{0,2},{1,3},{2,0},{3,1},{4,6},{5,7},{6,4},{7,5},{8,10},{9,11},{10,... | collective-permute-start | bytes 3538952 | tf_op jit(solution)/shard_map/ppermute | solution.py:892
  112.2 81.7 %collective-permute-start.15 = (bf16[896,768]{1,0:T(8,128)(2,1)S(1)}, bf16[896,768]{1,0:T(8,128)(2,1)S(1)}, u32[]{:S(2)}, u32[]{:S(2)}) collective-permute-start(bf16[896,768]{1,0:T(8,128)(2,1)S(1)} %pad_maximum_fusion.1.refs_0_), channel_id=1, source_target_pairs={{0,1},{1,0},{2,3},{3,2},{4,5},{5,4},{6,7},{7,6},{8,9},{9,8},{10,11... | collective-permute-start | bytes 4128776 | tf_op jit(solution)/shard_map/ppermute | solution.py:892
  112.9 81.2 %copy-start.33 = (bf16[768,768]{1,0:T(8,128)(2,1)}, bf16[768,768]{1,0:T(8,128)(2,1)S(1)}, u32[]{:S(2)}) copy-start(bf16[768,768]{1,0:T(8,128)(2,1)S(1)} %collective-permute-done.9.refs_5_.refs_9_) | copy-start | bytes 3538948
  112.9 85.9 %collective-permute-start.2 = (bf16[768,768]{1,0:T(8,128)(2,1)}, bf16[768,768]{1,0:T(8,128)(2,1)S(1)}, u32[]{:S(2)}, u32[]{:S(2)}) collective-permute-start(bf16[768,768]{1,0:T(8,128)(2,1)} %collective-permute-done.1.refs_2_), channel_id=1, source_target_pairs={{0,1},{1,0},{2,3},{3,2},{4,5},{5,4},{6,7},{7,6},{8,9},{9,8},{10,11... | collective-permute-start | bytes 3538952 | tf_op jit(solution)/shard_map/ppermute | solution.py:892
  167.0 32.2 %collective-permute-start.14 = (bf16[768,768]{1,0:T(8,128)(2,1)}, bf16[768,768]{1,0:T(8,128)(2,1)S(1)}, u32[]{:S(2)}, u32[]{:S(2)}) collective-permute-start(bf16[768,768]{1,0:T(8,128)(2,1)} %collective-permute-done.13.refs_2_), channel_id=1, source_target_pairs={{0,1},{1,0},{2,3},{3,2},{4,5},{5,4},{6,7},{7,6},{8,9},{9,8},{10,11... | collective-permute-start | bytes 3538952 | tf_op jit(solution)/shard_map/ppermute | solution.py:892
  191.5 8.0 %collective-permute-start.8 = (bf16[768,768]{1,0:T(8,128)(2,1)}, bf16[768,768]{1,0:T(8,128)(2,1)S(1)}, u32[]{:S(2)}, u32[]{:S(2)}) collective-permute-start(bf16[768,768]{1,0:T(8,128)(2,1)} %collective-permute-done.7.refs_2_.refs_6_), channel_id=1, source_target_pairs={{0,1},{1,0},{2,3},{3,2},{4,5},{5,4},{6,7},{7,6},{8,9},{9,8},{10,11... | collective-permute-start | bytes 3538952 | tf_op jit(solution)/shard_map/ppermute | solution.py:892
  191.5 5.4 copy-start.31
  191.5 8.2 %collective-permute-start.11 = (bf16[768,768]{1,0:T(8,128)(2,1)}, bf16[768,768]{1,0:T(8,128)(2,1)S(1)}, u32[]{:S(2)}, u32[]{:S(2)}) collective-permute-start(bf16[768,768]{1,0:T(8,128)(2,1)} %collective-permute-done.10.refs_6_.refs_10_), channel_id=1, source_target_pairs={{0,1},{1,0},{2,3},{3,2},{4,5},{5,4},{6,7},{7,6},{8,9},{9,8},{10,11... | collective-permute-start | bytes 3538952 | tf_op jit(solution)/shard_map/ppermute | solution.py:892
  193.9 1.1 copy-start.32
  193.9 47.2 %collective-permute-start.17 = (bf16[896,768]{1,0:T(8,128)(2,1)S(1)}, bf16[896,768]{1,0:T(8,128)(2,1)}, u32[]{:S(2)}, u32[]{:S(2)}) collective-permute-start(bf16[896,768]{1,0:T(8,128)(2,1)S(1)} %collective-permute-done.16.refs_2_), channel_id=1, source_target_pairs={{0,1},{1,0},{2,3},{3,2},{4,5},{5,4},{6,7},{7,6},{8,9},{9,8},{10,11... | collective-permute-start | bytes 4128776 | tf_op jit(solution)/shard_map/ppermute | solution.py:892
  198.9 2.8 copy-start.34
  198.9 63.4 %collective-permute-start.18 = (bf16[768,768]{1,0:T(8,128)(2,1)}, bf16[768,768]{1,0:T(8,128)(2,1)S(1)}, u32[]{:S(2)}, u32[]{:S(2)}) collective-permute-start(bf16[768,768]{1,0:T(8,128)(2,1)} %refs_3_.1), channel_id=1, source_target_pairs={{0,1},{1,0},{2,3},{3,2},{4,5},{5,4},{6,7},{7,6},{8,9},{9,8},{10,11... | collective-permute-start | bytes 3538952 | tf_op jit(solution)/shard_map/ppermute | solution.py:892
  199.2 2.5 copy-start.37
  199.2 63.1 %collective-permute-start.21 = (bf16[768,768]{1,0:T(8,128)(2,1)}, bf16[768,768]{1,0:T(8,128)(2,1)}, u32[]{:S(2)}, u32[]{:S(2)}) collective-permute-start(bf16[768,768]{1,0:T(8,128)(2,1)} %refs_7_.1), channel_id=1, source_target_pairs={{0,1},{1,0},{2,3},{3,2},{4,5},{5,4},{6,7},{7,6},{8,9},{9,8},{10,11... | collective-permute-start | bytes 3538952 | tf_op jit(solution)/shard_map/ppermute | solution.py:892
  199.5 2.2 copy-start.35
  199.5 62.8 %collective-permute-start.20 = (bf16[768,768]{1,0:T(8,128)(2,1)}, bf16[768,768]{1,0:T(8,128)(2,1)}, u32[]{:S(2)}, u32[]{:S(2)}) collective-permute-start(bf16[768,768]{1,0:T(8,128)(2,1)} %collective-permute-done.19.refs_2_.refs_5_), channel_id=1, source_target_pairs={{0,1},{1,0},{2,3},{3,2},{4,5},{5,4},{6,7},{7,6},{8,9},{9,8},{10,11... | collective-permute-start | bytes 3538952 | tf_op jit(solution)/shard_map/ppermute | solution.py:892
  199.7 2.0 copy-start.36
  199.7 62.6 %collective-permute-start.23 = (bf16[768,768]{1,0:T(8,128)(2,1)}, bf16[768,768]{1,0:T(8,128)(2,1)}, u32[]{:S(2)}, u32[]{:S(2)}) collective-permute-start(bf16[768,768]{1,0:T(8,128)(2,1)} %collective-permute-done.22.refs_6_.refs_9_), channel_id=1, source_target_pairs={{0,1},{1,0},{2,3},{3,2},{4,5},{5,4},{6,7},{7,6},{8,9},{9,8},{10,11... | collective-permute-start | bytes 3538952 | tf_op jit(solution)/shard_map/ppermute | solution.py:892
  262.3 1.0 copy-start.38
  362.1 21.9 %copy-start.26 = (f32[2,2,2,192]{3,2,1,0:T(2,128)S(1)}, f32[2,2,2,192]{3,2,1,0:T(2,128)}, u32[]{:S(2)}) copy-start(f32[2,2,2,192]{3,2,1,0:T(2,128)} %get-tuple-element.141) | copy-start | bytes 18436
  362.1 22.0 %copy-start.25 = (f32[2,2,2,192]{3,2,1,0:T(2,128)S(1)}, f32[2,2,2,192]{3,2,1,0:T(2,128)}, u32[]{:S(2)}) copy-start(f32[2,2,2,192]{3,2,1,0:T(2,128)} %get-tuple-element.142) | copy-start | bytes 18436
  362.1 22.1 %copy-start.21 = (f32[2,2,768]{2,1,0:T(2,128)S(1)}, f32[2,2,768]{2,1,0:T(2,128)}, u32[]{:S(2)}) copy-start(f32[2,2,768]{2,1,0:T(2,128)} %get-tuple-element.143) | copy-start | bytes 36868
  362.2 22.1 %copy-start.18 = (f32[2,2,768]{2,1,0:T(2,128)S(1)}, f32[2,2,768]{2,1,0:T(2,128)}, u32[]{:S(2)}) copy-start(f32[2,2,768]{2,1,0:T(2,128)} %get-tuple-element.144) | copy-start | bytes 36868
  362.2 22.9 %copy-start.20 = (f32[3,768]{1,0:T(4,128)S(1)}, f32[3,768]{1,0:T(4,128)}, u32[]{:S(2)}) copy-start(f32[3,768]{1,0:T(4,128)} %get-tuple-element.146) | copy-start | bytes 27652
  362.2 22.9 %copy-start.19 = (f32[3,768]{1,0:T(4,128)S(1)}, f32[3,768]{1,0:T(4,128)}, u32[]{:S(2)}) copy-start(f32[3,768]{1,0:T(4,128)} %get-tuple-element.147) | copy-start | bytes 27652
  362.2 23.0 %copy-start.17 = (f32[3,768]{1,0:T(4,128)S(1)}, f32[3,768]{1,0:T(4,128)}, u32[]{:S(2)}) copy-start(f32[3,768]{1,0:T(4,128)} %get-tuple-element.148) | copy-start | bytes 27652
  362.2 23.0 %copy-start.16 = (f32[3,768]{1,0:T(4,128)S(1)}, f32[3,768]{1,0:T(4,128)}, u32[]{:S(2)}) copy-start(f32[3,768]{1,0:T(4,128)} %get-tuple-element.149) | copy-start | bytes 27652
  620.0 5.5 copy-start.2
  625.5 1.8 copy-start.1
  628.1 1.4 copy-start
  639.4 4.1 copy-start.9
  643.5 1.7 copy-start.8
  645.2 1.7 copy-start.7
  646.9 2.6 copy-start.4

commit v3 on v2

--- a/solution.py
+++ b/solution.py
@@ -888,6 +888,479 @@
     return outs[:-1], outs[-1]
 
 
+class Flow:
+    def __init__(self, net, a, lo, hi, spread):
+        rows = hi - lo
+        own, got = net.own[a], net.got[a]
+        here = pl.ds(lo, rows)
+        self.copies = []
+        self.started = self.waited = 0
+        if spread and rows % (16 * net.n_dp) == 0:
+
+            def region(count):
+                size, start = rows, lo
+                for i in range(count):
+                    size //= 2
+                    start = start + net.dp_bits[i] * size
+                return pl.ds(pl.multiple_of(start, 16), size)
+
+            part = region(net.bits)
+            self.add(net, own.at[part], got.at[1, part], net.far_peer)
+            for b in reversed(range(net.bits)):
+                part = region(b + 1)
+                self.add(net, got.at[1, part], got.at[1, part], net.dp_peers[b])
+        else:
+            self.add(net, own.at[here], got.at[1, here], net.far_peer)
+        self.add(net, got.at[1, here], got.at[2, here], net.core_peer)
+
+    def add(self, net, source, target, peer):
+        self.copies.append(net.remote(source, target, peer))
+
+    def advance(self):
+        if self.started < len(self.copies):
+            if self.started > 0:
+                self.await_copy(self.started - 1)
+            self.copies[self.started].start()
+            self.started += 1
+
+    def await_copy(self, n):
+        while self.started <= n:
+            self.advance()
+        while self.waited <= n:
+            self.copies[self.waited].wait_recv()
+            self.waited += 1
+
+    def need(self, r):
+        self.await_copy(len(self.copies) - (2 if r == 2 else 1))
+
+    def close(self):
+        self.need(3)
+        for copy in self.copies:
+            copy.wait_send()
+
+
+class Direct:
+    def __init__(self, copy):
+        self.copy, self.state = copy, 0
+
+    def advance(self):
+        if self.state == 0:
+            self.copy.start()
+            self.state = 1
+
+    def need(self):
+        self.advance()
+        if self.state == 1:
+            self.copy.wait_recv()
+            self.state = 2
+
+    def close(self):
+        self.need()
+        self.copy.wait_send()
+
+
+class Net:
+    def __init__(self, n_tensor, n_dp, own, got, send_sem, recv_sem):
+        self.n_dp, self.bits = n_dp, n_dp.bit_length() - 1
+        self.own, self.got = own, got
+        self.send_sem, self.recv_sem = send_sem, recv_sem
+        self.count = 0
+        t, d = lax.axis_index("tensor"), lax.axis_index("dp")
+        self.core_peer = {"tensor": pair(t, 1)}
+        self.far_peer = {"tensor": lax.rem(t + 2, n_tensor)}
+        self.dp_peers = [{"dp": pair(d, 1 << b)} for b in range(self.bits)]
+        self.dp_bits = [(d // (1 << b)) % 2 for b in range(self.bits)]
+        peers = [self.core_peer, self.far_peer] + self.dp_peers
+        barrier = pltpu.get_barrier_semaphore()
+        for peer in peers:
+            pl.semaphore_signal(
+                barrier, inc=1, device_id=peer, device_id_type=pl.DeviceIdType.MESH
+            )
+        pl.semaphore_wait(barrier, len(peers))
+
+    def remote(self, source, target, peer):
+        n = self.count
+        self.count += 1
+        return pltpu.make_async_remote_copy(
+            src_ref=source,
+            dst_ref=target,
+            send_sem=self.send_sem.at[n],
+            recv_sem=self.recv_sem.at[n],
+            device_id=peer,
+            device_id_type=pl.DeviceIdType.MESH,
+        )
+
+
+ONE, EXPAND_ONE, CONTRACT_ONE, TWO, CROSS, EXPAND_TWO, CONTRACT_TWO = range(7)
+
+
+def forward_kernel(sizes, *refs):
+    n_tensor, n_dp, items, slots, patches, padded, width = sizes
+    refs = list(refs)
+
+    def take(n):
+        got, refs[:n] = refs[:n], []
+        return got
+
+    own = take(7)
+    bias_own, lengths, x, pf, vecs = take(5)
+    got = take(7)
+    text_out, join_out, e_out = take(3)
+    self_out = [take(5), take(5)]
+    cross_out = take(5)
+    feed_out = [take(2), take(2)]
+    ws, wf, wc, acc, u, ub, e_s = take(7)
+    q_st, k_st, v_st, a_st, p_st = self_st = take(5)
+    cross_st = take(5)
+    qc_st, kc_st, vc_st, ac_st, pc_st = cross_st
+    h_st, slope_st = feed_st = take(2)
+    q_s, k_s, v_s, a_s, bias = take(5)
+    send_sem, recv_sem, fetch_sem, store_sem = take(4)
+    model = x.shape[1]
+    hidden = own[EXPAND_ONE].shape[1]
+
+    net = Net(n_tensor, n_dp, own, got, send_sem, recv_sem)
+    middle = 2 * width
+    flows = {
+        "s1a": Flow(net, ONE, 0, middle, False),
+        "s1b": Flow(net, ONE, middle, 2 * middle, True),
+        "e1": Flow(net, EXPAND_ONE, 0, model, True),
+        "k1": Flow(net, CONTRACT_ONE, 0, hidden, True),
+        "s2a": Flow(net, TWO, middle, 2 * middle, False),
+        "s2b": Flow(net, TWO, 0, middle, True),
+        "ckv": Flow(net, CROSS, middle, own[CROSS].shape[0], False),
+        "cqo": Flow(net, CROSS, 0, middle, False),
+        "e2": Flow(net, EXPAND_TWO, 0, model, True),
+        "k2": Flow(net, CONTRACT_TWO, 0, hidden, True),
+    }
+    parts = {
+        ONE: ("s1a", "s1b"),
+        EXPAND_ONE: ("e1",),
+        CONTRACT_ONE: ("k1",),
+        TWO: ("s2a", "s2b"),
+        EXPAND_TWO: ("e2",),
+        CONTRACT_TWO: ("k2",),
+    }
+    near = [Direct(net.remote(own[a], got[a].at[0], net.core_peer)) for a in range(7)]
+    bias_near = Direct(net.remote(bias_own, bias.at[1], net.core_peer))
+    bias_far = Direct(net.remote(bias_own, bias.at[2], net.far_peer))
+    bias_last = Direct(net.remote(bias.at[2], bias.at[3], net.core_peer))
+
+    def move(names):
+        for name in names.split():
+            flows[name].advance()
+
+    fetches = {}
+
+    def fetch(key, a, r, target, lo=0, hi=None, names=None):
+        if key in fetches:
+            return
+        hi = own[a].shape[0] if hi is None else hi
+        if r == 1:
+            near[a].need()
+        elif r > 1:
+            for name in names or parts[a]:
+                flows[name].need(r)
+        source = own[a] if r == 0 else got[a].at[r - 1]
+        copy = pltpu.make_async_copy(
+            source.at[pl.ds(lo, hi - lo)], target, fetch_sem.at[len(fetches)]
+        )
+        copy.start()
+        fetches[key] = copy
+
+    stores = []
+
+    def store(source, target):
+        copy = pltpu.make_async_copy(source, target, store_sem.at[len(stores)])
+        copy.start()
+        stores.append(copy)
+        return len(stores) - 1
+
+    masks = head_masks(width)
+    pending = {"self": [], "feed": []}
+
+    def settle(kind):
+        for n in pending[kind]:
+            stores[n].wait()
+            stores[n] = None
+        pending[kind] = []
+
+    def close_layer(n, target=None):
+        e = acc[...]
+        e_s[n] = e
+        store(e_s.at[n], e_out.at[n])
+        y = norm_forward(e, vecs[n, 1:2], vecs[n, 2:3])
+        if target is not None:
+            yb = y.astype(BF)
+            target[...] = yb
+            ub[...] = yb
+            u[...] = yb.astype(F32)
+        else:
+            u[...] = y
+            ub[...] = y.astype(BF)
+
+    def open_layer(n):
+        acc[...] = u[...] + vecs[n, 0:1]
+
+    def fetch_self(layer, r):
+        a = (ONE, TWO)[layer]
+        fetch(("self", layer, r), a, r, ws.at[r])
+
+    def self_unit(layer, r):
+        fetch_self(layer, r)
+        fetches["self", layer, r].wait()
+        xb = ub[...]
+        q = (
+            dot_nt(xb, ws[r, 0:width]) + bias[r, 2 * layer : 2 * layer + 1, 0:width]
+        ).astype(BF)
+        k = dot_nt(xb, ws[r, width : 2 * width]).astype(BF)
+        v = (
+            dot_nt(xb, ws[r, 2 * width : 3 * width])
+            + bias[r, 2 * layer + 1 : 2 * layer + 2, 0:width]
+        ).astype(BF)
+        q_st[r], k_st[r], v_st[r] = q, k, v
+        q_s[...], k_s[...], v_s[...] = q.astype(F32), k.astype(F32), v.astype(F32)
+        for i in range(items):
+            rows = pl.ds(i * slots, slots)
+            probs, a = item_forward(
+                q_s[rows], k_s[rows].astype(BF), v_s[rows].astype(BF), masks, lengths[i]
+            )
+            p_st[r, i] = probs
+            a_s[rows] = a
+        ab = a_s[...].astype(BF)
+        a_st[r] = ab
+        acc[...] += dot_nn(ab, ws[r, 3 * width : 4 * width])
+
+    def self_close(layer):
+        for source, target in zip(self_st, self_out[layer]):
+            pending["self"].append(store(source, target))
+
+    def fetch_feed(layer, r):
+        a, b = ((EXPAND_ONE, CONTRACT_ONE), (EXPAND_TWO, CONTRACT_TWO))[layer]
+        fetch(("expand", layer, r), a, r, wf.at[r, 0])
+        fetch(("contract", layer, r), b, r, wf.at[r, 1])
+
+    def feed_unit(layer, r):
+        fetch_feed(layer, r)
+        fetches["expand", layer, r].wait()
+        z = dot_nn(ub[...], wf[r, 0]) + bias[r, 6 + layer : 7 + layer, 0:hidden]
+        cdf = 0.5 * (1.0 + lax.erf(z * 0.7071067811865476))
+        slope = cdf + z * (jnp.exp(-0.5 * z * z) * 0.3989422804014327)
+        h = (z * cdf).astype(BF)
+        h_st[r] = h
+        slope_st[r] = slope.astype(BF)
+        fetches["contract", layer, r].wait()
+        acc[...] += dot_nn(h, wf[r, 1])
+
+    def feed_close(layer):
+        for source, target in zip(feed_st, feed_out[layer]):
+            pending["feed"].append(store(source, target))
+
+    tail = own[CROSS].shape[0] - middle
+
+    def fetch_keys(r):
+        fetch(
+            ("keys", r), CROSS, r, wc.at[r, pl.ds(middle, tail)], middle, middle + tail, ("ckv",)
+        )
+
+    def keys_unit(r):
+        fetch_keys(r)
+        fetches["keys", r].wait()
+        low, high = key_value_weight(wc, r, middle, width, model)
+        chunk = 2 * padded
+        for m in range(items // 2):
+            rows = slice(m * chunk, (m + 1) * chunk)
+            left, right = pf[rows, 0:model], pf[rows, model:]
+            kc_st[r, rows] = (
+                dot_nt(left, low[0:width]) + dot_nt(right, high[0:width])
+            ).astype(BF)
+            vc_st[r, rows] = (
+                dot_nt(left, low[width:]) + dot_nt(right, high[width:]) + bias[r, 5:6, 0:width]
+            ).astype(BF)
+
+    def fetch_cross(r):
+        fetch(("cross", r), CROSS, r, wc.at[r, pl.ds(0, middle)], 0, middle, ("cqo",))
+
+    def cross_unit(r):
+        fetch_cross(r)
+        fetches["cross", r].wait()
+        q = (dot_nt(ub[...], wc[r, 0:width]) + bias[r, 4:5, 0:width]).astype(BF)
+        qc_st[r] = q
+        q_s[...] = q.astype(F32)
+        for i in range(items):
+            rows = pl.ds(i * slots, slots)
+            keys = pl.ds(i * padded, padded)
+            probs, a = item_forward(q_s[rows], kc_st[r, keys], vc_st[r, keys], masks, patches)
+            pc_st[r, i] = probs
+            a_s[rows] = a
+        ab = a_s[...].astype(BF)
+        ac_st[r] = ab
+        acc[...] += dot_nn(ab, wc[r, width:middle])
+
+    move("s1b e1 s1a")
+    near[ONE].advance()
+    bias_near.advance()
+    bias_far.advance()
+    near[CROSS].advance()
+    fetch_self(0, 0)
+    fetch_keys(0)
+    bias[0] = bias_own[...]
+    u[...] = x[...].astype(F32)
+    ub[...] = x[...]
+    open_layer(0)
+    self_unit(0, 0)
+    move("s1b e1 k1")
+    bias_near.need()
+    fetch_self(0, 1)
+    self_unit(0, 1)
+    move("s1b")
+    keys_unit(0)
+    move("e1 s1b k1")
+    bias_far.need()
+    bias_last.advance()
+    near[EXPAND_ONE].advance()
+    near[CONTRACT_ONE].advance()
+    fetch_keys(1)
+    keys_unit(1)
+    move("s1a ckv e1 k1 s2b")
+    bias_last.need()
+    move("s1b")
+    fetch_self(0, 2)
+    fetch_self(0, 3)
+    self_unit(0, 2)
+    fetch_feed(0, 0)
+    self_unit(0, 3)
+    self_close(0)
+    close_layer(0)
+    open_layer(1)
+    move("e1 k1 s2b s2a")
+    near[TWO].advance()
+    move("ckv")
+    fetch_feed(0, 1)
+    fetch_keys(2)
+    fetch_keys(3)
+    keys_unit(2)
+    move("e2 k2 s2b")
+    keys_unit(3)
+    for source, target in zip(cross_st[1:3], cross_out[1:3]):
+        store(source, target)
+    move("k1")
+    feed_unit(0, 0)
+    fetch_feed(0, 2)
+    feed_unit(0, 1)
+    move("e2")
+    fetch_feed(0, 3)
+    feed_unit(0, 2)
+    fetch_self(1, 0)
+    feed_unit(0, 3)
+    feed_close(0)
+    close_layer(1, text_out)
+    open_layer(2)
+    settle("self")
+    move("s2b s2a e2 k2 cqo")
+    near[EXPAND_TWO].advance()
+    near[CONTRACT_TWO].advance()
+    fetch_self(1, 1)
+    self_unit(1, 0)
+    fetch_self(1, 2)
+    self_unit(1, 1)
+    move("e2 k2")
+    fetch_self(1, 3)
+    self_unit(1, 2)
+    fetch_cross(0)
+    self_unit(1, 3)
+    self_close(1)
+    close_layer(2)
+    open_layer(3)
+    move("cqo k2")
+    fetch_cross(1)
+    fetch_feed(1, 0)
+    cross_unit(0)
+    move("e2")
+    fetch_cross(2)
+    cross_unit(1)
+    fetch_cross(3)
+    cross_unit(2)
+    move("k2")
+    fetch_feed(1, 1)
+    cross_unit(3)
+    for n in (0, 3, 4):
+        store(cross_st[n], cross_out[n])
+    close_layer(3)
+    open_layer(4)
+    settle("feed")
+    move("e2 k2")
+    fetch_feed(1, 2)
+    feed_unit(1, 0)
+    feed_unit(1, 1)
+    fetch_feed(1, 3)
+    feed_unit(1, 2)
+    feed_unit(1, 3)
+    feed_close(1)
+    close_layer(4, join_out)
+
+    for copy in stores:
+        if copy is not None:
+            copy.wait()
+    for flow in flows.values():
+        flow.close()
+    for direct in near + [bias_near, bias_far, bias_last]:
+        direct.close()
+
+
+def forward_all(links, own, bias, lengths, x, pf, vecs, patches, width):
+    items = lengths.shape[0]
+    rows, model = x.shape
+    slots, padded = rows // items, pf.shape[0] // items
+    hidden = own[EXPAND_ONE].shape[1]
+    heads = width // HEAD_DIM
+    anywhere = pl.BlockSpec(memory_space=ANY)
+    vmem = pl.BlockSpec(memory_space=pltpu.VMEM)
+    sizes = (links.tensor, links.dp, items, slots, patches, padded, width)
+    mid = ((4, rows, width), BF)
+    key = ((4, pf.shape[0], width), BF)
+    probs = ((4, items, heads * slots, slots), BF)
+    cross_probs = ((4, items, heads * slots, padded), BF)
+    feed = ((4, rows, hidden), BF)
+    self_kept = [mid] * 4 + [probs]
+    cross_kept = [mid, key, key, mid, cross_probs]
+    kept = self_kept * 2 + cross_kept + [feed] * 4
+    outputs = [((3,) + a.shape, BF) for a in own]
+    outputs += [((rows, model), BF)] * 2 + [((5, rows, model), F32)] + kept
+    remotes = 10 * (2 + links.bits) + 10
+    outs = pl.pallas_call(
+        functools.partial(forward_kernel, sizes),
+        in_specs=[anywhere] * 7
+        + [vmem, pl.BlockSpec(memory_space=pltpu.SMEM), vmem, vmem, vmem],
+        out_specs=[anywhere] * 7 + [vmem] * 2 + [anywhere] * (1 + len(kept)),
+        out_shape=[jax.ShapeDtypeStruct(shape, dtype) for shape, dtype in outputs],
+        scratch_shapes=[
+            pltpu.VMEM((4, 4 * width, model), BF),
+            pltpu.VMEM((4, 2, model, hidden), BF),
+            pltpu.VMEM((4,) + own[CROSS].shape, BF),
+            pltpu.VMEM((rows, model), F32),
+            pltpu.VMEM((rows, model), F32),
+            pltpu.VMEM((rows, model), BF),
+            pltpu.VMEM((5, rows, model), F32),
+        ]
+        + [pltpu.VMEM(*item) for item in self_kept + cross_kept + [feed] * 2]
+        + [pltpu.VMEM((rows, width), F32)] * 4
+        + [
+            pltpu.VMEM((4, 8, model), F32),
+            pltpu.SemaphoreType.DMA((remotes,)),
+            pltpu.SemaphoreType.DMA((remotes,)),
+            pltpu.SemaphoreType.DMA((40,)),
+            pltpu.SemaphoreType.DMA((32,)),
+        ],
+        compiler_params=pltpu.CompilerParams(
+            collective_id=1, has_side_effects=True, vmem_limit_bytes=60 * 1024 * 1024
+        ),
+        name="forward_and_gather",
+    )(*own, bias, lengths, x, pf, vecs)
+    got, (text_out, join_out, e), kept = outs[:7], outs[7:10], outs[10:]
+    return got, text_out, join_out, e, kept[0:5], kept[5:10], kept[10:15], kept[15:17], kept[17:19]
+
+
 def swap(array, axis, size, distance):
     return lax.ppermute(array, axis, [(i, i ^ distance) for i in range(size)])
 
@@ -911,6 +1384,10 @@
     def gather(self, own):
         across = self.far(own)
         return own, self.core(own), across, self.core(across)
+
+
+def layer_norm(e, vec):
+    return norm_forward(e, vec[1:2], vec[2:3])
 
 
 def flat(array):
@@ -989,30 +1466,24 @@
     width = text_project_in.shape[2]
     hidden = text_expand.shape[1]
 
+    own = [
+        self_pack(text_project_in, text_project_out),
+        text_expand,
+        text_contract,
+        self_pack(join_project_in[0:3], join_project_out),
+        cross_pack(join_project_in[3], cross_project_out, cross_key_value),
+        join_expand,
+        join_contract,
+    ]
+    biases = jnp.concatenate([text_project_bias, join_project_bias], axis=0)
     biases = jnp.concatenate(
         [
-            flat(text_project_bias),
-            flat(join_project_bias),
-            text_expand_bias,
-            join_expand_bias,
-        ]
-    )[None]
-    weights_one = links.gather(self_pack(text_project_in, text_project_out))
-    biases = jnp.concatenate(links.gather(biases), axis=0).astype(F32)
-    expand_one = links.gather(text_expand)
-    contract_one = links.gather(text_contract)
-    weights_two = links.gather(self_pack(join_project_in[0:3], join_project_out))
-    weights_cross = links.gather(
-        cross_pack(join_project_in[3], cross_project_out, cross_key_value)
-    )
-    expand_two = links.gather(join_expand)
-    contract_two = links.gather(join_contract)
-
-    bias_one = biases[:, : 2 * width].reshape(4, 2, width)
-    bias_two = biases[:, 2 * width : 4 * width].reshape(4, 2, width)
-    bias_cross = biases[:, 4 * width : 6 * width].reshape(4, 2, width)
-    hidden_one = biases[:, 6 * width : 6 * width + hidden].reshape(4, 1, hidden)
-    hidden_two = biases[:, 6 * width + hidden :].reshape(4, 1, hidden)
+            jnp.pad(biases, ((0, 0), (0, hidden - width))),
+            text_expand_bias[None],
+            join_expand_bias[None],
+        ],
+        axis=0,
+    ).astype(F32)
 
     def vec(bias, gain, shift, n):
         return jnp.stack([bias[n], gain[n], shift[n]]).astype(F32)
@@ -1027,34 +1498,34 @@
     text_cot = text_cotangent.reshape(items * slots, model)
     join_cot = join_cotangent.reshape(items * slots, model)
 
-    h1, saved_one = self_forward(lengths, x, weights_one, bias_one, text_vecs[0], "text_self_forward")
-    text_out, saved_two = feed_forward(
-        h1, expand_one, contract_one, hidden_one, text_vecs[1], "text_feed_forward"
-    )
-    h2, saved_three = self_forward(
-        lengths, text_out, weights_two, bias_two, join_vecs[0], "join_self_forward"
-    )
-    h3, saved_four = cross_forward(
-        h2, pf, patches, items, weights_cross, bias_cross, join_vecs[1], "cross_forward"
-    )
-    join_out, saved_five = feed_forward(
-        h3, expand_two, contract_two, hidden_two, join_vecs[2], "join_feed_forward"
-    )
+    vecs = jnp.stack(text_vecs + join_vecs)
+    got, text_out, join_out, e, kept_one, kept_two, kept_cross, feed_one, feed_two = forward_all(
+        links, own, biases, lengths, x, pf, vecs, patches, width
+    )
+    weights = [[own[a]] + [got[a][r] for r in range(3)] for a in range(7)]
+    h1 = layer_norm(e[0], text_vecs[0])
+    h2 = layer_norm(e[2], join_vecs[0])
+    h3 = layer_norm(e[3], join_vecs[1])
+    saved_one = (x, e[0], *kept_one[:3], kept_one[4], kept_one[3])
+    saved_two = (h1, e[1], *feed_one)
+    saved_three = (text_out, e[2], *kept_two[:3], kept_two[4], kept_two[3])
+    saved_four = (h2, e[3], *kept_cross[:3], kept_cross[4], kept_cross[3])
+    saved_five = (h3, e[4], *feed_two)
 
     du, e2k, e2s, k2k, k2s, dc_two, sums_five = feed_backward(
-        links, None, join_cot, saved_five, expand_two, contract_two, join_vecs[2], "join_feed_backward"
+        links, None, join_cot, saved_five, weights[EXPAND_TWO], weights[CONTRACT_TWO], join_vecs[2], "join_feed_backward"
     )
     du, grad_patches, ck, cs, db_cross, sums_four = cross_backward(
-        links, du, saved_four, pf, patches, items, weights_cross, join_vecs[1], "cross_backward"
+        links, du, saved_four, pf, patches, items, weights[CROSS], join_vecs[1], "cross_backward"
     )
     du, s2k, s2s, db_two, sums_three = self_backward(
-        links, du, saved_three, items, weights_two, join_vecs[0], F32, "join_self_backward"
+        links, du, saved_three, items, weights[TWO], join_vecs[0], F32, "join_self_backward"
     )
     du, e1k, e1s, k1k, k1s, dc_one, sums_two = feed_backward(
-        links, du, text_cot, saved_two, expand_one, contract_one, text_vecs[1], "text_feed_backward"
+        links, du, text_cot, saved_two, weights[EXPAND_ONE], weights[CONTRACT_ONE], text_vecs[1], "text_feed_backward"
     )
     grad_text, s1k, s1s, db_one, sums_one = self_backward(
-        links, du, saved_one, items, weights_one, text_vecs[0], BF, "text_self_backward"
+        links, du, saved_one, items, weights[ONE], text_vecs[0], BF, "text_self_backward"
     )
 
     blocks = jnp.concatenate(

time: 660 us -> 541 us (0.82)
  waiting for transfers between devices: 173 us -> 0 us
  Pallas kernels: 412 us -> 462 us
  starting transfers between devices: 14 us -> 0 us
  local copies, waits for them, and re-layouts: 33.9 us -> 44 us
    ppermute x24 -> x0, waiting for transfers between devices: 173 us -> none  [swap(): return lax.ppermute(array, axis, [(i, i ^ distance) for i in range(size)])]
    pallas_call x0 -> x1, Pallas kernels: none -> 121 us  [forward_all(): pl.pallas_call(functools.partial(forward_kernel, sizes), in_specs=[anywhe...]
    pallas_call x10 -> x5, Pallas kernels: 178 us -> 111 us  [call(): pl.pallas_call(kernel, grid=(2,), in_specs=[kinds[kind](a.shape) for a, k...]
    ppermute x24 -> x0, starting transfers between devices: 14 us -> none  [swap(): return lax.ppermute(array, axis, [(i, i ^ distance) for i in range(size)])]
    squeeze x0 -> x4, local copies, waits for them, and re-layouts: none -> 11 us  [per_device(): weights = [[own[a]] + [got[a][r] for r in range(3)] for a in range(7)]]
    unnamed x94 -> x100, local copies, waits for them, and re-layouts: 13.3 us -> 15 us
  transfers between devices with their start and end apart: 24 -> 0, of which waited for: 6 -> 0; matrix products, arithmetic and copies ran while one was open for 2% -> 0% of each run, Pallas kernels for 9% -> 0%
where the time goes in v3:
time: 541 us; the launch traced here: 532 us
  Pallas kernels  462 us (85%)
  local copies, waits for them, and re-layouts  44 us (8%)
  other arithmetic  24.4 us (5%)
    pallas_call x1, Pallas kernels, reduce_all(): pl.pallas_call(functools.partial(reduce_kernel, links.tensor, links.dp, c...  230 us
    pallas_call x1, Pallas kernels, forward_all(): pl.pallas_call(functools.partial(forward_kernel, sizes), in_specs=[anywhe...  121 us
    pallas_call x5, Pallas kernels, call(): pl.pallas_call(kernel, grid=(2,), in_specs=[kinds[kind](a.shape) for a, k...  111 us
    unnamed x100, local copies, waits for them, and re-layouts  15 us
    squeeze x4, local copies, waits for them, and re-layouts, per_device(): weights = [[own[a]] + [got[a][r] for r in range(3)] for a in range(7)]  11 us

profile of v3, /device:TPU:0, one launch (start us, length us, event | category | flops | bytes accessed | tf_op | source)
XLA Modules:
  0.0 532.0 jit_solution(11167070207069826456)
XLA Ops:
  0.7 0.8 fusion.8
  1.5 0.8 fusion.9
  2.3 0.8 fusion.10
  3.1 0.8 fusion.5
  4.0 0.8 fusion.6
  4.8 0.8 fusion.7
  5.7 0.6 stack.104.refs_11_
  6.3 0.9 slice.349
  7.3 0.2 copy.67
  7.7 1.2 pad_maximum_fusion.1.refs_4_.refs_0_
  8.9 0.9 copy-done.11
  9.8 1.3 copy.82
  11.2 1.8 pad.17.clone
  13.0 1.2 slice-done.2
  14.2 1.1 pad_maximum_fusion.3.refs_3_.refs_0_
  15.3 1.1 pad_maximum_fusion.2.refs_0_
  16.5 0.6 maximum_convert_fusion.refs_7_
  17.1 121.0 %forward_and_gather.1 = (bf16[3,768,768]{2,1,0:T(8,128)(2,1)}, bf16[3,768,768]{2,1,0:T(8,128)(2,1)}, bf16[3,768,768]{2,1,0:T(8,128)(2,1)}, bf16[3,768,768]{2,1,0...) custom-call(bf16[768,768]{1,0:T(8,128)(2,1)} %pad_maximum_fusion.2.r, ...), custom_call_target="tpu_custom_call" | custom-call | tf_op jit(solution)/shard_map/forward_and_gather/pallas_call | solution.py:1331
  138.1 5.0 slice_reduce_fusion
  143.2 0.5 multiply_reduce_fusion
  143.7 0.6 maximum_convert_fusion.1
  144.4 0.6 maximum_convert_fusion.4
  145.1 2.7 multiply_add_fusion
  147.9 3.0 slice_bitcast_fusion.15
  150.9 17.1 %join_feed_backward.1 = (f32[320,768]{1,0:T(8,128)}, bf16[2,768,768]{2,1,0:T(8,128)(2,1)}, bf16[2,768,768]{2,1,0:T(8,128)(2,1)}, bf16[2,768,768]{2,1,0:T(8,128)(...) custom-call(bf16[320,768]{1,0:T(8,128)(2,1)} %bitcast.202, ...), custom_call_target="tpu_custom_call" | custom-call | flops 6039797760 | bytes 26277888 | tf_op jit(solution)/shard_map/join_feed_backward/pallas_call | solution.py:432
  168.0 2.1 slice_bitcast_fusion
  170.1 33.6 %cross_backward.1 = (f32[320,768]{1,0:T(8,128)}, bf16[8,145,1024]{2,1,0:T(8,128)(2,1)}, bf16[2,1024,768]{2,1,0:T(8,128)(2,1)}, bf16[2,1024,768]{2,1,0:T(8,128)(2...) custom-call(f32[320,768]{1,0:T(8,128)} %get-tuple-element.98.dy, f32[320,768]{1,0:T(8,128)} %get-tuple-element.248.e_in, ...), custom_call_target="tpu_custom_call" | custom-call | flops 9563013120 | bytes 26894336 | tf_op jit(solution)/shard_map/cross_backward/pallas_call | solution.py:432
  203.7 3.0 slice_bitcast_fusion.9
  206.7 22.0 %join_self_backward.1 = (f32[320,768]{1,0:T(8,128)}, bf16[2,768,768]{2,1,0:T(8,128)(2,1)}, bf16[2,768,768]{2,1,0:T(8,128)(2,1)}, f32[2,2,2,192]{3,2,1,0:T(2,128)}, f32[3,768]{1,0:T(4,128)}) custom-call(f32[320,768]{1,0:T(8,128)} %get-tuple-element.105.dy, f32[320,768]{1,0:T(8,128)} %get-tuple-element.247.e_in, bf16[320,768]{1,0:T(8,128)(2,1)} %get-tuple-element.91.x, ...), custom_call_target="tpu_custom_call" | custom-call | flops 3019898880 | bytes 15175680 | tf_op jit(solution)/shard_map/join_self_backward/pallas_call | solution.py:432
  228.8 2.9 slice_bitcast_fusion.3
  231.7 17.2 %text_feed_backward.1 = (f32[320,768]{1,0:T(8,128)}, bf16[2,768,768]{2,1,0:T(8,128)(2,1)}, bf16[2,768,768]{2,1,0:T(8,128)(2,1)}, bf16[2,768,768]{2,1,0:T(8,128)(...) custom-call(f32[320,768]{1,0:T(8,128)} %get-tuple-element.112.refs_0_, ...), custom_call_target="tpu_custom_call" | custom-call | flops 6039797760 | bytes 27260928 | tf_op jit(solution)/shard_map/text_feed_backward/pallas_call | solution.py:432
  249.0 21.0 %text_self_backward.1 = (bf16[320,768]{1,0:T(8,128)(2,1)}, bf16[2,768,768]{2,1,0:T(8,128)(2,1)}, bf16[2,768,768]{2,1,0:T(8,128)(2,1)}, f32[2,2,2,192]{3,2,1,0:T(2,128)}, f32[3,768]{1,0:T(4,128)}) custom-call(f32[320,768]{1,0:T(8,128)} %get-tuple-element.117.dy, f32[320,768]{1,0:T(8,128)} %get-tuple-element.242.e_in, bf16[320,768]{1,0:T(8,128)(2,1)} %bitcast.188, ...), custom_call_target="tpu_custom_call" | custom-call | flops 3019898880 | bytes 14684160 | tf_op jit(solution)/shard_map/text_self_backward/pallas_call | solution.py:432
  270.0 0.8 reshape.395
  271.2 0.7 constant_dynamic-update-slice_fusion.14
  272.1 0.7 pad_maximum_fusion.4
  272.7 230.1 %reduce_gradients.1 = (bf16[768,768]{1,0:T(8,128)(2,1)}, bf16[768,768]{1,0:T(8,128)(2,1)}, bf16[1024,768]{1,0:T(8,128)(2,1)}, bf16[768,768]{1,0:T(8,128)(2,1)}, ...) custom-call(bf16[2,768,768]{2,1,0:T(8,128)(2,1)} %get-tuple-element.126.refs, ...), custom_call_target="tpu_custom_call" | custom-call | tf_op jit(solution)/shard_map/reduce_gradients/pallas_call | solution.py:854
  502.8 1.3 slice.365
  504.1 0.3 copy-done
  504.4 0.2 copy.70
  504.6 0.2 copy.71
  504.8 1.4 maximum_bitcast_fusion
  506.1 0.2 convert_element_type.57
  506.4 1.2 copy-done.1
  507.8 1.6 pad_maximum_fusion
  509.5 1.6 convert_element_type.54
  511.2 1.6 convert_element_type.55
  512.8 1.6 convert_element_type.58
  514.5 1.6 convert_element_type.59
  516.2 1.3 slice.356
  517.5 0.9 slice.357
  518.4 0.9 slice.363
  519.2 0.9 slice.364
  520.1 0.6 copy.89
  520.7 0.6 copy.90
  521.3 0.6 copy.91
  522.0 0.6 copy.92
  522.6 0.6 copy.93
  523.2 0.6 copy.94
  523.8 0.6 slice_bitcast_fusion.28
  524.4 0.7 slice.336
  525.0 0.7 slice.324
  525.7 4.5 copy.75
  530.2 0.8 copy.109
  531.0 0.8 copy.110
  (127 shorter events, 1.9 us)
Async XLA Ops:
  0.7 6.9 %copy-start.17 = (bf16[2,1024,192]{1,2,0:T(8,128)(2,1)S(1)}, bf16[2,1024,192]{1,2,0:T(8,128)(2,1)}, u32[]{:S(2)}) copy-start(bf16[2,1024,192]{1,2,0:T(8,128)(2,1)} %param.43) | copy-start | bytes 2359300
  0.7 7.0 %copy-start.10 = (bf16[4,768,192]{1,2,0:T(8,128)(2,1)S(1)}, bf16[4,768,192]{1,2,0:T(8,128)(2,1)}, u32[]{:S(2)}) copy-start(bf16[4,768,192]{1,2,0:T(8,128)(2,1)} %param.39) | copy-start | bytes 3538948
  4.8 2.9 copy-start.22
  7.7 2.2 copy-start.11
  13.0 1.2 slice-start.2
  13.0 1.2 copy-start.20
  13.0 2.3 copy-start.16
  13.0 2.4 copy-start.21
  15.3 1.1 copy-start.35
  15.3 1.1 copy-start.38
  15.3 1.2 copy-start.36
  15.3 1.2 copy-start.37
  138.1 5.0 slice-start
  138.1 5.0 slice-start.1
  143.2 4.7 copy-start.9
  144.3 3.5 copy-start.25
  145.0 2.8 copy-start.24
  145.0 2.8 copy-start.26
  145.1 2.8 copy-start.8
  150.9 17.1 %copy-start.3 = (bf16[3,896,768]{2,1,0:T(8,128)(2,1)S(1)}, bf16[3,896,768]{2,1,0:T(8,128)(2,1)}, u32[]{:S(2)}) copy-start(bf16[3,896,768]{2,1,0:T(8,128)(2,1)} %get-tuple-element.99) | copy-start | bytes 12386308
  170.1 33.6 %copy-start.6 = (bf16[3,768,768]{2,1,0:T(8,128)(2,1)S(1)}, bf16[3,768,768]{2,1,0:T(8,128)(2,1)}, u32[]{:S(2)}) copy-start(bf16[3,768,768]{2,1,0:T(8,128)(2,1)} %get-tuple-element.113) | copy-start | bytes 10616836
  170.1 33.6 %copy-start.7 = (bf16[3,768,768]{2,1,0:T(8,128)(2,1)S(1)}, bf16[3,768,768]{2,1,0:T(8,128)(2,1)}, u32[]{:S(2)}) copy-start(bf16[3,768,768]{2,1,0:T(8,128)(2,1)} %get-tuple-element.106) | copy-start | bytes 10616836
  206.7 22.1 %copy-start.4 = (bf16[3,768,768]{2,1,0:T(8,128)(2,1)S(1)}, bf16[3,768,768]{2,1,0:T(8,128)(2,1)}, u32[]{:S(2)}) copy-start(bf16[3,768,768]{2,1,0:T(8,128)(2,1)} %get-tuple-element.118) | copy-start | bytes 10616836
  206.7 22.1 %copy-start.5 = (bf16[3,768,768]{2,1,0:T(8,128)(2,1)S(1)}, bf16[3,768,768]{2,1,0:T(8,128)(2,1)}, u32[]{:S(2)}) copy-start(bf16[3,768,768]{2,1,0:T(8,128)(2,1)} %get-tuple-element.114) | copy-start | bytes 10616836
  248.9 21.9 %copy-start.34 = (f32[2,2,2,192]{3,2,1,0:T(2,128)S(1)}, f32[2,2,2,192]{3,2,1,0:T(2,128)}, u32[]{:S(2)}) copy-start(f32[2,2,2,192]{3,2,1,0:T(2,128)} %get-tuple-element.141) | copy-start | bytes 18436
  248.9 22.0 %copy-start.33 = (f32[2,2,2,192]{3,2,1,0:T(2,128)S(1)}, f32[2,2,2,192]{3,2,1,0:T(2,128)}, u32[]{:S(2)}) copy-start(f32[2,2,2,192]{3,2,1,0:T(2,128)} %get-tuple-element.142) | copy-start | bytes 18436
  248.9 22.1 %copy-start.32 = (f32[2,2,768]{2,1,0:T(2,128)S(1)}, f32[2,2,768]{2,1,0:T(2,128)}, u32[]{:S(2)}) copy-start(f32[2,2,768]{2,1,0:T(2,128)} %get-tuple-element.143) | copy-start | bytes 36868
  249.0 22.1 %copy-start.28 = (f32[2,2,768]{2,1,0:T(2,128)S(1)}, f32[2,2,768]{2,1,0:T(2,128)}, u32[]{:S(2)}) copy-start(f32[2,2,768]{2,1,0:T(2,128)} %get-tuple-element.144) | copy-start | bytes 36868
  249.0 22.9 %copy-start.31 = (f32[3,768]{1,0:T(4,128)S(1)}, f32[3,768]{1,0:T(4,128)}, u32[]{:S(2)}) copy-start(f32[3,768]{1,0:T(4,128)} %get-tuple-element.146) | copy-start | bytes 27652
  249.0 22.9 %copy-start.30 = (f32[3,768]{1,0:T(4,128)S(1)}, f32[3,768]{1,0:T(4,128)}, u32[]{:S(2)}) copy-start(f32[3,768]{1,0:T(4,128)} %get-tuple-element.147) | copy-start | bytes 27652
  249.0 22.9 %copy-start.29 = (f32[3,768]{1,0:T(4,128)S(1)}, f32[3,768]{1,0:T(4,128)}, u32[]{:S(2)}) copy-start(f32[3,768]{1,0:T(4,128)} %get-tuple-element.148) | copy-start | bytes 27652
  249.0 22.9 %copy-start.27 = (f32[3,768]{1,0:T(4,128)S(1)}, f32[3,768]{1,0:T(4,128)}, u32[]{:S(2)}) copy-start(f32[3,768]{1,0:T(4,128)} %get-tuple-element.149) | copy-start | bytes 27652
  502.8 1.6 copy-start
  506.4 1.3 copy-start.1
  507.8 1.7 copy-start.15
  509.5 1.7 copy-start.14
  511.2 1.7 copy-start.13
  512.8 1.7 copy-start.12
  514.5 1.7 copy-start.2
  517.5 2.6 copy-start.23
  525.7 4.5 copy-start.19
  525.7 5.3 copy-start.18
